TPU v7x, 32 devices: a whole 2x2x4 slice. The times are simulated.
32 devices in a mesh: groups: 2 (over x), dp: 16 (over z, y, core).
Axes of the slice: x: 2, y: 2, z: 4, core: 2. Of those that a mesh axis runs over, the one named last changes fastest.
Arguments:
- query_rows: bfloat16 [32, 32, 768], P(('groups', 'dp')), parts along dimension 0, may hold values from -6 to 6
- proj_weight: bfloat16 [768, 4096], replicated, may hold values from -0.21875 to 0.21875
- proj_bias: bfloat16 [4096], replicated, may hold values from -3 to 3
- candidates: int32 [32, 2], P(('groups', 'dp')), parts along dimension 0, may hold values from 0 to 15, as said below
- caption_states: bfloat16 [32, 4, 4096], P(('groups', 'dp')), parts along dimension 0, may hold values from -24 to 24
- caption_ids: int32 [32, 4], P(('groups', 'dp')), parts along dimension 0, may hold values from 0 to 32127
- caption_lengths: int32 [32], P(('groups', 'dp')), parts along dimension 0, may hold values from 1 to 4
- norm_gain: float32 [4096], replicated, may hold values from 0.5 to 1.5
- head_weight: bfloat16 [4096, 32128], P(None, 'dp'), may hold values from -0.5 to 0.5
Outputs:
- token_loglik: float32 [32, 2, 4], P(('groups', 'dp')), parts along dimension 0
There are 2 independent parts, one for each index of `groups`. A program takes and returns all parts, laid end to end along the dimension named above; an argument that names none is the same for every part. Nothing has to cross between parts.
Inputs may be any that keep to these rules, and one draw needn't show every extreme that they name: Entry (i, k) names stored caption c, held on data shard c. The candidates of one data shard's images name distinct data shards. Each data shard's captions are named by at most 4 candidates in all, and some data shard's by exactly that many.
All inputs are finite; a program needn't handle non-finite values.
Results may differ from a plain program's by a relative error of at most 0.0006.
Values may be sent and summed in bfloat16 or wider, within the bound.
No kernel may reach another device: no remote copies, remote signals or barrier semaphores. Data moves between devices by JAX's collectives and lax.ppermute only.
A program may use at most 128 MiB of HBM per device.

v0:
```python
import jax
import jax.numpy as jnp
from jax import lax
from jax.sharding import PartitionSpec as P

HEAD_DIM = 64


score_scale = 0.015625
eps = 1e-06


def merged(part, axis, combine):
    gathered = jax.tree.map(lambda a: lax.all_gather(a, axis), part)

    def take(source):
        return jax.tree.map(lambda a: lax.dynamic_index_in_dim(a, source, 0, False), gathered)

    return lax.fori_loop(
        1, lax.axis_size(axis), lambda source, state: combine(state, take(source)), take(0)
    )


def project(rows, proj_weight, proj_bias):
    row_total, prefix_len, query_width = rows.shape
    summed = jnp.dot(
        rows.reshape(row_total * prefix_len, query_width),
        proj_weight,
        preferred_element_type=jnp.float32,
    )
    projected = (summed + proj_bias.astype(jnp.float32)).astype(jnp.bfloat16)
    return projected.reshape(row_total, prefix_len, proj_weight.shape[1])


def attend(projected, states, norm_gain):
    prefix_len = projected.shape[0]
    cap_len, model_width = states.shape
    heads = model_width // HEAD_DIM
    keys = jnp.concatenate([projected, states], 0)
    query = states.reshape(cap_len, heads, HEAD_DIM)
    keyed = keys.reshape(prefix_len + cap_len, heads, HEAD_DIM)
    scores = (
        jnp.einsum("thd,jhd->htj", query, keyed, preferred_element_type=jnp.float32) * score_scale
    )
    key_pos = jnp.arange(prefix_len + cap_len)[None, :]
    tok_pos = jnp.arange(cap_len)[:, None]
    allowed = (key_pos < prefix_len) | (key_pos - prefix_len <= tok_pos)
    scores = jnp.where(allowed[None], scores, -jnp.inf)
    row_max = jnp.max(scores, -1, keepdims=True)
    expo = jnp.exp(scores - row_max)
    weights = (expo / jnp.sum(expo, -1, keepdims=True)).astype(jnp.bfloat16)
    mixed_out = jnp.einsum(
        "htj,jhd->thd", weights, keyed, preferred_element_type=jnp.float32
    ).reshape(cap_len, model_width)
    mixed = states.astype(jnp.float32) + mixed_out
    normed = mixed * lax.rsqrt(jnp.mean(mixed * mixed, -1, keepdims=True) + eps) * norm_gain
    return normed.astype(jnp.bfloat16)


def merge_totals(first, second):
    larger = jnp.maximum(first[0], second[0])
    summed = first[1] * jnp.exp(first[0] - larger) + second[1] * jnp.exp(second[0] - larger)
    return (larger, summed, first[2] + second[2])


def local(
    query_rows,
    proj_weight,
    proj_bias,
    candidates,
    caption_states,
    caption_ids,
    caption_lengths,
    norm_gain,
    head_weight,
):
    position = lax.axis_index("dp")
    img_local, top_count = candidates.shape
    pair_count = img_local * top_count
    cap_local, cap_len, model_width = caption_states.shape
    own_cand = candidates.reshape(pair_count)
    all_cand, all_len = (
        lax.all_gather(candidates, "dp", axis=0, tiled=True),
        lax.all_gather(caption_lengths, "dp", axis=0, tiled=True),
    )
    caption_total = all_len.shape[0]
    length_match = own_cand[:, None] == jnp.arange(caption_total)[None, :]
    pair_len = jnp.sum(jnp.where(length_match, all_len[None, :], 0), 1)
    piece_states = lax.all_gather(caption_states, "dp", axis=0, tiled=True)
    piece_ids = lax.all_gather(caption_ids, "dp", axis=0, tiled=True)
    piece_rows = piece_states.shape[0]
    matches = own_cand[:, None] == jnp.arange(piece_rows)[None, :]
    picked = jnp.dot(
        matches.astype(jnp.bfloat16),
        piece_states.reshape(piece_rows, cap_len * model_width),
        preferred_element_type=jnp.float32,
    )
    fetched_ids = jnp.sum(jnp.where(matches[:, :, None], piece_ids[None, :, :], 0), 1).astype(
        jnp.int32
    )
    pair_states = picked.astype(jnp.bfloat16).reshape(pair_count, cap_len, model_width)
    image_proj = project(query_rows, proj_weight, proj_bias)
    pair_proj = jnp.repeat(image_proj, top_count, axis=0)
    work_hidden = jax.vmap(lambda one, two: attend(one, two, norm_gain))(pair_proj, pair_states)
    row_base = (position * pair_count + jnp.arange(pair_count)) * cap_len
    row_count = work_hidden.shape[0] * cap_len
    hidden_rows = work_hidden.reshape(row_count, model_width)
    id_rows = fetched_ids.reshape(row_count)
    vocab_dev = head_weight.shape[1]
    vocab_start = position * vocab_dev
    every_state, every_id = (
        lax.all_gather(hidden_rows, "dp", axis=0, tiled=True),
        lax.all_gather(id_rows, "dp", axis=0, tiled=True),
    )
    logits = jnp.dot(every_state, head_weight, preferred_element_type=jnp.float32)
    local_max = jnp.max(logits, 1)
    local_sum = jnp.sum(jnp.exp(logits - local_max[:, None]), 1)
    target_hit = jnp.arange(vocab_dev)[None, :] == (every_id - vocab_start)[:, None]
    local_pick = jnp.sum(jnp.where(target_hit, logits, 0.0), 1)
    top_all, sum_all, picked_all = merged((local_max, local_sum, local_pick), "dp", merge_totals)
    row_index = row_base[:, None] + jnp.arange(cap_len)[None, :]
    own_top = jnp.take(top_all, row_index)
    own_sum = jnp.take(sum_all, row_index)
    own_picked = jnp.take(picked_all, row_index)
    loglik = own_picked - (own_top + jnp.log(own_sum))
    inside = jnp.arange(cap_len)[None, :] < pair_len[:, None]
    result = jnp.where(inside, loglik, jnp.float32(0.0))
    return result.reshape(img_local, top_count, cap_len)


def solution(mesh):
    in_specs = (
        P(("groups", "dp"), None, None),
        P(),
        P(),
        P(("groups", "dp"), None),
        P(("groups", "dp"), None, None),
        P(("groups", "dp"), None),
        P(("groups", "dp")),
        P(),
        P(None, "dp"),
    )
    out_specs = P(("groups", "dp"), None, None)
    return jax.shard_map(local, mesh=mesh, in_specs=in_specs, out_specs=out_specs, check_vma=False)
```

profile of v0, /device:TPU:0, one launch (start us, length us, event | category | flops | bytes accessed | tf_op | source)
XLA Modules:
  0.0 150.1 jit_solution(12446172078241694290)
XLA Ops:
  6.6 24.8 %all_gather.34 = bf16[16,4,4096]{2,1,0:T(4,128)(2,1)S(1)} all-gather(bf16[1,4,4096]{2,1,0:T(4,128)(2,1)} %param.17), channel_id=1, replica_groups=mesh['groups'=2,'dp'=16] {'dp'}, dimensions={0}, use_global_device_ids=true | all-gather | bytes 557056 | tf_op jit(solution)/shard_map/all_gather | solution.py:89
  31.4 0.3 copy.36
  31.7 0.9 convolution_convert_fusion
  32.6 0.1 concatenate.6
  32.8 0.1 copy.31
  32.9 4.0 %fusion.8 = bf16[32,4096]{1,0:T(8,128)(2,1)S(1)} fusion(bf16[768,4096]{1,0:T(8,128)(2,1)} %param.14, f32[4096]{0:T(1024)S(1)} %convert_element_type.30, bf16[1,32,768]{2,1,0:T(8,128)(2,1)S(1)} %copy-done), kind=kOutput, calls=%fused_computation.16 | convolution fusion | flops 201588736 | bytes 6619136 | tf_op jit(solution)/shard_map/dot_general | solution.py:26
  36.9 0.5 reshape.104
  37.4 0.3 copy.30
  37.8 0.1 reshape.105
  37.9 1.0 fusion.30
  38.9 0.6 multiply_reduce_fusion
  39.6 0.1 reshape.106
  39.8 0.7 multiply_convert_fusion
  40.5 17.4 %all-gather.5 = s32[16,1,4]{2,1,0:T(1,128)S(1)} all-gather(s32[1,1,4]{2,1,0:T(1,128)S(1)} %bitcast.61), channel_id=1, replica_groups=mesh['groups'=2,'dp'=16] {'dp'}, dimensions={0}, use_global_device_ids=true | all-gather | bytes 272 | tf_op jit(solution)/shard_map/all_gather | solution.py:90
  58.1 0.2 select_reduce_fusion.1
  58.2 0.1 reshape.152
  59.2 0.6 dynamic-slice
  60.3 0.2 dynamic-update-slice.1
  60.5 0.7 dynamic-update-slice
  61.2 9.3 %all-reduce.2 = (s32[128]{0:T(128)S(1)}, s32[16]{0:T(128)S(1)}) all-reduce(s32[128]{0:T(128)S(1)} %dynamic-update-slice.1, s32[16]{0:T(128)S(1)} %dynamic-update-slice), channel_id=1, replica_groups=mesh['groups'=2,'dp'=16] {'dp'}, use_global_device_ids=true, to_apply=%add.1 | all-reduce | flops 144 | bytes 1152
  70.6 0.2 select_reduce_fusion.2
  70.8 5.1 %all-gather.9.cloned.1.call-done = bf16[128,4096]{1,0:T(8,128)(2,1)} async-done(((bf16[8,4096]{1,0:T(8,128)(2,1)}), bf16[128,4096]{1,0:T(8,128)(2,1)}) %all-gather.9.cloned.1.call-update) | async-done | bytes 1048592 | tf_op jit(solution)/shard_map/all_gather | solution.py:112
  75.9 8.3 %fusion.31 = (f32[128]{0:T(128)S(1)}, f32[128,2008]{0,1:T(8,128)S(1)}) fusion(bf16[128,4096]{1,0:T(8,128)(2,1)} %all-gather.9.cloned.1.call-done, bf16[4096,2008]{0,1:T(8,128)(2,1)} %param.21), kind=kOutput, calls=%fused_computation.61 | convolution fusion | flops 2105797504 | bytes 18526720 | tf_op jit(solution)/shard_map/dot_general | solution.py:115
  84.2 0.3 select_reduce_fusion
  84.5 19.3 %all-gather.6 = f32[16,1,128]{2,1,0:T(1,128)S(1)} all-gather(f32[1,1,128]{2,1,0:T(1,128)S(1)} %bitcast.60), channel_id=4, replica_groups=mesh['groups'=2,'dp'=16] {'dp'}, dimensions={0}, use_global_device_ids=true | all-gather | bytes 8704 | tf_op jit(solution)/shard_map/all_gather | solution.py:14
  103.7 17.3 %all-gather.4 = f32[16,1,128]{2,1,0:T(1,128)S(1)} all-gather(f32[1,1,128]{2,1,0:T(1,128)S(1)} %bitcast.59), channel_id=3, replica_groups=mesh['groups'=2,'dp'=16] {'dp'}, dimensions={0}, use_global_device_ids=true | all-gather | bytes 8704 | tf_op jit(solution)/shard_map/all_gather | solution.py:14
  121.0 18.7 %all-gather.3 = f32[16,1,128]{2,1,0:T(1,128)S(1)} all-gather(f32[1,1,128]{2,1,0:T(1,128)S(1)} %bitcast.58), channel_id=2, replica_groups=mesh['groups'=2,'dp'=16] {'dp'}, dimensions={0}, use_global_device_ids=true | all-gather | bytes 8704 | tf_op jit(solution)/shard_map/all_gather | solution.py:14
  139.7 0.7 while.19
  140.4 0.6 gather_fusion
  141.1 0.6 gather_fusion.1
  141.9 0.6 gather_fusion.2
  142.6 0.7 fusion.19
  (52 shorter events, 1.2 us)
Async XLA Ops:
  6.5 26.4 %copy-start = (bf16[1,32,768]{2,1,0:T(8,128)(2,1)S(1)}, bf16[1,32,768]{2,1,0:T(8,128)(2,1)}, u32[]{:S(2)}) copy-start(bf16[1,32,768]{2,1,0:T(8,128)(2,1)} %param.13) | copy-start | bytes 147460
  6.5 26.3 %copy-start.2 = (bf16[4096]{0:T(1024)(128)(2,1)S(1)}, bf16[4096]{0:T(1024)(128)(2,1)}, u32[]{:S(2)}) copy-start(bf16[4096]{0:T(1024)(128)(2,1)} %param.15) | copy-start | bytes 24580
  6.5 69.3 %all-gather.9.cloned.1.call-start = ((), (), s32[]{:S(2)}) async-start(), calls=%async_computation | async-start | bytes 1114112 | tf_op jit(solution)/shard_map/all_gather | solution.py:112
  38.9 0.9 copy-start.1
  38.9 1.6 %copy-start.3 = (s32[1,4]{1,0:T(1,128)S(1)}, s32[1,4]{1,0:T(1,128)}, u32[]{:S(2)}) copy-start(s32[1,4]{1,0:T(1,128)} %param.18) | copy-start | bytes 52
  38.9 19.1 %copy-start.4 = (s32[1,2]{1,0:T(1,128)S(1)}, s32[1,2]{1,0:T(1,128)}, u32[]{:S(2)}) copy-start(s32[1,2]{1,0:T(1,128)} %param.16) | copy-start | bytes 28
  38.9 20.2 %copy-start.5 = (u32[32]{0:T(128)S(1)}, u32[32]{0:T(128)}, u32[]{:S(2)}) copy-start(u32[32]{0:T(128)} %constant.94) | copy-start | bytes 388
Sparse Core Ops, SparseCore 0:
  40.6 35.1 all-gather.8
where the time goes:
time: 150 us
  blocking collectives  107 us (71%)
  matrix products  14.8 us (10%)
  between operations  14.8 us (10%)
  local copies, waits for them, and re-layouts  5.74 us (4%)
  waiting for transfers between devices  5.12 us (3%)
  other arithmetic  2.59 us (2%)
    all_gather x3, blocking collectives, merged(): gathered = jax.tree.map(lambda a: lax.all_gather(a, axis), part)  55.2 us
    all_gather x1, blocking collectives, local(): piece_states = lax.all_gather(caption_states, 'dp', axis=0, tiled=True)  24.8 us
    all_gather x1, blocking collectives, local(): piece_ids = lax.all_gather(caption_ids, 'dp', axis=0, tiled=True)  17.4 us
    unnamed x1, blocking collectives  9.34 us
    dot_general x1, matrix products, local(): jnp.dot(every_state, head_weight, preferred_element_type=jnp.float32)  8.32 us
    all_gather x1, waiting for transfers between devices, local(): lax.all_gather(hidden_rows, 'dp', axis=0, tiled=True)  5.1 us
    dot_general x1, matrix products, project(): jnp.dot(rows.reshape(row_total * prefix_len, query_width), proj_weight, p...  3.97 us
  transfers between devices with their start and end apart: 1, of which 1 were waited for; matrix products, arithmetic and copies ran while one was open for 1% of the time, Pallas kernels for 0%

commit v1 on v0

--- a/solution.py
+++ b/solution.py
@@ -1,13 +1,262 @@
 import jax
 import jax.numpy as jnp
 from jax import lax
+from jax.experimental import pallas as pl
+from jax.experimental.pallas import tpu as pltpu
 from jax.sharding import PartitionSpec as P
 
 HEAD_DIM = 64
+LANES = 128
+DIGIT = 256
+MIB = 1 << 20
 
 
 score_scale = 0.015625
 eps = 1e-06
+
+VMEM = pl.BlockSpec(memory_space=pltpu.VMEM)
+SMEM = pl.BlockSpec(memory_space=pltpu.SMEM)
+
+
+def iota(shape, dim):
+    return lax.broadcasted_iota(jnp.int32, shape, dim)
+
+
+def pack_kernel(cand_ref, ids_ref, len_ref, rows_ref, states_ref, out_ref, stage):
+    prefix, width = rows_ref.shape[1:]
+    cap_len, model_width = states_ref.shape[1:]
+    out_ref[0:prefix, :] = rows_ref[0]
+    states = states_ref[0].astype(jnp.float32)
+    pieces = -(-model_width // width)
+    for c in range(pieces - 1):
+        stage[c * cap_len : (c + 1) * cap_len, :] = states[:, c * width : (c + 1) * width]
+    rest = model_width - (pieces - 1) * width
+    last = (pieces - 1) * cap_len
+    stage[last : last + cap_len, 0:rest] = states[:, model_width - rest :]
+    token, lane = iota((cap_len, width - rest), 0), iota((cap_len, width - rest), 1)
+    ids = jnp.zeros_like(token)
+    for t in range(cap_len):
+        ids = jnp.where(token == t, ids_ref[0, t], ids)
+    digits = jnp.where(lane == 0, ids // DIGIT, jnp.where(lane == 1, ids % DIGIT, 0))
+    digits = jnp.where(lane == 2, len_ref[0], digits)
+    stage[last : last + cap_len, rest:] = digits.astype(jnp.float32)
+    tail = stage.shape[0] - last - cap_len
+    row, lane = iota((tail, width), 0), iota((tail, width), 1)
+    cand = jnp.where(row < cap_len, cand_ref[0, 0], cand_ref[0, 1])
+    digits = jnp.where(lane == 0, cand // DIGIT, jnp.where(lane == 1, cand % DIGIT, 0))
+    stage[last + cap_len :, :] = digits.astype(jnp.float32)
+    out_ref[prefix:, :] = stage[...].astype(jnp.bfloat16)
+
+
+def number(digits):
+    lane = iota(digits.shape, 1)
+    scaled = jnp.where(lane == 0, digits * DIGIT, jnp.where(lane == 1, digits, 0.0))
+    return jnp.sum(scaled, 1, keepdims=True).astype(jnp.int32)
+
+
+def hidden_kernel(blocks, *refs):
+    (pos_ref, *msgs), (weight_ref, bias_ref, gain_ref, out_ref, keys, caps, rows, query, mixed) = (
+        refs[: 2 * blocks + 1],
+        refs[2 * blocks + 1 :],
+    )
+    width = rows.shape[1]
+    model_width = query.shape[1] - LANES
+    prefix = rows.shape[0] // blocks
+    held = msgs[0].shape[0] - prefix
+    pair_rows = query.shape[0] // blocks
+    cap_len = 4
+    row_total = query.shape[0]
+    for j in range(blocks):
+        rows[j * prefix : (j + 1) * prefix, :] = msgs[j][0:prefix, :]
+    for j in range(2 * blocks):
+        caps[j * held : (j + 1) * held, :] = msgs[j][prefix:, :]
+    tail = 16
+    cand = jnp.concatenate(
+        [msgs[j][prefix + held - tail :, 0:LANES].astype(jnp.float32)[tail - pair_rows :] for j in range(blocks)], 0
+    )
+    away = number(cand) ^ pos_ref[0]
+    token = iota((row_total, 1), 0) % cap_len
+    first = ((away & 1) * blocks + (away >> 1)) * held + token
+    column = iota((row_total, 2 * blocks * held), 1)
+    pieces = -(-model_width // width)
+    for c in range(pieces):
+        pick = jnp.where(column == first + c * cap_len, 1.0, 0.0).astype(jnp.bfloat16)
+        span = min(width, query.shape[1] - c * width)
+        query[:, c * width : c * width + span] = jnp.dot(
+            pick, caps[:, 0:span], preferred_element_type=jnp.float32
+        ).astype(jnp.bfloat16)
+    step = 512
+
+    @pl.loop(0, model_width // step)
+    def _(i):
+        cols = pl.ds(pl.multiple_of(i * step, step), step)
+        summed = jnp.dot(rows[...], weight_ref[:, cols], preferred_element_type=jnp.float32)
+        keys[:, cols] = (summed + bias_ref[:, cols].astype(jnp.float32)).astype(jnp.bfloat16)
+
+    lane = iota((row_total, LANES), 1)
+    low = lane < HEAD_DIM
+    key_total = keys.shape[0]
+    two = 2 * row_total
+    r, k = iota((two, key_total), 0) % row_total, iota((two, key_total), 1)
+    image_ok = (r // pair_rows) == (k // prefix)
+    r, k = iota((two, row_total), 0) % row_total, iota((two, row_total), 1)
+    own_ok = ((r // cap_len) == (k // cap_len)) & (k <= r)
+    nothing = jnp.float32(-1e30)
+    contract = (((1,), (1,)), ((), ()))
+
+    def heads(i, square):
+        cols = pl.ds(pl.multiple_of(i * LANES, LANES), LANES)
+        q, key = query[:, cols], keys[:, cols]
+        zero = jnp.zeros_like(q)
+        both = jnp.concatenate([jnp.where(low, q, zero), jnp.where(low, zero, q)], 0)
+        image = lax.dot_general(both, key, contract, preferred_element_type=jnp.float32) * score_scale
+        own = lax.dot_general(both, q, contract, preferred_element_type=jnp.float32) * score_scale
+        image, own = jnp.where(image_ok, image, nothing), jnp.where(own_ok, own, nothing)
+        top = jnp.maximum(jnp.max(image, 1, keepdims=True), jnp.max(own, 1, keepdims=True))
+        image, own = jnp.exp(image - top), jnp.exp(own - top)
+        total = 1.0 / (jnp.sum(image, 1, keepdims=True) + jnp.sum(own, 1, keepdims=True))
+        out = jnp.dot((image * total).astype(jnp.bfloat16), key, preferred_element_type=jnp.float32)
+        out += jnp.dot((own * total).astype(jnp.bfloat16), q, preferred_element_type=jnp.float32)
+        value = q.astype(jnp.float32) + jnp.where(low, out[:row_total], out[row_total:])
+        mixed[:, cols] = value
+        return square + value * value
+
+    square = lax.fori_loop(
+        0, model_width // LANES, heads, jnp.zeros((row_total, LANES), jnp.float32), unroll=4
+    )
+    scale = lax.rsqrt(jnp.sum(square, 1, keepdims=True) / model_width + eps)
+    out_ref[:, 0:model_width] = (mixed[...] * scale * gain_ref[...]).astype(jnp.bfloat16)
+    out_ref[:, model_width:] = query[:, model_width:]
+
+
+def logits_kernel(pos_ref, mine_ref, other_ref, head_ref, out_ref, states, logits):
+    half = mine_ref.shape[0]
+    model_width, vocab = head_ref.shape
+    states[0:half, :] = mine_ref[:, 0:model_width]
+    states[half:, :] = other_ref[:, 0:model_width]
+    row_total = 2 * half
+    step = 256
+
+    @pl.loop(0, vocab // step)
+    def _(i):
+        cols = pl.ds(pl.multiple_of(i * step, step), step)
+        logits[:, cols] = jnp.dot(states[...], head_ref[:, cols], preferred_element_type=jnp.float32)
+
+    done = vocab // step * step
+    if done < vocab:
+        logits[:, done:vocab] = jnp.dot(
+            states[...], head_ref[:, done:vocab], preferred_element_type=jnp.float32
+        )
+    ids = jnp.concatenate(
+        [number(ref[:, model_width:].astype(jnp.float32)) for ref in (mine_ref, other_ref)], 0
+    )
+    values = logits[:, 0:vocab]
+    top = jnp.max(values, 1, keepdims=True)
+    total = jnp.sum(jnp.exp(values - top), 1, keepdims=True)
+    hit = iota((row_total, vocab), 1) == ids - pos_ref[0] * vocab
+    target = jnp.sum(jnp.where(hit, values, 0.0), 1, keepdims=True)
+    lane = iota((row_total, LANES), 1)
+    packed = jnp.where(lane == 0, top, jnp.where(lane == 1, total, jnp.where(lane == 2, target, 0.0)))
+    shards, rows = out_ref.shape[:2]
+    for j in range(shards):
+        away = (j % (shards // 2)) * 2 + j // (shards // 2)
+        out_ref[pos_ref[0] ^ away] = packed[j * rows : (j + 1) * rows]
+
+
+def finish_kernel(stats_ref, mine_ref, out_ref):
+    stats = stats_ref[...]
+    shards, rows, _ = stats.shape
+    cap_len = out_ref.shape[2]
+    model_width = mine_ref.shape[1] - LANES
+    lane = iota((rows, LANES), 1)
+    top = jnp.max(stats, 0)[:, 0:1]
+    total = jnp.zeros((rows, 1), jnp.float32)
+    target = jnp.zeros((rows, 1), jnp.float32)
+    for e in range(shards):
+        total += stats[e][:, 1:2] * jnp.exp(stats[e][:, 0:1] - top)
+        target += stats[e][:, 2:3]
+    loglik = target - (top + jnp.log(total))
+    lengths = mine_ref[0:16, model_width:].astype(jnp.float32)[0:rows, 2:3]
+    token = iota((rows, LANES), 0) % cap_len
+    kept = (token == lane) & (token.astype(jnp.float32) < lengths)
+    spread = jnp.where(kept, loglik, 0.0)
+    for k in range(out_ref.shape[1]):
+        out_ref[0, k : k + 1, :] = jnp.sum(spread[k * cap_len : (k + 1) * cap_len], 0, keepdims=True)[:, 0:cap_len]
+
+
+def paired(
+    query_rows, proj_weight, proj_bias, candidates, caption_states, caption_ids, caption_lengths, norm_gain, head_weight
+):
+    shards = lax.axis_size("dp")
+    blocks = shards // 2
+    _, prefix, width = query_rows.shape
+    _, cap_len, model_width = caption_states.shape
+    top_count = candidates.shape[1]
+    pair_rows = top_count * cap_len
+    held = cap_len * -(-model_width // width) + pair_rows
+    row_total = blocks * pair_rows
+    vocab = head_weight.shape[1]
+    position = lax.axis_index("dp").astype(jnp.int32).reshape(1)
+
+    def swap(a, away):
+        return lax.ppermute(a, "dp", [(i, i ^ away) for i in range(shards)])
+
+    message = pl.pallas_call(
+        pack_kernel,
+        out_shape=jax.ShapeDtypeStruct((prefix + held, width), jnp.bfloat16),
+        in_specs=[SMEM, SMEM, SMEM, VMEM, VMEM],
+        out_specs=VMEM,
+        scratch_shapes=[pltpu.VMEM((held, width), jnp.float32)],
+        compiler_params=pltpu.CompilerParams(vmem_limit_bytes=2 * MIB),
+        name="pack",
+    )(candidates, caption_ids, caption_lengths, query_rows, caption_states)
+
+    got = {0: message}
+    for away in (12, 8, 4, 2):
+        got[away] = swap(message, away)
+    for away in (4, 8, 12):
+        got[away + 2] = swap(got[away], 2)
+    mine = [got[2 * j] for j in range(blocks)]
+    other = [swap(a, 1) for a in mine]
+
+    hidden = pl.pallas_call(
+        lambda *refs: hidden_kernel(blocks, *refs),
+        out_shape=jax.ShapeDtypeStruct((row_total, model_width + LANES), jnp.bfloat16),
+        in_specs=[SMEM] + [VMEM] * (2 * blocks + 3),
+        out_specs=VMEM,
+        scratch_shapes=[
+            pltpu.VMEM((blocks * prefix, model_width), jnp.bfloat16),
+            pltpu.VMEM((2 * blocks * held, width), jnp.bfloat16),
+            pltpu.VMEM((blocks * prefix, width), jnp.bfloat16),
+            pltpu.VMEM((row_total, model_width + LANES), jnp.bfloat16),
+            pltpu.VMEM((row_total, model_width), jnp.float32),
+        ],
+        compiler_params=pltpu.CompilerParams(vmem_limit_bytes=20 * MIB),
+        name="hidden",
+    )(position, *mine, *other, proj_weight, proj_bias.reshape(1, -1), norm_gain.reshape(1, -1))
+
+    stats = pl.pallas_call(
+        logits_kernel,
+        out_shape=jax.ShapeDtypeStruct((shards, pair_rows, LANES), jnp.float32),
+        in_specs=[SMEM, VMEM, VMEM, VMEM],
+        out_specs=VMEM,
+        scratch_shapes=[
+            pltpu.VMEM((2 * row_total, model_width), jnp.bfloat16),
+            pltpu.VMEM((2 * row_total, -(-vocab // LANES) * LANES), jnp.float32),
+        ],
+        compiler_params=pltpu.CompilerParams(vmem_limit_bytes=32 * MIB),
+        name="logits",
+    )(position, hidden, swap(hidden, 1), head_weight)
+
+    stats = lax.all_to_all(stats, "dp", 0, 0, tiled=True)
+    return pl.pallas_call(
+        finish_kernel,
+        out_shape=jax.ShapeDtypeStruct((1, top_count, cap_len), jnp.float32),
+        in_specs=[VMEM, VMEM],
+        out_specs=VMEM,
+        compiler_params=pltpu.CompilerParams(vmem_limit_bytes=2 * MIB),
+        name="finish",
+    )(stats, hidden)
 
 
 def merged(part, axis, combine):
@@ -63,7 +312,7 @@
     return (larger, summed, first[2] + second[2])
 
 
-def local(
+def spread(
     query_rows,
     proj_weight,
     proj_bias,
@@ -128,6 +377,13 @@
     return result.reshape(img_local, top_count, cap_len)
 
 
+def local(query_rows, proj_weight, proj_bias, candidates, caption_states, *rest):
+    one_each = candidates.shape[0] == 1 and caption_states.shape[0] == 1
+    fits = candidates.shape[1] == 2 and caption_states.shape[1] == 4 and query_rows.shape[1] == 32
+    plan = paired if lax.axis_size("dp") == 16 and one_each and fits else spread
+    return plan(query_rows, proj_weight, proj_bias, candidates, caption_states, *rest)
+
+
 def solution(mesh):
     in_specs = (
         P(("groups", "dp"), None, None),

time: 150 us -> 92.7 us (0.62)
  blocking collectives: 107 us -> 11.6 us
  local copies, waits for them, and re-layouts: 5.74 us -> 35.4 us
  Pallas kernels: 0 us -> 22.5 us
  matrix products: 14.8 us -> 0 us
  between operations: 14.8 us -> 0.73 us
  starting transfers between devices: 0.01 us -> 11.8 us
  waiting for transfers between devices: 5.12 us -> 9.69 us
  other arithmetic: 2.59 us -> 0 us
    all_gather x5 -> x0, blocking collectives: 97.4 us -> none  [the longest x3 55.2 us: merged(): gathered = jax.tree.map(lambda a: lax.all_gather(a, axis), part)]
    unnamed x18 -> x15, local copies, waits for them, and re-layouts: 1.8 us -> 34.7 us
    pallas_call x0 -> x4, Pallas kernels: none -> 22.5 us  [the longest x1 16.7 us: paired(): pl.pallas_call(lambda *refs: hidden_kernel(blocks, *refs), out_shape=jax....]
    dot_general x4 -> x0, matrix products: 13.9 us -> none  [the longest x1 8.32 us: local(): jnp.dot(every_state, head_weight, preferred_element_type=jnp.float32)]
    ppermute x0 -> x16, starting transfers between devices: none -> 11.8 us  [swap(): return lax.ppermute(a, 'dp', [(i, i ^ away) for i in range(shards)])]
    all_to_all x0 -> x1, blocking collectives: none -> 11.6 us  [paired(): stats = lax.all_to_all(stats, 'dp', 0, 0, tiled=True)]
    ppermute x0 -> x16, waiting for transfers between devices: none -> 9.69 us  [swap(): return lax.ppermute(a, 'dp', [(i, i ^ away) for i in range(shards)])]
    unnamed x1 -> x0, blocking collectives: 9.34 us -> none
  transfers between devices with their start and end apart: 1 -> 16, of which waited for: 1 -> 5; matrix products, arithmetic and copies ran while one was open for 1% -> 25% of each run, Pallas kernels for 0% -> 0%
where the time goes in v1:
time: 92.7 us; the launch traced here: 91.7 us
  local copies, waits for them, and re-layouts  35.4 us (38%)
  Pallas kernels  22.5 us (24%)
  starting transfers between devices  11.8 us (13%)
  blocking collectives  11.6 us (13%)
  waiting for transfers between devices  9.69 us (10%)
    unnamed x15, local copies, waits for them, and re-layouts  34.7 us
    pallas_call x1, Pallas kernels, paired(): pl.pallas_call(lambda *refs: hidden_kernel(blocks, *refs), out_shape=jax....  16.7 us
    ppermute x16, starting transfers between devices, swap(): return lax.ppermute(a, 'dp', [(i, i ^ away) for i in range(shards)])  11.8 us
    all_to_all x1, blocking collectives, paired(): stats = lax.all_to_all(stats, 'dp', 0, 0, tiled=True)  11.6 us
    ppermute x16, waiting for transfers between devices, swap(): return lax.ppermute(a, 'dp', [(i, i ^ away) for i in range(shards)])  9.69 us
    pallas_call x1, Pallas kernels, paired(): pl.pallas_call(logits_kernel, out_shape=jax.ShapeDtypeStruct((shards, pai...  4.35 us
  transfers between devices with their start and end apart: 16, of which 5 were waited for; matrix products, arithmetic and copies ran while one was open for 25% of the time, Pallas kernels for 0%

profile of v1, /device:TPU:0, one launch (start us, length us, event | category | flops | bytes accessed | tf_op | source)
XLA Modules:
  0.0 91.7 jit_solution(17508984112440305613)
XLA Ops:
  0.7 0.8 copy-done.2
  1.5 0.8 copy-done.3
  2.2 0.7 copy-done.5
  2.9 0.7 copy-done.6
  3.5 0.6 pack.1.refs_1_
  4.1 5.1 %collective-permute-start.5 = (bf16[64,768]{1,0:T(8,128)(2,1)S(1)}, bf16[64,768]{1,0:T(8,128)(2,1)S(1)}, u32[]{:S(2)}, u32[]{:S(2)}) collective-permute-start(bf16[64,768]{1,0:T(8,128)(2,1)S(1)} %pack.1.refs_1_), channel_id=1, source_target_pairs={{0,12},{1,13},{2,14},{3,15},{4,8},{5,9},{6,10},{7,11},{8,4},{9,5},... | collective-permute-start | bytes 294920 | tf_op jit(solution)/shard_map/ppermute | solution.py:202
  9.2 0.0 collective-permute-start.7
  9.2 0.7 collective-permute-start.1
  9.9 1.6 %collective-permute-start = (bf16[64,768]{1,0:T(8,128)(2,1)S(1)}, bf16[64,768]{1,0:T(8,128)(2,1)S(1)}, u32[]{:S(2)}, u32[]{:S(2)}) collective-permute-start(bf16[64,768]{1,0:T(8,128)(2,1)S(1)} %pack.1.refs_1_), channel_id=1, source_target_pairs={{0,2},{1,3},{2,0},{3,1},{4,6},{5,7},{6,4},{7,5},{8,10},{9,11},{10,... | collective-permute-start | bytes 294920 | tf_op jit(solution)/shard_map/ppermute | solution.py:202
  11.5 0.9 collective-permute-done.5.refs_7_
  12.4 0.0 collective-permute-start.13
  12.4 0.0 collective-permute-done.7.refs_9_
  12.4 1.5 %collective-permute-start.6 = (bf16[64,768]{1,0:T(8,128)(2,1)S(1)}, bf16[64,768]{1,0:T(8,128)(2,1)S(1)}, u32[]{:S(2)}, u32[]{:S(2)}) collective-permute-start(bf16[64,768]{1,0:T(8,128)(2,1)S(1)} %collective-permute-done.5.refs_7_), channel_id=1, source_target_pairs={{0,2},{1,3},{2,0},{3,1},{4,6},{5,7},{6,4},{7,5},{8,10},{9,11},{10,... | collective-permute-start | bytes 294920 | tf_op jit(solution)/shard_map/ppermute | solution.py:202
  13.9 3.5 %collective-permute-done.3.refs_5_ = bf16[64,768]{1,0:T(8,128)(2,1)S(1)} collective-permute-done((bf16[64,768]{1,0:T(8,128)(2,1)S(1)}, bf16[64,768]{1,0:T(8,128)(2,1)S(1)}, u32[]{:S(2)}, u32[]{:S(2)}) %collective-permute-start.3) | collective-permute-done | bytes 98336 | tf_op jit(solution)/shard_map/ppermute | solution.py:202
  17.5 0.0 collective-permute-start.11
  17.5 1.5 %collective-permute-start.4 = (bf16[64,768]{1,0:T(8,128)(2,1)S(1)}, bf16[64,768]{1,0:T(8,128)(2,1)S(1)}, u32[]{:S(2)}, u32[]{:S(2)}) collective-permute-start(bf16[64,768]{1,0:T(8,128)(2,1)S(1)} %collective-permute-done.3.refs_5_), channel_id=1, source_target_pairs={{0,2},{1,3},{2,0},{3,1},{4,6},{5,7},{6,4},{7,5},{8,10},{9,11},{10,... | collective-permute-start | bytes 294920 | tf_op jit(solution)/shard_map/ppermute | solution.py:202
  19.0 0.5 collective-permute-start.2
  19.5 0.5 collective-permute-start.8
  20.0 0.1 collective-permute-start.14
  20.1 3.0 %collective-permute-done.4.refs_6_ = bf16[64,768]{1,0:T(8,128)(2,1)S(1)} collective-permute-done((bf16[64,768]{1,0:T(8,128)(2,1)S(1)}, bf16[64,768]{1,0:T(8,128)(2,1)S(1)}, u32[]{:S(2)}, u32[]{:S(2)}) %collective-permute-start.4) | collective-permute-done | bytes 98336 | tf_op jit(solution)/shard_map/ppermute | solution.py:202
  23.1 1.7 %collective-permute-done.2.refs_4_ = bf16[64,768]{1,0:T(8,128)(2,1)S(1)} collective-permute-done((bf16[64,768]{1,0:T(8,128)(2,1)S(1)}, bf16[64,768]{1,0:T(8,128)(2,1)S(1)}, u32[]{:S(2)}, u32[]{:S(2)}) %collective-permute-start.2) | collective-permute-done | bytes 98336 | tf_op jit(solution)/shard_map/ppermute | solution.py:202
  24.8 0.7 reshape.10.refs_18_
  25.6 0.5 collective-permute-done.10.refs_12_
  26.1 2.8 %copy-done.1 = bf16[768,4096]{1,0:T(8,128)(2,1)S(1)} copy-done((bf16[768,4096]{1,0:T(8,128)(2,1)S(1)}, bf16[768,4096]{1,0:T(8,128)(2,1)}, u32[]{:S(2)}) %copy-start.1) | copy-done | bytes 6291480
  28.9 0.7 copy-done.4
  29.6 16.7 %hidden.1.mine_ref = bf16[64,4224]{1,0:T(8,128)(2,1)S(1)} custom-call(s32[1]{0:T(128)} %bitcast.refs_0_.pos_ref, bf16[64,768]{1,0:T(8,128)(2,1)S(1)} %pack.1.refs_1_, bf16[64,768]{1,0:T(8,128)(2,1)S(1)} %collective-permute-done.refs_2_, bf16[64,768]{1,0:T(8,128)(2,1)S(1)} %collective-permute-done.1.refs_3_, ...), custom_call_target="tpu_custom_call" | custom-call | tf_op jit(solution)/shard_map/hidden/pallas_call | solution.py:222
  46.3 0.2 collective-permute-start.15
  46.5 22.6 %copy.10.head_ref = bf16[4096,2008]{1,0:T(8,128)(2,1)} copy(bf16[4096,2008]{0,1:T(8,128)(2,1)} %param.17) | data formatting | bytes 32899072 | tf_op args[8]
  69.1 5.8 %copy-done = bf16[4096,2008]{1,0:T(8,128)(2,1)S(1)} copy-done((bf16[4096,2008]{1,0:T(8,128)(2,1)S(1)}, bf16[4096,2008]{1,0:T(8,128)(2,1)}, u32[]{:S(2)}) %copy-start) | copy-done | bytes 16449560
  74.9 4.4 %logits.1 = f32[16,8,128]{2,1,0:T(8,128)S(1)} custom-call(s32[1]{0:T(128)} %bitcast.refs_0_.pos_ref, bf16[64,4224]{1,0:T(8,128)(2,1)S(1)} %hidden.1.mine_ref, bf16[64,4224]{1,0:T(8,128)(2,1)S(1)} %collective-permute-done.15.other_ref, bf16[4096,2008]{1,0:T(8,128)(2,1)S(1)} %copy-done), custom_call_target="tpu_custom_call" | custom-call | tf_op jit(solution)/shard_map/logits/pallas_call | solution.py:238
  79.2 11.6 %all_to_all.5.stats_ref = f32[16,8,128]{2,1,0:T(8,128)S(1)} all-to-all(f32[16,8,128]{2,1,0:T(8,128)S(1)} %logits.1), channel_id=1, replica_groups=mesh['groups'=2,'dp'=16] {'dp'}, dimensions={0} | all-to-all | bytes 131072 | tf_op jit(solution)/shard_map/all_to_all | solution.py:251
  90.8 0.9 finish.1
  (21 shorter events, 0.0 us)
Async XLA Ops:
  0.7 0.8 copy-start.2
  1.5 0.8 copy-start.3
  2.2 0.7 copy-start.5
  2.9 0.7 copy-start.6
  4.1 8.3 %collective-permute-start.5 = (bf16[64,768]{1,0:T(8,128)(2,1)S(1)}, bf16[64,768]{1,0:T(8,128)(2,1)S(1)}, u32[]{:S(2)}, u32[]{:S(2)}) collective-permute-start(bf16[64,768]{1,0:T(8,128)(2,1)S(1)} %pack.1.refs_1_), channel_id=1, source_target_pairs={{0,12},{1,13},{2,14},{3,15},{4,8},{5,9},{6,10},{7,11},{8,4},{9,5},... | collective-permute-start | bytes 294920 | tf_op jit(solution)/shard_map/ppermute | solution.py:202
  9.2 3.2 %collective-permute-start.7 = (bf16[64,768]{1,0:T(8,128)(2,1)S(1)}, bf16[64,768]{1,0:T(8,128)(2,1)S(1)}, u32[]{:S(2)}, u32[]{:S(2)}) collective-permute-start(bf16[64,768]{1,0:T(8,128)(2,1)S(1)} %pack.1.refs_1_), channel_id=1, source_target_pairs={{0,1},{1,0},{2,3},{3,2},{4,5},{5,4},{6,7},{7,6},{8,9},{9,8},{10,11... | collective-permute-start | bytes 294920 | tf_op jit(solution)/shard_map/ppermute | solution.py:202
  9.2 8.3 %collective-permute-start.3 = (bf16[64,768]{1,0:T(8,128)(2,1)S(1)}, bf16[64,768]{1,0:T(8,128)(2,1)S(1)}, u32[]{:S(2)}, u32[]{:S(2)}) collective-permute-start(bf16[64,768]{1,0:T(8,128)(2,1)S(1)} %pack.1.refs_1_), channel_id=1, source_target_pairs={{0,8},{1,9},{2,10},{3,11},{4,12},{5,13},{6,14},{7,15},{8,0},{9,1},... | collective-permute-start | bytes 294920 | tf_op jit(solution)/shard_map/ppermute | solution.py:202
  9.2 8.3 %collective-permute-start.1 = (bf16[64,768]{1,0:T(8,128)(2,1)S(1)}, bf16[64,768]{1,0:T(8,128)(2,1)S(1)}, u32[]{:S(2)}, u32[]{:S(2)}) collective-permute-start(bf16[64,768]{1,0:T(8,128)(2,1)S(1)} %pack.1.refs_1_), channel_id=1, source_target_pairs={{0,4},{1,5},{2,6},{3,7},{4,0},{5,1},{6,2},{7,3},{8,12},{9,13},{10,... | collective-permute-start | bytes 294920 | tf_op jit(solution)/shard_map/ppermute | solution.py:202
  9.9 9.1 %collective-permute-start = (bf16[64,768]{1,0:T(8,128)(2,1)S(1)}, bf16[64,768]{1,0:T(8,128)(2,1)S(1)}, u32[]{:S(2)}, u32[]{:S(2)}) collective-permute-start(bf16[64,768]{1,0:T(8,128)(2,1)S(1)} %pack.1.refs_1_), channel_id=1, source_target_pairs={{0,2},{1,3},{2,0},{3,1},{4,6},{5,7},{6,4},{7,5},{8,10},{9,11},{10,... | collective-permute-start | bytes 294920 | tf_op jit(solution)/shard_map/ppermute | solution.py:202
  12.4 7.1 %collective-permute-start.13 = (bf16[64,768]{1,0:T(8,128)(2,1)S(1)}, bf16[64,768]{1,0:T(8,128)(2,1)S(1)}, u32[]{:S(2)}, u32[]{:S(2)}) collective-permute-start(bf16[64,768]{1,0:T(8,128)(2,1)S(1)} %collective-permute-done.5.refs_7_), channel_id=1, source_target_pairs={{0,1},{1,0},{2,3},{3,2},{4,5},{5,4},{6,7},{7,6},{8,9},{9,8},{10,11... | collective-permute-start | bytes 294920 | tf_op jit(solution)/shard_map/ppermute | solution.py:202
  12.4 7.1 %collective-permute-start.6 = (bf16[64,768]{1,0:T(8,128)(2,1)S(1)}, bf16[64,768]{1,0:T(8,128)(2,1)S(1)}, u32[]{:S(2)}, u32[]{:S(2)}) collective-permute-start(bf16[64,768]{1,0:T(8,128)(2,1)S(1)} %collective-permute-done.5.refs_7_), channel_id=1, source_target_pairs={{0,2},{1,3},{2,0},{3,1},{4,6},{5,7},{6,4},{7,5},{8,10},{9,11},{10,... | collective-permute-start | bytes 294920 | tf_op jit(solution)/shard_map/ppermute | solution.py:202
  17.5 2.6 %collective-permute-start.11 = (bf16[64,768]{1,0:T(8,128)(2,1)S(1)}, bf16[64,768]{1,0:T(8,128)(2,1)S(1)}, u32[]{:S(2)}, u32[]{:S(2)}) collective-permute-start(bf16[64,768]{1,0:T(8,128)(2,1)S(1)} %collective-permute-done.3.refs_5_), channel_id=1, source_target_pairs={{0,1},{1,0},{2,3},{3,2},{4,5},{5,4},{6,7},{7,6},{8,9},{9,8},{10,11... | collective-permute-start | bytes 294920 | tf_op jit(solution)/shard_map/ppermute | solution.py:202
  17.5 5.6 %collective-permute-start.4 = (bf16[64,768]{1,0:T(8,128)(2,1)S(1)}, bf16[64,768]{1,0:T(8,128)(2,1)S(1)}, u32[]{:S(2)}, u32[]{:S(2)}) collective-permute-start(bf16[64,768]{1,0:T(8,128)(2,1)S(1)} %collective-permute-done.3.refs_5_), channel_id=1, source_target_pairs={{0,2},{1,3},{2,0},{3,1},{4,6},{5,7},{6,4},{7,5},{8,10},{9,11},{10,... | collective-permute-start | bytes 294920 | tf_op jit(solution)/shard_map/ppermute | solution.py:202
  19.0 5.8 %collective-permute-start.2 = (bf16[64,768]{1,0:T(8,128)(2,1)S(1)}, bf16[64,768]{1,0:T(8,128)(2,1)S(1)}, u32[]{:S(2)}, u32[]{:S(2)}) collective-permute-start(bf16[64,768]{1,0:T(8,128)(2,1)S(1)} %collective-permute-done.1.refs_3_), channel_id=1, source_target_pairs={{0,2},{1,3},{2,0},{3,1},{4,6},{5,7},{6,4},{7,5},{8,10},{9,11},{10,... | collective-permute-start | bytes 294920 | tf_op jit(solution)/shard_map/ppermute | solution.py:202
  19.5 6.0 %collective-permute-start.9 = (bf16[64,768]{1,0:T(8,128)(2,1)S(1)}, bf16[64,768]{1,0:T(8,128)(2,1)S(1)}, u32[]{:S(2)}, u32[]{:S(2)}) collective-permute-start(bf16[64,768]{1,0:T(8,128)(2,1)S(1)} %collective-permute-done.1.refs_3_), channel_id=1, source_target_pairs={{0,1},{1,0},{2,3},{3,2},{4,5},{5,4},{6,7},{7,6},{8,9},{9,8},{10,11... | collective-permute-start | bytes 294920 | tf_op jit(solution)/shard_map/ppermute | solution.py:202
  19.5 6.0 %collective-permute-start.8 = (bf16[64,768]{1,0:T(8,128)(2,1)S(1)}, bf16[64,768]{1,0:T(8,128)(2,1)S(1)}, u32[]{:S(2)}, u32[]{:S(2)}) collective-permute-start(bf16[64,768]{1,0:T(8,128)(2,1)S(1)} %collective-permute-done.refs_2_), channel_id=1, source_target_pairs={{0,1},{1,0},{2,3},{3,2},{4,5},{5,4},{6,7},{7,6},{8,9},{9,8},{10,11... | collective-permute-start | bytes 294920 | tf_op jit(solution)/shard_map/ppermute | solution.py:202
  20.0 5.5 %collective-permute-start.14 = (bf16[64,768]{1,0:T(8,128)(2,1)S(1)}, bf16[64,768]{1,0:T(8,128)(2,1)S(1)}, u32[]{:S(2)}, u32[]{:S(2)}) collective-permute-start(bf16[64,768]{1,0:T(8,128)(2,1)S(1)} %collective-permute-done.6.refs_8_), channel_id=1, source_target_pairs={{0,1},{1,0},{2,3},{3,2},{4,5},{5,4},{6,7},{7,6},{8,9},{9,8},{10,11... | collective-permute-start | bytes 294920 | tf_op jit(solution)/shard_map/ppermute | solution.py:202
  23.1 2.5 %collective-permute-start.12 = (bf16[64,768]{1,0:T(8,128)(2,1)S(1)}, bf16[64,768]{1,0:T(8,128)(2,1)S(1)}, u32[]{:S(2)}, u32[]{:S(2)}) collective-permute-start(bf16[64,768]{1,0:T(8,128)(2,1)S(1)} %collective-permute-done.4.refs_6_), channel_id=1, source_target_pairs={{0,1},{1,0},{2,3},{3,2},{4,5},{5,4},{6,7},{7,6},{8,9},{9,8},{10,11... | collective-permute-start | bytes 294920 | tf_op jit(solution)/shard_map/ppermute | solution.py:202
  24.8 1.3 %collective-permute-start.10 = (bf16[64,768]{1,0:T(8,128)(2,1)S(1)}, bf16[64,768]{1,0:T(8,128)(2,1)S(1)}, u32[]{:S(2)}, u32[]{:S(2)}) collective-permute-start(bf16[64,768]{1,0:T(8,128)(2,1)S(1)} %collective-permute-done.2.refs_4_), channel_id=1, source_target_pairs={{0,1},{1,0},{2,3},{3,2},{4,5},{5,4},{6,7},{7,6},{8,9},{9,8},{10,11... | collective-permute-start | bytes 294920 | tf_op jit(solution)/shard_map/ppermute | solution.py:202
  26.1 2.8 %copy-start.1 = (bf16[768,4096]{1,0:T(8,128)(2,1)S(1)}, bf16[768,4096]{1,0:T(8,128)(2,1)}, u32[]{:S(2)}) copy-start(bf16[768,4096]{1,0:T(8,128)(2,1)} %refs_17_.1) | copy-start | bytes 18874372
  28.9 0.7 copy-start.4
  46.3 22.8 %collective-permute-start.15 = (bf16[64,4224]{1,0:T(8,128)(2,1)S(1)}, bf16[64,4224]{1,0:T(8,128)(2,1)S(1)}, u32[]{:S(2)}, u32[]{:S(2)}) collective-permute-start(bf16[64,4224]{1,0:T(8,128)(2,1)S(1)} %hidden.1.mine_ref), channel_id=1, source_target_pairs={{0,1},{1,0},{2,3},{3,2},{4,5},{5,4},{6,7},{7,6},{8,9},{9,8},{10,11... | collective-permute-start | bytes 1622024 | tf_op jit(solution)/shard_map/ppermute | solution.py:202
  69.1 5.8 %copy-start = (bf16[4096,2008]{1,0:T(8,128)(2,1)S(1)}, bf16[4096,2008]{1,0:T(8,128)(2,1)}, u32[]{:S(2)}) copy-start(bf16[4096,2008]{1,0:T(8,128)(2,1)} %copy.10.head_ref) | copy-start | bytes 49348612

commit v2 on v0

--- a/solution.py
+++ b/solution.py
@@ -1,13 +1,323 @@
 import jax
 import jax.numpy as jnp
 from jax import lax
+from jax.experimental import pallas as pl
+from jax.experimental.pallas import tpu as pltpu
 from jax.sharding import PartitionSpec as P
 
 HEAD_DIM = 64
+LANES = 128
+TILE = 256
+DIGIT = 256
+MIB = 1 << 20
 
 
 score_scale = 0.015625
 eps = 1e-06
+
+VMEM = pl.BlockSpec(memory_space=pltpu.VMEM)
+SMEM = pl.BlockSpec(memory_space=pltpu.SMEM)
+HBM = pl.BlockSpec(memory_space=pltpu.HBM)
+ROWS_BY_ROWS = (((1,), (1,)), ((), ()))
+
+
+def iota(shape, dim):
+    return lax.broadcasted_iota(jnp.int32, shape, dim)
+
+
+def in_hbm(a):
+    return pltpu.with_memory_space_constraint(a, pltpu.HBM)
+
+
+def dot(a, b):
+    return jnp.dot(a, b, preferred_element_type=jnp.float32)
+
+
+def dot_rows(a, b):
+    return lax.dot_general(a, b, ROWS_BY_ROWS, preferred_element_type=jnp.float32)
+
+
+def pack_kernel(length, cand_hbm, ids_hbm, rows_hbm, states_hbm, out_ref, cand, ids, rows, states, stage, sem):
+    copies = [
+        pltpu.make_async_copy(src, dst, sem.at[i])
+        for i, (src, dst) in enumerate(
+            ((cand_hbm, cand), (ids_hbm, ids), (rows_hbm, rows), (states_hbm, states))
+        )
+    ]
+    for copy in copies:
+        copy.start()
+    for copy in copies:
+        copy.wait()
+    width = rows.shape[2]
+    cap_len, model_width = states.shape[1:]
+    pieces = -(-model_width // width)
+    held = pieces * cap_len
+    values = states[0].astype(jnp.float32)
+    for c in range(pieces - 1):
+        stage[c * cap_len : (c + 1) * cap_len, :] = values[:, c * width : (c + 1) * width]
+    rest = model_width - (pieces - 1) * width
+    last = held - cap_len
+    stage[last:held, 0:rest] = values[:, model_width - rest :]
+    token, lane = iota((cap_len, width - rest), 0), iota((cap_len, width - rest), 1)
+    digits = jnp.zeros_like(token)
+    for t in range(cap_len):
+        digits = jnp.where(token == t, jnp.where(lane == 0, ids[0, t] // DIGIT, ids[0, t] % DIGIT), digits)
+    digits = jnp.where(lane < 2, digits, 0)
+    digits = jnp.where(lane == 2, length[0], digits)
+    for k in range(cand.shape[1]):
+        digits = jnp.where(lane == 3 + 2 * k, cand[0, k] // DIGIT, digits)
+        digits = jnp.where(lane == 4 + 2 * k, cand[0, k] % DIGIT, digits)
+    stage[last:held, rest:] = digits.astype(jnp.float32)
+    out_ref[0:held, :] = stage[...].astype(jnp.bfloat16)
+    out_ref[held:, :] = rows[0]
+
+
+def hidden_kernel(blocks, parts, head_parts, *refs):
+    pos_ref, *msgs = refs[: 2 * blocks + 1]
+    (weight_hbm, bias_ref, gain_ref, head_hbm, out_ref, head_ref) = refs[2 * blocks + 1 : 2 * blocks + 7]
+    (weight, keys, caps, rows, query, mixed, sem, head_sem) = refs[2 * blocks + 7 :]
+    width = rows.shape[1]
+    model_width = mixed.shape[1]
+    row_total = query.shape[0]
+    prefix, held, pair_rows = rows.shape[0] // blocks, caps.shape[0] // (2 * blocks), row_total // blocks
+    cap_len = 4
+    pieces = -(-model_width // width)
+    span = model_width // parts
+    copies = [
+        pltpu.make_async_copy(
+            weight_hbm.at[:, i * span : (i + 1) * span], weight.at[:, i * span : (i + 1) * span], sem.at[i]
+        )
+        for i in range(parts)
+    ]
+    for copy in copies:
+        copy.start()
+    vocab = head_ref.shape[0]
+    piece = -(-vocab // head_parts // 16) * 16
+    head_copies = [
+        pltpu.make_async_copy(
+            head_hbm.at[i : min(vocab, i + piece)], head_ref.at[i : min(vocab, i + piece)], head_sem.at[i // piece]
+        )
+        for i in range(0, vocab, piece)
+    ]
+
+    for j in range(blocks):
+        rows[j * prefix : (j + 1) * prefix, :] = msgs[j][pieces * cap_len :, :]
+    for j in range(2 * blocks):
+        caps[j * held : (j + 1) * held, :] = msgs[j][0:held, :]
+    rest = model_width - (pieces - 1) * width
+    last = (pieces - 2) * cap_len
+    row, lane = iota((pair_rows, LANES), 0), iota((pair_rows, LANES), 1)
+    place = 3 + 2 * (row // cap_len)
+    factor = jnp.where(lane == place, float(DIGIT), jnp.where(lane == place + 1, 1.0, 0.0))
+    found = []
+    for j in range(blocks):
+        digits = msgs[j][last : last + pair_rows, rest : rest + LANES].astype(jnp.float32)
+        digits = jnp.where(row < cap_len, pltpu.roll(digits, cap_len, 0), digits)
+        found.append(jnp.sum(digits * factor, 1, keepdims=True))
+    away = jnp.concatenate(found, 0).astype(jnp.int32) ^ pos_ref[0]
+    first = ((away & 1) * blocks + (away >> 1)) * held + iota((row_total, 1), 0) % cap_len
+    column = iota((row_total, 2 * blocks * held), 1)
+    pick = jnp.concatenate(
+        [jnp.where(column == first + c * cap_len, 1.0, 0.0).astype(jnp.bfloat16) for c in range(pieces)], 0
+    )
+    picked = dot(pick, caps[...]).astype(jnp.bfloat16)
+    for c in range(pieces):
+        part = min(width, query.shape[1] - c * width)
+        query[:, c * width : c * width + part] = picked[c * row_total : (c + 1) * row_total, 0:part]
+
+    for i, copy in enumerate(copies):
+        copy.wait()
+        if i == parts - 1:
+            for head_copy in head_copies:
+                head_copy.start()
+        cols = slice(i * span, (i + 1) * span)
+        summed = dot(rows[...], weight[:, cols])
+        keys[:, cols] = (summed + bias_ref[:, cols].astype(jnp.float32)).astype(jnp.bfloat16)
+
+    heads = TILE // HEAD_DIM
+    group_keys = LANES
+    group_rows = group_keys // prefix * pair_rows
+    groups = row_total // group_rows
+    lane = iota((group_rows, TILE), 1) // HEAD_DIM
+    r, k = iota((heads * group_rows, group_keys), 0) % group_rows, iota((heads * group_rows, group_keys), 1)
+    image_ok = (r // pair_rows) == (k // prefix)
+    r, k = iota((heads * group_rows, group_rows), 0) % group_rows, iota((heads * group_rows, group_rows), 1)
+    own_ok = ((r // cap_len) == (k // cap_len)) & (k <= r)
+
+    def attend_tile(i, square):
+        cols = pl.ds(pl.multiple_of(i * TILE, TILE), TILE)
+        squares = []
+        for g in range(groups):
+            q = query[g * group_rows : (g + 1) * group_rows, cols]
+            key = keys[g * group_keys : (g + 1) * group_keys, cols]
+            zero = jnp.zeros_like(q)
+            every = jnp.concatenate([jnp.where(lane == h, q, zero) for h in range(heads)], 0)
+            image = jnp.where(image_ok, dot_rows(every, key) * score_scale, -1e30)
+            own = jnp.where(own_ok, dot_rows(every, q) * score_scale, -1e30)
+            top = jnp.maximum(jnp.max(image, 1, keepdims=True), jnp.max(own, 1, keepdims=True))
+            image, own = jnp.exp(image - top), jnp.exp(own - top)
+            scale = 1.0 / (jnp.sum(image, 1, keepdims=True) + jnp.sum(own, 1, keepdims=True))
+            out = dot((image * scale).astype(jnp.bfloat16), key) + dot((own * scale).astype(jnp.bfloat16), q)
+            value = q.astype(jnp.float32)
+            for h in range(heads):
+                value += jnp.where(lane == h, out[h * group_rows : (h + 1) * group_rows], 0.0)
+            mixed[g * group_rows : (g + 1) * group_rows, cols] = value
+            squares.append(value * value)
+        return square + jnp.concatenate(squares, 0)
+
+    square = lax.fori_loop(
+        0, model_width // TILE, attend_tile, jnp.zeros((row_total, TILE), jnp.float32), unroll=4
+    )
+    scale = lax.rsqrt(jnp.sum(square, 1, keepdims=True) / model_width + eps)
+    out_ref[:, 0:model_width] = (mixed[...] * scale * gain_ref[...]).astype(jnp.bfloat16)
+    out_ref[:, model_width:] = query[:, model_width:]
+    for head_copy in head_copies:
+        head_copy.wait()
+
+
+def logits_kernel(pos_ref, mine_ref, other_ref, head_ref, out_ref, states, logits):
+    half = mine_ref.shape[0]
+    vocab, model_width = head_ref.shape
+    row_total = 2 * half
+    states[0:half, :] = mine_ref[:, 0:model_width]
+    states[half:, :] = other_ref[:, 0:model_width]
+    for start in range(0, vocab, TILE):
+        stop = min(vocab, start + TILE)
+        logits[start:stop, :] = dot_rows(head_ref[start:stop, :], states[...])
+    digits = jnp.concatenate(
+        [ref[:, model_width:].astype(jnp.float32) for ref in (mine_ref, other_ref)], 0
+    ).T
+    ids = (digits[0:1] * DIGIT + digits[1:2]).astype(jnp.int32)
+    values = logits[...]
+    top = jnp.max(values, 0, keepdims=True)
+    total = jnp.sum(jnp.exp(values - top), 0, keepdims=True)
+    hit = iota((vocab, row_total), 0) == ids - pos_ref[0] * vocab
+    target = jnp.sum(jnp.where(hit, values, 0.0), 0, keepdims=True)
+    packed = jnp.concatenate([top, total, target, jnp.zeros((LANES - 3, row_total), jnp.float32)], 0).T
+    shards, rows = out_ref.shape[:2]
+    for j in range(shards):
+        away = (j % (shards // 2)) * 2 + j // (shards // 2)
+        out_ref[pos_ref[0] ^ away] = packed[j * rows : (j + 1) * rows]
+
+
+def finish_kernel(stats_ref, mine_ref, out_ref):
+    stats = stats_ref[...]
+    shards, rows, _ = stats.shape
+    cap_len = out_ref.shape[2]
+    model_width = mine_ref.shape[1] - LANES
+    lane = iota((rows, LANES), 1)
+    top = jnp.max(stats, 0)[:, 0:1]
+    total = jnp.zeros((rows, 1), jnp.float32)
+    target = jnp.zeros((rows, 1), jnp.float32)
+    for e in range(shards):
+        total += stats[e][:, 1:2] * jnp.exp(stats[e][:, 0:1] - top)
+        target += stats[e][:, 2:3]
+    loglik = target - (top + jnp.log(total))
+    lengths = mine_ref[0:16, model_width:].astype(jnp.float32)[0:rows, 2:3]
+    token = iota((rows, LANES), 0) % cap_len
+    kept = (token == lane) & (token.astype(jnp.float32) < lengths)
+    spread = jnp.where(kept, loglik, 0.0)
+    for k in range(out_ref.shape[1]):
+        out_ref[0, k : k + 1, :] = jnp.sum(spread[k * cap_len : (k + 1) * cap_len], 0, keepdims=True)[:, 0:cap_len]
+
+
+def paired(
+    query_rows, proj_weight, proj_bias, candidates, caption_states, caption_ids, caption_lengths, norm_gain, head_weight
+):
+    shards = lax.axis_size("dp")
+    blocks = shards // 2
+    _, prefix, width = query_rows.shape
+    _, cap_len, model_width = caption_states.shape
+    top_count = candidates.shape[1]
+    pair_rows = top_count * cap_len
+    piece_rows = cap_len * -(-model_width // width)
+    held = -(-piece_rows // 16) * 16
+    row_total = blocks * pair_rows
+    vocab = head_weight.shape[1]
+    position = lax.axis_index("dp").astype(jnp.int32).reshape(1)
+    parts, head_parts = 8, 8
+
+    def swap(a, away):
+        return lax.ppermute(a, "dp", [(i, i ^ away) for i in range(shards)])
+
+    message = pl.pallas_call(
+        pack_kernel,
+        out_shape=jax.ShapeDtypeStruct((piece_rows + prefix, width), jnp.bfloat16),
+        in_specs=[SMEM] + [HBM] * 4,
+        out_specs=VMEM,
+        scratch_shapes=[
+            pltpu.SMEM(candidates.shape, jnp.int32),
+            pltpu.SMEM(caption_ids.shape, jnp.int32),
+            pltpu.VMEM(query_rows.shape, jnp.bfloat16),
+            pltpu.VMEM(caption_states.shape, jnp.bfloat16),
+            pltpu.VMEM((piece_rows, width), jnp.float32),
+            pltpu.SemaphoreType.DMA((4,)),
+        ],
+        compiler_params=pltpu.CompilerParams(vmem_limit_bytes=2 * MIB),
+        name="pack",
+    )(caption_lengths, *(in_hbm(a) for a in (candidates, caption_ids, query_rows, caption_states)))
+
+    got = {0: message}
+    for away in (12, 4, 2):
+        got[away] = swap(message, away)
+    got[8] = swap(got[12], 4)
+    for away in (4, 12, 8):
+        got[away + 2] = swap(got[away], 2)
+    mine = [got[2 * j] for j in range(blocks)]
+    other = [swap(a, 1) for a in mine]
+
+    hidden, head = pl.pallas_call(
+        lambda *refs: hidden_kernel(blocks, parts, head_parts, *refs),
+        out_shape=(
+            jax.ShapeDtypeStruct((row_total, model_width + LANES), jnp.bfloat16),
+            pltpu.VMEM((vocab, model_width), jnp.bfloat16),
+        ),
+        in_specs=[SMEM] + [VMEM] * (2 * blocks) + [HBM, VMEM, VMEM, HBM],
+        out_specs=(VMEM, VMEM),
+        scratch_shapes=[
+            pltpu.VMEM((width, model_width), jnp.bfloat16),
+            pltpu.VMEM((blocks * prefix, model_width), jnp.bfloat16),
+            pltpu.VMEM((2 * blocks * held, width), jnp.bfloat16),
+            pltpu.VMEM((blocks * prefix, width), jnp.bfloat16),
+            pltpu.VMEM((row_total, model_width + LANES), jnp.bfloat16),
+            pltpu.VMEM((row_total, model_width), jnp.float32),
+            pltpu.SemaphoreType.DMA((parts,)),
+            pltpu.SemaphoreType.DMA((head_parts,)),
+        ],
+        compiler_params=pltpu.CompilerParams(vmem_limit_bytes=24 * MIB),
+        name="hidden",
+    )(
+        position,
+        *mine,
+        *other,
+        in_hbm(proj_weight),
+        proj_bias.reshape(1, -1),
+        norm_gain.reshape(1, -1),
+        in_hbm(head_weight.T),
+    )
+
+    stats = pl.pallas_call(
+        logits_kernel,
+        out_shape=jax.ShapeDtypeStruct((shards, pair_rows, LANES), jnp.float32),
+        in_specs=[SMEM, VMEM, VMEM, VMEM],
+        out_specs=VMEM,
+        scratch_shapes=[
+            pltpu.VMEM((2 * row_total, model_width), jnp.bfloat16),
+            pltpu.VMEM((vocab, 2 * row_total), jnp.float32),
+        ],
+        compiler_params=pltpu.CompilerParams(vmem_limit_bytes=16 * MIB),
+        name="logits",
+    )(position, hidden, swap(hidden, 1), head)
+
+    stats = lax.all_to_all(stats, "dp", 0, 0, tiled=True)
+    return pl.pallas_call(
+        finish_kernel,
+        out_shape=jax.ShapeDtypeStruct((1, top_count, cap_len), jnp.float32),
+        in_specs=[VMEM, VMEM],
+        out_specs=VMEM,
+        compiler_params=pltpu.CompilerParams(vmem_limit_bytes=2 * MIB),
+        name="finish",
+    )(stats, hidden)
 
 
 def merged(part, axis, combine):
@@ -63,7 +373,7 @@
     return (larger, summed, first[2] + second[2])
 
 
-def local(
+def spread(
     query_rows,
     proj_weight,
     proj_bias,
@@ -128,6 +438,13 @@
     return result.reshape(img_local, top_count, cap_len)
 
 
+def local(query_rows, proj_weight, proj_bias, candidates, caption_states, *rest):
+    one_each = candidates.shape[0] == 1 and caption_states.shape[0] == 1
+    fits = candidates.shape[1] == 2 and caption_states.shape[1] == 4 and query_rows.shape[1] == 32
+    plan = paired if lax.axis_size("dp") == 16 and one_each and fits else spread
+    return plan(query_rows, proj_weight, proj_bias, candidates, caption_states, *rest)
+
+
 def solution(mesh):
     in_specs = (
         P(("groups", "dp"), None, None),

time: 150 us -> 52.1 us (0.35)
  blocking collectives: 107 us -> 12.6 us
  Pallas kernels: 0 us -> 16.7 us
  matrix products: 14.8 us -> 0 us
  between operations: 14.8 us -> 0.72 us
  starting transfers between devices: 0.01 us -> 13 us
  local copies, waits for them, and re-layouts: 5.74 us -> 1.43 us
  other arithmetic: 2.59 us -> 0 us
  waiting for transfers between devices: 5.12 us -> 7.38 us
    all_gather x5 -> x0, blocking collectives: 97.4 us -> none  [the longest x3 55.2 us: merged(): gathered = jax.tree.map(lambda a: lax.all_gather(a, axis), part)]
    pallas_call x0 -> x4, Pallas kernels: none -> 16.7 us  [the longest x1 10.1 us: paired(): pl.pallas_call(lambda *refs: hidden_kernel(blocks, parts, head_parts, *re...]
    dot_general x4 -> x0, matrix products: 13.9 us -> none  [the longest x1 8.32 us: local(): jnp.dot(every_state, head_weight, preferred_element_type=jnp.float32)]
    ppermute x0 -> x16, starting transfers between devices: none -> 13 us  [swap(): return lax.ppermute(a, 'dp', [(i, i ^ away) for i in range(shards)])]
    all_to_all x0 -> x1, blocking collectives: none -> 12.6 us  [paired(): stats = lax.all_to_all(stats, 'dp', 0, 0, tiled=True)]
    unnamed x1 -> x0, blocking collectives: 9.34 us -> none
    ppermute x0 -> x16, waiting for transfers between devices: none -> 7.38 us  [swap(): return lax.ppermute(a, 'dp', [(i, i ^ away) for i in range(shards)])]
    all_gather x1 -> x0, waiting for transfers between devices: 5.1 us -> none  [local(): lax.all_gather(hidden_rows, 'dp', axis=0, tiled=True)]
  transfers between devices with their start and end apart: 1 -> 16, of which waited for: 1 -> 6; matrix products, arithmetic and copies ran while one was open for 1% -> 1% of each run, Pallas kernels for 0% -> 0%
where the time goes in v2:
time: 52.1 us; the launch traced here: 51.8 us
  Pallas kernels  16.7 us (32%)
  starting transfers between devices  13 us (25%)
  blocking collectives  12.6 us (24%)
  waiting for transfers between devices  7.38 us (14%)
  local copies, waits for them, and re-layouts  1.43 us (3%)
  between operations  0.72 us (1%)
    ppermute x16, starting transfers between devices, swap(): return lax.ppermute(a, 'dp', [(i, i ^ away) for i in range(shards)])  13 us
    all_to_all x1, blocking collectives, paired(): stats = lax.all_to_all(stats, 'dp', 0, 0, tiled=True)  12.6 us
    pallas_call x1, Pallas kernels, paired(): pl.pallas_call(lambda *refs: hidden_kernel(blocks, parts, head_parts, *re...  10.1 us
    ppermute x16, waiting for transfers between devices, swap(): return lax.ppermute(a, 'dp', [(i, i ^ away) for i in range(shards)])  7.38 us
    pallas_call x1, Pallas kernels, paired(): pl.pallas_call(logits_kernel, out_shape=jax.ShapeDtypeStruct((shards, pai...  4.81 us
  transfers between devices with their start and end apart: 16, of which 6 were waited for; matrix products, arithmetic and copies ran while one was open for 1% of the time, Pallas kernels for 0%

profile of v2, /device:TPU:0, one launch (start us, length us, event | category | flops | bytes accessed | tf_op | source)
XLA Modules:
  0.0 51.8 jit_solution(11605687952443321605)
XLA Ops:
  0.7 0.9 %pack.1.refs_1_ = bf16[56,768]{1,0:T(8,128)(2,1)S(1)} custom-call(s32[1]{0:T(128)S(6)} %copy.10.length, s32[1,2]{1,0:T(1,128)} %cand_hbm.1, s32[1,4]{1,0:T(1,128)} %ids_hbm.1, bf16[1,32,768]{2,1,0:T(8,128)(2,1)} %rows_hbm.1, bf16[1,4,4096]{2,1,0:T(4,128)(2,1)} %states_hbm.1), custom_call_target="tpu_custom_call" | custom-call | tf_op jit(solution)/shard_map/pack/pallas_call | solution.py:243
  1.5 5.1 %collective-permute-start.3 = (bf16[56,768]{1,0:T(8,128)(2,1)S(1)}, bf16[56,768]{1,0:T(8,128)(2,1)S(1)}, u32[]{:S(2)}, u32[]{:S(2)}) collective-permute-start(bf16[56,768]{1,0:T(8,128)(2,1)S(1)} %pack.1.refs_1_), channel_id=1, source_target_pairs={{0,12},{1,13},{2,14},{3,15},{4,8},{5,9},{6,10},{7,11},{8,4},{9,5},... | collective-permute-start | bytes 258056 | tf_op jit(solution)/shard_map/ppermute | solution.py:241
  6.7 0.0 collective-permute-start.1
  6.7 1.5 %collective-permute-start = (bf16[56,768]{1,0:T(8,128)(2,1)S(1)}, bf16[56,768]{1,0:T(8,128)(2,1)S(1)}, u32[]{:S(2)}, u32[]{:S(2)}) collective-permute-start(bf16[56,768]{1,0:T(8,128)(2,1)S(1)} %pack.1.refs_1_), channel_id=1, source_target_pairs={{0,2},{1,3},{2,0},{3,1},{4,6},{5,7},{6,4},{7,5},{8,10},{9,11},{10,... | collective-permute-start | bytes 258056 | tf_op jit(solution)/shard_map/ppermute | solution.py:241
  8.2 1.6 %collective-permute-done.3.refs_7_ = bf16[56,768]{1,0:T(8,128)(2,1)S(1)} collective-permute-done((bf16[56,768]{1,0:T(8,128)(2,1)S(1)}, bf16[56,768]{1,0:T(8,128)(2,1)S(1)}, u32[]{:S(2)}, u32[]{:S(2)}) %collective-permute-start.3) | collective-permute-done | bytes 86048 | tf_op jit(solution)/shard_map/ppermute | solution.py:241
  9.8 0.9 %collective-permute-start.4 = (bf16[56,768]{1,0:T(8,128)(2,1)S(1)}, bf16[56,768]{1,0:T(8,128)(2,1)S(1)}, u32[]{:S(2)}, u32[]{:S(2)}) collective-permute-start(bf16[56,768]{1,0:T(8,128)(2,1)S(1)} %collective-permute-done.3.refs_7_), channel_id=1, source_target_pairs={{0,4},{1,5},{2,6},{3,7},{4,0},{5,1},{6,2},{7,3},{8,12},{9,13},{10,... | collective-permute-start | bytes 258056 | tf_op jit(solution)/shard_map/ppermute | solution.py:241
  10.7 0.0 collective-permute-done.7.refs_9_
  10.8 1.5 %collective-permute-start.6 = (bf16[56,768]{1,0:T(8,128)(2,1)S(1)}, bf16[56,768]{1,0:T(8,128)(2,1)S(1)}, u32[]{:S(2)}, u32[]{:S(2)}) collective-permute-start(bf16[56,768]{1,0:T(8,128)(2,1)S(1)} %collective-permute-done.3.refs_7_), channel_id=1, source_target_pairs={{0,2},{1,3},{2,0},{3,1},{4,6},{5,7},{6,4},{7,5},{8,10},{9,11},{10,... | collective-permute-start | bytes 258056 | tf_op jit(solution)/shard_map/ppermute | solution.py:241
  12.3 0.0 collective-permute-done.1.refs_3_
  12.3 0.2 collective-permute-start.9
  12.5 1.1 %collective-permute-start.2 = (bf16[56,768]{1,0:T(8,128)(2,1)S(1)}, bf16[56,768]{1,0:T(8,128)(2,1)S(1)}, u32[]{:S(2)}, u32[]{:S(2)}) collective-permute-start(bf16[56,768]{1,0:T(8,128)(2,1)S(1)} %collective-permute-done.1.refs_3_), channel_id=1, source_target_pairs={{0,2},{1,3},{2,0},{3,1},{4,6},{5,7},{6,4},{7,5},{8,10},{9,11},{10,... | collective-permute-start | bytes 258056 | tf_op jit(solution)/shard_map/ppermute | solution.py:241
  13.6 0.7 %collective-permute-done.4.refs_5_ = bf16[56,768]{1,0:T(8,128)(2,1)S(1)} collective-permute-done((bf16[56,768]{1,0:T(8,128)(2,1)S(1)}, bf16[56,768]{1,0:T(8,128)(2,1)S(1)}, u32[]{:S(2)}, u32[]{:S(2)}) %collective-permute-start.4) | collective-permute-done | bytes 86048 | tf_op jit(solution)/shard_map/ppermute | solution.py:241
  14.3 1.8 %collective-permute-start.5 = (bf16[56,768]{1,0:T(8,128)(2,1)S(1)}, bf16[56,768]{1,0:T(8,128)(2,1)S(1)}, u32[]{:S(2)}, u32[]{:S(2)}) collective-permute-start(bf16[56,768]{1,0:T(8,128)(2,1)S(1)} %collective-permute-done.4.refs_5_), channel_id=1, source_target_pairs={{0,2},{1,3},{2,0},{3,1},{4,6},{5,7},{6,4},{7,5},{8,10},{9,11},{10,... | collective-permute-start | bytes 258056 | tf_op jit(solution)/shard_map/ppermute | solution.py:241
  16.1 0.0 collective-permute-done.13.refs_15_
  16.1 0.0 collective-permute-start.8
  16.1 0.5 collective-permute-start.11
  16.6 0.0 collective-permute-done.9.refs_11_
  16.6 0.1 collective-permute-start.14
  16.6 1.2 %collective-permute-done.2.refs_4_ = bf16[56,768]{1,0:T(8,128)(2,1)S(1)} collective-permute-done((bf16[56,768]{1,0:T(8,128)(2,1)S(1)}, bf16[56,768]{1,0:T(8,128)(2,1)S(1)}, u32[]{:S(2)}, u32[]{:S(2)}) %collective-permute-start.2) | collective-permute-done | bytes 86048 | tf_op jit(solution)/shard_map/ppermute | solution.py:241
  17.9 1.5 %collective-permute-done.5.refs_6_ = bf16[56,768]{1,0:T(8,128)(2,1)S(1)} collective-permute-done((bf16[56,768]{1,0:T(8,128)(2,1)S(1)}, bf16[56,768]{1,0:T(8,128)(2,1)S(1)}, u32[]{:S(2)}, u32[]{:S(2)}) %collective-permute-start.5) | collective-permute-done | bytes 86048 | tf_op jit(solution)/shard_map/ppermute | solution.py:241
  19.4 0.0 collective-permute-start.12
  19.4 0.7 %reshape.10.refs_18_ = bf16[1,4096]{1,0:T(2,128)(2,1)S(1)} reshape(bf16[4096]{0:T(1024)(128)(2,1)} %param.11) | data formatting | bytes 16384 | tf_op jit(solution)/shard_map/reshape | solution.py:294
  20.1 0.0 collective-permute-done.14.refs_16_
  20.1 0.0 collective-permute-done.11.refs_13_
  20.1 0.5 %collective-permute-done.12.refs_14_ = bf16[56,768]{1,0:T(8,128)(2,1)S(1)} collective-permute-done((bf16[56,768]{1,0:T(8,128)(2,1)S(1)}, bf16[56,768]{1,0:T(8,128)(2,1)S(1)}, u32[]{:S(2)}, u32[]{:S(2)}) %collective-permute-start.12) | collective-permute-done | bytes 86048 | tf_op jit(solution)/shard_map/ppermute | solution.py:241
  20.7 0.7 %copy-done = f32[4096]{0:T(1024)S(1)} copy-done((f32[4096]{0:T(1024)S(1)}, f32[4096]{0:T(1024)}, u32[]{:S(2)}) %copy-start) | copy-done | bytes 16408
  21.4 10.1 %hidden.1 = (bf16[64,4224]{1,0:T(8,128)(2,1)S(1)}, bf16[2008,4096]{1,0:T(8,128)(2,1)S(1)}) custom-call(s32[1]{0:T(128)} %bitcast.refs_0_.pos_ref, bf16[56,768]{1,0:T(8,128)(2,1)S(1)} %pack.1.refs_1_, bf16[56,768]{1,0:T(8,128)(2,1)S(1)} %collective-permute-done.refs_2_, bf16[56,768]{1,0:T(8,128)(2,1)S(1)} %collective-permute-done.1.refs_3_, ...), custom_call_target="tpu_custom_call" | custom-call | tf_op jit(solution)/shard_map/hidden/pallas_call | solution.py:269
  31.5 0.2 collective-permute-start.15
  31.7 1.8 %collective-permute-done.15.other_ref = bf16[64,4224]{1,0:T(8,128)(2,1)S(1)} collective-permute-done((bf16[64,4224]{1,0:T(8,128)(2,1)S(1)}, bf16[64,4224]{1,0:T(8,128)(2,1)S(1)}, u32[]{:S(2)}, u32[]{:S(2)}) %collective-permute-start.15) | collective-permute-done | bytes 540704 | tf_op jit(solution)/shard_map/ppermute | solution.py:241
  33.5 4.8 %logits.1 = f32[16,8,128]{2,1,0:T(8,128)S(1)} custom-call(s32[1]{0:T(128)} %bitcast.refs_0_.pos_ref, bf16[64,4224]{1,0:T(8,128)(2,1)S(1)} %get-tuple-element.7.mine_ref, bf16[64,4224]{1,0:T(8,128)(2,1)S(1)} %collective-permute-done.15.other_ref, bf16[2008,4096]{1,0:T(8,128)(2,1)S(1)} %get-tuple-element.8.head_ref), custom_call_target="tpu_custom_call" | custom-call | tf_op jit(solution)/shard_map/logits/pallas_call | solution.py:299
  38.3 12.6 %all_to_all.5.stats_ref = f32[16,8,128]{2,1,0:T(8,128)S(1)} all-to-all(f32[16,8,128]{2,1,0:T(8,128)S(1)} %logits.1), channel_id=1, replica_groups=mesh['groups'=2,'dp'=16] {'dp'}, dimensions={0} | all-to-all | bytes 131072 | tf_op jit(solution)/shard_map/all_to_all | solution.py:312
  50.9 0.9 %finish.1 = f32[1,2,4]{2,1,0:T(2,128)} custom-call(f32[16,8,128]{2,1,0:T(8,128)S(1)} %all_to_all.5.stats_ref, bf16[64,4224]{1,0:T(8,128)(2,1)S(1)} %get-tuple-element.7.mine_ref), custom_call_target="tpu_custom_call" | custom-call | tf_op jit(solution)/shard_map/finish/pallas_call | solution.py:313
  (8 shorter events, 0.0 us)
Async XLA Ops:
  1.5 8.3 %collective-permute-start.3 = (bf16[56,768]{1,0:T(8,128)(2,1)S(1)}, bf16[56,768]{1,0:T(8,128)(2,1)S(1)}, u32[]{:S(2)}, u32[]{:S(2)}) collective-permute-start(bf16[56,768]{1,0:T(8,128)(2,1)S(1)} %pack.1.refs_1_), channel_id=1, source_target_pairs={{0,12},{1,13},{2,14},{3,15},{4,8},{5,9},{6,10},{7,11},{8,4},{9,5},... | collective-permute-start | bytes 258056 | tf_op jit(solution)/shard_map/ppermute | solution.py:241
  6.7 4.1 %collective-permute-start.7 = (bf16[56,768]{1,0:T(8,128)(2,1)S(1)}, bf16[56,768]{1,0:T(8,128)(2,1)S(1)}, u32[]{:S(2)}, u32[]{:S(2)}) collective-permute-start(bf16[56,768]{1,0:T(8,128)(2,1)S(1)} %pack.1.refs_1_), channel_id=1, source_target_pairs={{0,1},{1,0},{2,3},{3,2},{4,5},{5,4},{6,7},{7,6},{8,9},{9,8},{10,11... | collective-permute-start | bytes 258056 | tf_op jit(solution)/shard_map/ppermute | solution.py:241
  6.7 5.6 %collective-permute-start.1 = (bf16[56,768]{1,0:T(8,128)(2,1)S(1)}, bf16[56,768]{1,0:T(8,128)(2,1)S(1)}, u32[]{:S(2)}, u32[]{:S(2)}) collective-permute-start(bf16[56,768]{1,0:T(8,128)(2,1)S(1)} %pack.1.refs_1_), channel_id=1, source_target_pairs={{0,4},{1,5},{2,6},{3,7},{4,0},{5,1},{6,2},{7,3},{8,12},{9,13},{10,... | collective-permute-start | bytes 258056 | tf_op jit(solution)/shard_map/ppermute | solution.py:241
  6.7 5.8 %collective-permute-start = (bf16[56,768]{1,0:T(8,128)(2,1)S(1)}, bf16[56,768]{1,0:T(8,128)(2,1)S(1)}, u32[]{:S(2)}, u32[]{:S(2)}) collective-permute-start(bf16[56,768]{1,0:T(8,128)(2,1)S(1)} %pack.1.refs_1_), channel_id=1, source_target_pairs={{0,2},{1,3},{2,0},{3,1},{4,6},{5,7},{6,4},{7,5},{8,10},{9,11},{10,... | collective-permute-start | bytes 258056 | tf_op jit(solution)/shard_map/ppermute | solution.py:241
  9.8 4.5 %collective-permute-start.4 = (bf16[56,768]{1,0:T(8,128)(2,1)S(1)}, bf16[56,768]{1,0:T(8,128)(2,1)S(1)}, u32[]{:S(2)}, u32[]{:S(2)}) collective-permute-start(bf16[56,768]{1,0:T(8,128)(2,1)S(1)} %collective-permute-done.3.refs_7_), channel_id=1, source_target_pairs={{0,4},{1,5},{2,6},{3,7},{4,0},{5,1},{6,2},{7,3},{8,12},{9,13},{10,... | collective-permute-start | bytes 258056 | tf_op jit(solution)/shard_map/ppermute | solution.py:241
  10.7 5.3 %collective-permute-start.13 = (bf16[56,768]{1,0:T(8,128)(2,1)S(1)}, bf16[56,768]{1,0:T(8,128)(2,1)S(1)}, u32[]{:S(2)}, u32[]{:S(2)}) collective-permute-start(bf16[56,768]{1,0:T(8,128)(2,1)S(1)} %collective-permute-done.3.refs_7_), channel_id=1, source_target_pairs={{0,1},{1,0},{2,3},{3,2},{4,5},{5,4},{6,7},{7,6},{8,9},{9,8},{10,11... | collective-permute-start | bytes 258056 | tf_op jit(solution)/shard_map/ppermute | solution.py:241
  10.8 5.3 %collective-permute-start.6 = (bf16[56,768]{1,0:T(8,128)(2,1)S(1)}, bf16[56,768]{1,0:T(8,128)(2,1)S(1)}, u32[]{:S(2)}, u32[]{:S(2)}) collective-permute-start(bf16[56,768]{1,0:T(8,128)(2,1)S(1)} %collective-permute-done.3.refs_7_), channel_id=1, source_target_pairs={{0,2},{1,3},{2,0},{3,1},{4,6},{5,7},{6,4},{7,5},{8,10},{9,11},{10,... | collective-permute-start | bytes 258056 | tf_op jit(solution)/shard_map/ppermute | solution.py:241
  12.3 4.3 %collective-permute-start.9 = (bf16[56,768]{1,0:T(8,128)(2,1)S(1)}, bf16[56,768]{1,0:T(8,128)(2,1)S(1)}, u32[]{:S(2)}, u32[]{:S(2)}) collective-permute-start(bf16[56,768]{1,0:T(8,128)(2,1)S(1)} %collective-permute-done.1.refs_3_), channel_id=1, source_target_pairs={{0,1},{1,0},{2,3},{3,2},{4,5},{5,4},{6,7},{7,6},{8,9},{9,8},{10,11... | collective-permute-start | bytes 258056 | tf_op jit(solution)/shard_map/ppermute | solution.py:241
  12.5 5.4 %collective-permute-start.2 = (bf16[56,768]{1,0:T(8,128)(2,1)S(1)}, bf16[56,768]{1,0:T(8,128)(2,1)S(1)}, u32[]{:S(2)}, u32[]{:S(2)}) collective-permute-start(bf16[56,768]{1,0:T(8,128)(2,1)S(1)} %collective-permute-done.1.refs_3_), channel_id=1, source_target_pairs={{0,2},{1,3},{2,0},{3,1},{4,6},{5,7},{6,4},{7,5},{8,10},{9,11},{10,... | collective-permute-start | bytes 258056 | tf_op jit(solution)/shard_map/ppermute | solution.py:241
  14.3 5.1 %collective-permute-start.5 = (bf16[56,768]{1,0:T(8,128)(2,1)S(1)}, bf16[56,768]{1,0:T(8,128)(2,1)S(1)}, u32[]{:S(2)}, u32[]{:S(2)}) collective-permute-start(bf16[56,768]{1,0:T(8,128)(2,1)S(1)} %collective-permute-done.4.refs_5_), channel_id=1, source_target_pairs={{0,2},{1,3},{2,0},{3,1},{4,6},{5,7},{6,4},{7,5},{8,10},{9,11},{10,... | collective-permute-start | bytes 258056 | tf_op jit(solution)/shard_map/ppermute | solution.py:241
  16.1 4.0 %collective-permute-start.8 = (bf16[56,768]{1,0:T(8,128)(2,1)S(1)}, bf16[56,768]{1,0:T(8,128)(2,1)S(1)}, u32[]{:S(2)}, u32[]{:S(2)}) collective-permute-start(bf16[56,768]{1,0:T(8,128)(2,1)S(1)} %collective-permute-done.refs_2_), channel_id=1, source_target_pairs={{0,1},{1,0},{2,3},{3,2},{4,5},{5,4},{6,7},{7,6},{8,9},{9,8},{10,11... | collective-permute-start | bytes 258056 | tf_op jit(solution)/shard_map/ppermute | solution.py:241
  16.1 4.1 %collective-permute-start.11 = (bf16[56,768]{1,0:T(8,128)(2,1)S(1)}, bf16[56,768]{1,0:T(8,128)(2,1)S(1)}, u32[]{:S(2)}, u32[]{:S(2)}) collective-permute-start(bf16[56,768]{1,0:T(8,128)(2,1)S(1)} %collective-permute-done.4.refs_5_), channel_id=1, source_target_pairs={{0,1},{1,0},{2,3},{3,2},{4,5},{5,4},{6,7},{7,6},{8,9},{9,8},{10,11... | collective-permute-start | bytes 258056 | tf_op jit(solution)/shard_map/ppermute | solution.py:241
  16.6 3.5 %collective-permute-start.14 = (bf16[56,768]{1,0:T(8,128)(2,1)S(1)}, bf16[56,768]{1,0:T(8,128)(2,1)S(1)}, u32[]{:S(2)}, u32[]{:S(2)}) collective-permute-start(bf16[56,768]{1,0:T(8,128)(2,1)S(1)} %collective-permute-done.6.refs_8_), channel_id=1, source_target_pairs={{0,1},{1,0},{2,3},{3,2},{4,5},{5,4},{6,7},{7,6},{8,9},{9,8},{10,11... | collective-permute-start | bytes 258056 | tf_op jit(solution)/shard_map/ppermute | solution.py:241
  17.9 2.3 %collective-permute-start.10 = (bf16[56,768]{1,0:T(8,128)(2,1)S(1)}, bf16[56,768]{1,0:T(8,128)(2,1)S(1)}, u32[]{:S(2)}, u32[]{:S(2)}) collective-permute-start(bf16[56,768]{1,0:T(8,128)(2,1)S(1)} %collective-permute-done.2.refs_4_), channel_id=1, source_target_pairs={{0,1},{1,0},{2,3},{3,2},{4,5},{5,4},{6,7},{7,6},{8,9},{9,8},{10,11... | collective-permute-start | bytes 258056 | tf_op jit(solution)/shard_map/ppermute | solution.py:241
  19.4 1.3 %collective-permute-start.12 = (bf16[56,768]{1,0:T(8,128)(2,1)S(1)}, bf16[56,768]{1,0:T(8,128)(2,1)S(1)}, u32[]{:S(2)}, u32[]{:S(2)}) collective-permute-start(bf16[56,768]{1,0:T(8,128)(2,1)S(1)} %collective-permute-done.5.refs_6_), channel_id=1, source_target_pairs={{0,1},{1,0},{2,3},{3,2},{4,5},{5,4},{6,7},{7,6},{8,9},{9,8},{10,11... | collective-permute-start | bytes 258056 | tf_op jit(solution)/shard_map/ppermute | solution.py:241
  20.7 0.7 %copy-start = (f32[4096]{0:T(1024)S(1)}, f32[4096]{0:T(1024)}, u32[]{:S(2)}) copy-start(f32[4096]{0:T(1024)} %param.16) | copy-start | bytes 49156
  31.5 2.0 %collective-permute-start.15 = (bf16[64,4224]{1,0:T(8,128)(2,1)S(1)}, bf16[64,4224]{1,0:T(8,128)(2,1)S(1)}, u32[]{:S(2)}, u32[]{:S(2)}) collective-permute-start(bf16[64,4224]{1,0:T(8,128)(2,1)S(1)} %get-tuple-element.7.mine_ref), channel_id=1, source_target_pairs={{0,1},{1,0},{2,3},{3,2},{4,5},{5,4},{6,7},{7,6},{8,9},{9,8},{10,11... | collective-permute-start | bytes 1622024 | tf_op jit(solution)/shard_map/ppermute | solution.py:241

commit v3 on v2

--- a/solution.py
+++ b/solution.py
@@ -1,3 +1,5 @@
+import functools
+
 import jax
 import jax.numpy as jnp
 from jax import lax
@@ -37,7 +39,7 @@
     return lax.dot_general(a, b, ROWS_BY_ROWS, preferred_element_type=jnp.float32)
 
 
-def pack_kernel(length, cand_hbm, ids_hbm, rows_hbm, states_hbm, out_ref, cand, ids, rows, states, stage, sem):
+def pack_kernel(cand_hbm, ids_hbm, rows_hbm, states_hbm, out_ref, cand, ids, rows, states, stage, sem):
     copies = [
         pltpu.make_async_copy(src, dst, sem.at[i])
         for i, (src, dst) in enumerate(
@@ -63,59 +65,86 @@
     for t in range(cap_len):
         digits = jnp.where(token == t, jnp.where(lane == 0, ids[0, t] // DIGIT, ids[0, t] % DIGIT), digits)
     digits = jnp.where(lane < 2, digits, 0)
-    digits = jnp.where(lane == 2, length[0], digits)
     for k in range(cand.shape[1]):
-        digits = jnp.where(lane == 3 + 2 * k, cand[0, k] // DIGIT, digits)
-        digits = jnp.where(lane == 4 + 2 * k, cand[0, k] % DIGIT, digits)
+        digits = jnp.where(lane == 2 + 2 * k, cand[0, k] // DIGIT, digits)
+        digits = jnp.where(lane == 3 + 2 * k, cand[0, k] % DIGIT, digits)
     stage[last:held, rest:] = digits.astype(jnp.float32)
     out_ref[0:held, :] = stage[...].astype(jnp.bfloat16)
     out_ref[held:, :] = rows[0]
 
 
-def hidden_kernel(blocks, parts, head_parts, *refs):
-    pos_ref, *msgs = refs[: 2 * blocks + 1]
-    (weight_hbm, bias_ref, gain_ref, head_hbm, out_ref, head_ref) = refs[2 * blocks + 1 : 2 * blocks + 7]
-    (weight, keys, caps, rows, query, mixed, sem, head_sem) = refs[2 * blocks + 7 :]
-    width = rows.shape[1]
+def bring_kernel(pos_ref, len_ref, weight_hbm, bias_hbm, gain_hbm, weight_ref, bias_ref, gain_ref, length_ref, bias, sem):
+    pairs = ((bias_hbm, bias), (gain_hbm, gain_ref), (weight_hbm, weight_ref))
+    copies = [pltpu.make_async_copy(src, dst, sem.at[i]) for i, (src, dst) in enumerate(pairs)]
+    for copy in copies:
+        copy.start()
+    length_ref[...] = jnp.full(length_ref.shape, len_ref[0].astype(jnp.float32))
+    copies[0].wait()
+    bias_ref[...] = bias[...].astype(jnp.float32).reshape(bias_ref.shape)
+    for copy in copies[1:]:
+        copy.wait()
+
+
+def copies_of(src, dst, sem, parts):
+    total = src.shape[0]
+    piece = -(-total // parts // 16) * 16
+    return [
+        pltpu.make_async_copy(src.at[i : min(total, i + piece)], dst.at[i : min(total, i + piece)], sem.at[i // piece])
+        for i in range(0, total, piece)
+    ]
+
+
+def collect_kernel(*refs):
+    *msgs, out_ref = refs
+    held = out_ref.shape[0] // len(msgs)
+    for i, msg in enumerate(msgs):
+        out_ref[i * held : (i + 1) * held, :] = msg[0:held, :]
+
+
+def keys_kernel(blocks, *refs):
+    msgs, (weight, bias, keys, rows) = refs[:blocks], refs[blocks:]
+    prefix = rows.shape[0] // blocks
+    for j, msg in enumerate(msgs):
+        rows[j * prefix : (j + 1) * prefix, :] = msg[msg.shape[0] - prefix :, :]
+    step = 512
+    for i in range(0, keys.shape[1], step):
+        summed = dot(rows[...], weight[:, i : i + step])
+        keys[:, i : i + step] = (summed + bias[:, i : i + step]).astype(jnp.bfloat16)
+
+
+def hidden_kernel(order, prefix, cap_len, *refs):
+    pos_ref, *cap_refs = refs[:5]
+    keys, gain_ref, head_hbm, out_ref, head_ref, caps, query, mixed, bias, scores, weights, sem = refs[5:]
+    head_copies = copies_of(head_hbm, head_ref, sem, sem.shape[0])
+    for copy in head_copies:
+        copy.start()
+    blocks = len(order)
+    width = caps.shape[1]
     model_width = mixed.shape[1]
     row_total = query.shape[0]
-    prefix, held, pair_rows = rows.shape[0] // blocks, caps.shape[0] // (2 * blocks), row_total // blocks
-    cap_len = 4
+    held, pair_rows = caps.shape[0] // (2 * blocks), row_total // blocks
     pieces = -(-model_width // width)
-    span = model_width // parts
-    copies = [
-        pltpu.make_async_copy(
-            weight_hbm.at[:, i * span : (i + 1) * span], weight.at[:, i * span : (i + 1) * span], sem.at[i]
-        )
-        for i in range(parts)
-    ]
-    for copy in copies:
-        copy.start()
-    vocab = head_ref.shape[0]
-    piece = -(-vocab // head_parts // 16) * 16
-    head_copies = [
-        pltpu.make_async_copy(
-            head_hbm.at[i : min(vocab, i + piece)], head_ref.at[i : min(vocab, i + piece)], head_sem.at[i // piece]
-        )
-        for i in range(0, vocab, piece)
-    ]
-
-    for j in range(blocks):
-        rows[j * prefix : (j + 1) * prefix, :] = msgs[j][pieces * cap_len :, :]
-    for j in range(2 * blocks):
-        caps[j * held : (j + 1) * held, :] = msgs[j][0:held, :]
+
+    start = 0
+    for ref in cap_refs:
+        caps[start : start + ref.shape[0], :] = ref[...]
+        start += ref.shape[0]
     rest = model_width - (pieces - 1) * width
     last = (pieces - 2) * cap_len
     row, lane = iota((pair_rows, LANES), 0), iota((pair_rows, LANES), 1)
-    place = 3 + 2 * (row // cap_len)
+    place = 2 + 2 * (row // cap_len)
     factor = jnp.where(lane == place, float(DIGIT), jnp.where(lane == place + 1, 1.0, 0.0))
     found = []
-    for j in range(blocks):
-        digits = msgs[j][last : last + pair_rows, rest : rest + LANES].astype(jnp.float32)
+    for s in range(blocks):
+        digits = caps[s * held + last : s * held + last + pair_rows, rest : rest + LANES].astype(jnp.float32)
         digits = jnp.where(row < cap_len, pltpu.roll(digits, cap_len, 0), digits)
         found.append(jnp.sum(digits * factor, 1, keepdims=True))
-    away = jnp.concatenate(found, 0).astype(jnp.int32) ^ pos_ref[0]
-    first = ((away & 1) * blocks + (away >> 1)) * held + iota((row_total, 1), 0) % cap_len
+    found = jnp.concatenate(found, 0)
+    away = found.astype(jnp.int32) ^ pos_ref[0]
+    block = (away & 1) * blocks
+    for s, distance in enumerate(order):
+        block += jnp.where(away - (away & 1) == distance, s, 0)
+    first = block * held + iota((row_total, 1), 0) % cap_len
     column = iota((row_total, 2 * blocks * held), 1)
     pick = jnp.concatenate(
         [jnp.where(column == first + c * cap_len, 1.0, 0.0).astype(jnp.bfloat16) for c in range(pieces)], 0
@@ -125,57 +154,54 @@
         part = min(width, query.shape[1] - c * width)
         query[:, c * width : c * width + part] = picked[c * row_total : (c + 1) * row_total, 0:part]
 
-    for i, copy in enumerate(copies):
-        copy.wait()
-        if i == parts - 1:
-            for head_copy in head_copies:
-                head_copy.start()
-        cols = slice(i * span, (i + 1) * span)
-        summed = dot(rows[...], weight[:, cols])
-        keys[:, cols] = (summed + bias_ref[:, cols].astype(jnp.float32)).astype(jnp.bfloat16)
-
     heads = TILE // HEAD_DIM
-    group_keys = LANES
-    group_rows = group_keys // prefix * pair_rows
-    groups = row_total // group_rows
+    group_rows = bias.shape[0] // heads
+    image_keys = bias.shape[1] - group_rows
     lane = iota((group_rows, TILE), 1) // HEAD_DIM
-    r, k = iota((heads * group_rows, group_keys), 0) % group_rows, iota((heads * group_rows, group_keys), 1)
-    image_ok = (r // pair_rows) == (k // prefix)
-    r, k = iota((heads * group_rows, group_rows), 0) % group_rows, iota((heads * group_rows, group_rows), 1)
-    own_ok = ((r // cap_len) == (k // cap_len)) & (k <= r)
-
-    def attend_tile(i, square):
-        cols = pl.ds(pl.multiple_of(i * TILE, TILE), TILE)
-        squares = []
-        for g in range(groups):
-            q = query[g * group_rows : (g + 1) * group_rows, cols]
-            key = keys[g * group_keys : (g + 1) * group_keys, cols]
-            zero = jnp.zeros_like(q)
-            every = jnp.concatenate([jnp.where(lane == h, q, zero) for h in range(heads)], 0)
-            image = jnp.where(image_ok, dot_rows(every, key) * score_scale, -1e30)
-            own = jnp.where(own_ok, dot_rows(every, q) * score_scale, -1e30)
-            top = jnp.maximum(jnp.max(image, 1, keepdims=True), jnp.max(own, 1, keepdims=True))
-            image, own = jnp.exp(image - top), jnp.exp(own - top)
-            scale = 1.0 / (jnp.sum(image, 1, keepdims=True) + jnp.sum(own, 1, keepdims=True))
-            out = dot((image * scale).astype(jnp.bfloat16), key) + dot((own * scale).astype(jnp.bfloat16), q)
-            value = q.astype(jnp.float32)
-            for h in range(heads):
-                value += jnp.where(lane == h, out[h * group_rows : (h + 1) * group_rows], 0.0)
-            mixed[g * group_rows : (g + 1) * group_rows, cols] = value
-            squares.append(value * value)
-        return square + jnp.concatenate(squares, 0)
-
-    square = lax.fori_loop(
-        0, model_width // TILE, attend_tile, jnp.zeros((row_total, TILE), jnp.float32), unroll=4
-    )
+    r, k = iota(bias.shape, 0) % group_rows, iota(bias.shape, 1)
+    own = k - image_keys
+    allowed = ((k < image_keys) & (k // prefix == r // pair_rows)) | (
+        (own >= 0) & (own <= r) & (own // cap_len == r // cap_len)
+    )
+    bias[...] = jnp.where(allowed, 0.0, -1e30)
+    tiles = [
+        (g, slice(i * TILE, (i + 1) * TILE))
+        for i in range(model_width // TILE)
+        for g in range(row_total // group_rows)
+    ]
+
+    def keys_of(g, cols):
+        q = query[g * group_rows : (g + 1) * group_rows, cols]
+        return q, jnp.concatenate([keys[g * image_keys : (g + 1) * image_keys, cols], q], 0)
+
+    for n, (g, cols) in enumerate(tiles):
+        q, key = keys_of(g, cols)
+        scaled, zero = q * score_scale, jnp.zeros_like(q)
+        every = jnp.concatenate([jnp.where(lane == h, scaled, zero) for h in range(heads)], 0)
+        scores[n] = dot_rows(every, key)
+    for n in range(len(tiles)):
+        score = scores[n] + bias[...]
+        expo = jnp.exp(score - jnp.max(score, 1, keepdims=True))
+        weights[n] = (expo * (1.0 / jnp.sum(expo, 1, keepdims=True))).astype(jnp.bfloat16)
+    squares = [jnp.zeros((group_rows, TILE), jnp.float32) for _ in range(row_total // group_rows)]
+    for n, (g, cols) in enumerate(tiles):
+        q, key = keys_of(g, cols)
+        out = dot(weights[n], key)
+        value = q.astype(jnp.float32)
+        for h in range(heads):
+            value += jnp.where(lane == h, out[h * group_rows : (h + 1) * group_rows], 0.0)
+        mixed[g * group_rows : (g + 1) * group_rows, cols] = value
+        squares[g] += value * value
+    square = jnp.concatenate(squares, 0)
     scale = lax.rsqrt(jnp.sum(square, 1, keepdims=True) / model_width + eps)
     out_ref[:, 0:model_width] = (mixed[...] * scale * gain_ref[...]).astype(jnp.bfloat16)
-    out_ref[:, model_width:] = query[:, model_width:]
-    for head_copy in head_copies:
-        head_copy.wait()
-
-
-def logits_kernel(pos_ref, mine_ref, other_ref, head_ref, out_ref, states, logits):
+    marks = query[:, model_width:]
+    out_ref[:, model_width:] = jnp.where(iota(marks.shape, 1) == 2, found.astype(jnp.bfloat16), marks)
+    for copy in head_copies:
+        copy.wait()
+
+
+def logits_kernel(order, pos_ref, mine_ref, other_ref, head_ref, length_ref, out_ref, states, logits):
     half = mine_ref.shape[0]
     vocab, model_width = head_ref.shape
     row_total = 2 * half
@@ -193,10 +219,12 @@
     total = jnp.sum(jnp.exp(values - top), 0, keepdims=True)
     hit = iota((vocab, row_total), 0) == ids - pos_ref[0] * vocab
     target = jnp.sum(jnp.where(hit, values, 0.0), 0, keepdims=True)
-    packed = jnp.concatenate([top, total, target, jnp.zeros((LANES - 3, row_total), jnp.float32)], 0).T
+    packed = jnp.concatenate(
+        [top, total, target, length_ref[...], jnp.zeros((LANES - 4, row_total), jnp.float32)], 0
+    ).T
     shards, rows = out_ref.shape[:2]
     for j in range(shards):
-        away = (j % (shards // 2)) * 2 + j // (shards // 2)
+        away = order[j % len(order)] + j // len(order)
         out_ref[pos_ref[0] ^ away] = packed[j * rows : (j + 1) * rows]
 
 
@@ -209,13 +237,15 @@
     top = jnp.max(stats, 0)[:, 0:1]
     total = jnp.zeros((rows, 1), jnp.float32)
     target = jnp.zeros((rows, 1), jnp.float32)
+    length = jnp.zeros((rows, 1), jnp.float32)
+    cand = mine_ref[0:16, model_width:].astype(jnp.float32)[0:rows, 2:3]
     for e in range(shards):
         total += stats[e][:, 1:2] * jnp.exp(stats[e][:, 0:1] - top)
         target += stats[e][:, 2:3]
+        length += jnp.where(cand == e, stats[e][:, 3:4], 0.0)
     loglik = target - (top + jnp.log(total))
-    lengths = mine_ref[0:16, model_width:].astype(jnp.float32)[0:rows, 2:3]
     token = iota((rows, LANES), 0) % cap_len
-    kept = (token == lane) & (token.astype(jnp.float32) < lengths)
+    kept = (token == lane) & (token.astype(jnp.float32) < length)
     spread = jnp.where(kept, loglik, 0.0)
     for k in range(out_ref.shape[1]):
         out_ref[0, k : k + 1, :] = jnp.sum(spread[k * cap_len : (k + 1) * cap_len], 0, keepdims=True)[:, 0:cap_len]
@@ -235,7 +265,9 @@
     row_total = blocks * pair_rows
     vocab = head_weight.shape[1]
     position = lax.axis_index("dp").astype(jnp.int32).reshape(1)
-    parts, head_parts = 8, 8
+    head_parts = 8
+    heads, group = TILE // HEAD_DIM, LANES // prefix
+    score_tiles = model_width // TILE * blocks // group
 
     def swap(a, away):
         return lax.ppermute(a, "dp", [(i, i ^ away) for i in range(shards)])
@@ -243,7 +275,7 @@
     message = pl.pallas_call(
         pack_kernel,
         out_shape=jax.ShapeDtypeStruct((piece_rows + prefix, width), jnp.bfloat16),
-        in_specs=[SMEM] + [HBM] * 4,
+        in_specs=[HBM] * 4,
         out_specs=VMEM,
         scratch_shapes=[
             pltpu.SMEM(candidates.shape, jnp.int32),
@@ -255,51 +287,84 @@
         ],
         compiler_params=pltpu.CompilerParams(vmem_limit_bytes=2 * MIB),
         name="pack",
-    )(caption_lengths, *(in_hbm(a) for a in (candidates, caption_ids, query_rows, caption_states)))
+    )(*(in_hbm(a) for a in (candidates, caption_ids, query_rows, caption_states)))
 
     got = {0: message}
     for away in (12, 4, 2):
         got[away] = swap(message, away)
+    weight, bias, gain, length = pl.pallas_call(
+        bring_kernel,
+        out_shape=(
+            pltpu.VMEM((width, model_width), jnp.bfloat16),
+            pltpu.VMEM((1, model_width), jnp.float32),
+            pltpu.VMEM((1, model_width), jnp.float32),
+            pltpu.VMEM((1, LANES), jnp.float32),
+        ),
+        in_specs=[SMEM] * 2 + [HBM] * 3,
+        out_specs=(VMEM,) * 4,
+        scratch_shapes=[pltpu.VMEM((model_width,), jnp.bfloat16), pltpu.SemaphoreType.DMA((3,))],
+        compiler_params=pltpu.CompilerParams(vmem_limit_bytes=2 * MIB),
+        cost_estimate=pl.CostEstimate(flops=0, bytes_accessed=4 * width * model_width, transcendentals=0),
+        name="bring",
+    )(position, caption_lengths, *(in_hbm(a) for a in (proj_weight, proj_bias, norm_gain.reshape(1, -1))))
+    got[12], got[4], got[2], length = lax.optimization_barrier((got[12], got[4], got[2], length))
     got[8] = swap(got[12], 4)
-    for away in (4, 12, 8):
+    for away in (12, 4, 8):
         got[away + 2] = swap(got[away], 2)
-    mine = [got[2 * j] for j in range(blocks)]
-    other = [swap(a, 1) for a in mine]
+    order = (0, 12, 4, 2, 8, 14, 6, 10)
+    mine = [got[away] for away in order]
+
+    def collect(msgs):
+        return pl.pallas_call(
+            collect_kernel,
+            out_shape=jax.ShapeDtypeStruct((len(msgs) * held, width), jnp.bfloat16),
+            in_specs=[VMEM] * len(msgs),
+            out_specs=VMEM,
+            compiler_params=pltpu.CompilerParams(vmem_limit_bytes=2 * MIB),
+            name="collect",
+        )(*msgs)
+
+    near, far = collect(mine[: blocks // 2]), collect(mine[blocks // 2 :])
+    other_near, other_far = swap(near, 1), swap(far, 1)
+
+    keys = pl.pallas_call(
+        functools.partial(keys_kernel, blocks),
+        out_shape=pltpu.VMEM((blocks * prefix, model_width), jnp.bfloat16),
+        in_specs=[VMEM] * (blocks + 2),
+        out_specs=VMEM,
+        scratch_shapes=[pltpu.VMEM((blocks * prefix, width), jnp.bfloat16)],
+        compiler_params=pltpu.CompilerParams(vmem_limit_bytes=8 * MIB),
+        cost_estimate=pl.CostEstimate(
+            flops=2 * blocks * prefix * width * model_width, bytes_accessed=4 * width * model_width, transcendentals=0
+        ),
+        name="keys",
+    )(*mine, weight, bias)
 
     hidden, head = pl.pallas_call(
-        lambda *refs: hidden_kernel(blocks, parts, head_parts, *refs),
+        functools.partial(hidden_kernel, order, prefix, cap_len),
         out_shape=(
             jax.ShapeDtypeStruct((row_total, model_width + LANES), jnp.bfloat16),
             pltpu.VMEM((vocab, model_width), jnp.bfloat16),
         ),
-        in_specs=[SMEM] + [VMEM] * (2 * blocks) + [HBM, VMEM, VMEM, HBM],
+        in_specs=[SMEM] + [VMEM] * 6 + [HBM],
         out_specs=(VMEM, VMEM),
         scratch_shapes=[
-            pltpu.VMEM((width, model_width), jnp.bfloat16),
-            pltpu.VMEM((blocks * prefix, model_width), jnp.bfloat16),
             pltpu.VMEM((2 * blocks * held, width), jnp.bfloat16),
-            pltpu.VMEM((blocks * prefix, width), jnp.bfloat16),
             pltpu.VMEM((row_total, model_width + LANES), jnp.bfloat16),
             pltpu.VMEM((row_total, model_width), jnp.float32),
-            pltpu.SemaphoreType.DMA((parts,)),
+            pltpu.VMEM((heads * group * pair_rows, group * (prefix + pair_rows)), jnp.float32),
+            pltpu.VMEM((score_tiles, heads * group * pair_rows, group * (prefix + pair_rows)), jnp.float32),
+            pltpu.VMEM((score_tiles, heads * group * pair_rows, group * (prefix + pair_rows)), jnp.bfloat16),
             pltpu.SemaphoreType.DMA((head_parts,)),
         ],
         compiler_params=pltpu.CompilerParams(vmem_limit_bytes=24 * MIB),
         name="hidden",
-    )(
-        position,
-        *mine,
-        *other,
-        in_hbm(proj_weight),
-        proj_bias.reshape(1, -1),
-        norm_gain.reshape(1, -1),
-        in_hbm(head_weight.T),
-    )
+    )(position, near, far, other_near, other_far, keys, gain, in_hbm(head_weight.T))
 
     stats = pl.pallas_call(
-        logits_kernel,
+        functools.partial(logits_kernel, order),
         out_shape=jax.ShapeDtypeStruct((shards, pair_rows, LANES), jnp.float32),
-        in_specs=[SMEM, VMEM, VMEM, VMEM],
+        in_specs=[SMEM, VMEM, VMEM, VMEM, VMEM],
         out_specs=VMEM,
         scratch_shapes=[
             pltpu.VMEM((2 * row_total, model_width), jnp.bfloat16),
@@ -307,7 +372,7 @@
         ],
         compiler_params=pltpu.CompilerParams(vmem_limit_bytes=16 * MIB),
         name="logits",
-    )(position, hidden, swap(hidden, 1), head)
+    )(position, hidden, swap(hidden, 1), head, length)
 
     stats = lax.all_to_all(stats, "dp", 0, 0, tiled=True)
     return pl.pallas_call(

time: 52.1 us -> 47.5 us (0.912)
  blocking collectives: 12.6 us -> 10.4 us
  starting transfers between devices: 13 us -> 10.9 us
  local copies, waits for them, and re-layouts: 1.43 us -> 0 us
  Pallas kernels: 16.7 us -> 17.3 us
    all_to_all x1, blocking collectives: 12.6 us -> 10.4 us  [paired(): stats = lax.all_to_all(stats, 'dp', 0, 0, tiled=True)]
    ppermute x16 -> x10, starting transfers between devices: 13 us -> 10.9 us  [swap(): return lax.ppermute(a, 'dp', [(i, i ^ away) for i in range(shards)])]
    unnamed x2 -> x0, local copies, waits for them, and re-layouts: 0.72 us -> none
    reshape x1 -> x0, local copies, waits for them, and re-layouts: 0.71 us -> none  [paired(): proj_bias.reshape(1, -1)]
    pallas_call x2 -> x6, Pallas kernels: 14.9 us -> 15.6 us  [the longest x1 6.04 us: paired(): pl.pallas_call(functools.partial(hidden_kernel, order, prefix, cap_len),...]
    ppermute x16 -> x10, waiting for transfers between devices: 7.38 us -> 7.88 us  [swap(): return lax.ppermute(a, 'dp', [(i, i ^ away) for i in range(shards)])]
  transfers between devices with their start and end apart: 16 -> 10, of which waited for: 6 -> 5; matrix products, arithmetic and copies ran while one was open for 1% -> 0% of each run, Pallas kernels for 0% -> 10%
where the time goes in v3:
time: 47.5 us; the launch traced here: 47.3 us
  Pallas kernels  17.3 us (36%)
  starting transfers between devices  10.9 us (23%)
  blocking collectives  10.4 us (22%)
  waiting for transfers between devices  7.88 us (17%)
  between operations  0.74 us (2%)
    ppermute x10, starting transfers between devices, swap(): return lax.ppermute(a, 'dp', [(i, i ^ away) for i in range(shards)])  10.9 us
    all_to_all x1, blocking collectives, paired(): stats = lax.all_to_all(stats, 'dp', 0, 0, tiled=True)  10.4 us
    ppermute x10, waiting for transfers between devices, swap(): return lax.ppermute(a, 'dp', [(i, i ^ away) for i in range(shards)])  7.88 us
    pallas_call x1, Pallas kernels, paired(): pl.pallas_call(functools.partial(hidden_kernel, order, prefix, cap_len),...  6.04 us
    pallas_call x1, Pallas kernels, paired(): pl.pallas_call(functools.partial(logits_kernel, order), out_shape=jax.Sha...  4.82 us
    pallas_call x1, Pallas kernels, paired(): pl.pallas_call(bring_kernel, out_shape=(pltpu.VMEM((width, model_width),...  2.85 us
    pallas_call x1, Pallas kernels, paired(): pl.pallas_call(functools.partial(keys_kernel, blocks), out_shape=pltpu.VM...  1.85 us
  transfers between devices with their start and end apart: 10, of which 5 were waited for; matrix products, arithmetic and copies ran while one was open for 0% of the time, Pallas kernels for 10%

profile of v3, /device:TPU:0, one launch (start us, length us, event | category | flops | bytes accessed | tf_op | source)
XLA Modules:
  0.0 47.3 jit_solution(4258959080398420393)
XLA Ops:
  0.0 0.9 %pack.1.refs_0_ = bf16[56,768]{1,0:T(8,128)(2,1)S(1)} custom-call(s32[1,2]{1,0:T(1,128)} %cand_hbm.1, s32[1,4]{1,0:T(1,128)} %ids_hbm.1, bf16[1,32,768]{2,1,0:T(8,128)(2,1)} %rows_hbm.1, bf16[1,4,4096]{2,1,0:T(4,128)(2,1)} %states_hbm.1), custom_call_target="tpu_custom_call" | custom-call | tf_op jit(solution)/shard_map/pack/pallas_call | solution.py:275
  0.9 3.0 %collective-permute-start.2 = (bf16[56,768]{1,0:T(8,128)(2,1)S(1)}, bf16[56,768]{1,0:T(8,128)(2,1)S(1)}, u32[]{:S(2)}, u32[]{:S(2)}) collective-permute-start(bf16[56,768]{1,0:T(8,128)(2,1)S(1)} %pack.1.refs_0_), channel_id=1, source_target_pairs={{0,2},{1,3},{2,0},{3,1},{4,6},{5,7},{6,4},{7,5},{8,10},{9,11},{10,... | collective-permute-start | bytes 258056 | tf_op jit(solution)/shard_map/ppermute | solution.py:273
  3.9 1.6 %collective-permute-start.1 = (bf16[56,768]{1,0:T(8,128)(2,1)S(1)}, bf16[56,768]{1,0:T(8,128)(2,1)S(1)}, u32[]{:S(2)}, u32[]{:S(2)}) collective-permute-start(bf16[56,768]{1,0:T(8,128)(2,1)S(1)} %pack.1.refs_0_), channel_id=1, source_target_pairs={{0,4},{1,5},{2,6},{3,7},{4,0},{5,1},{6,2},{7,3},{8,12},{9,13},{10,... | collective-permute-start | bytes 258056 | tf_op jit(solution)/shard_map/ppermute | solution.py:273
  5.5 2.5 %collective-permute-start = (bf16[56,768]{1,0:T(8,128)(2,1)S(1)}, bf16[56,768]{1,0:T(8,128)(2,1)S(1)}, u32[]{:S(2)}, u32[]{:S(2)}) collective-permute-start(bf16[56,768]{1,0:T(8,128)(2,1)S(1)} %pack.1.refs_0_), channel_id=1, source_target_pairs={{0,12},{1,13},{2,14},{3,15},{4,8},{5,9},{6,10},{7,11},{8,4},{9,5},... | collective-permute-start | bytes 258056 | tf_op jit(solution)/shard_map/ppermute | solution.py:273
  8.6 2.8 %bring.1 = (bf16[768,4096]{1,0:T(8,128)(2,1)S(1)}, f32[1,4096]{1,0:T(1,128)S(1)}, f32[1,4096]{1,0:T(1,128)S(1)}, f32[1,128]{1,0:T(1,128)S(1)}) custom-call(s32[1]{0:T(128)} %bitcast.pos_ref.refs_0_, s32[1]{0:T(128)S(6)} %copy.10.len_ref, bf16[768,4096]{1,0:T(8,128)(2,1)} %weight_hbm.1, bf16[4096]{0:T(1024)(128)(2,1)} %bias_hbm.1, f32[1,4096]{1,0:T(1,128)} %bitcast.4), custom_call_target="tpu_custom_call" | custom-call | bytes 12582912 | tf_op jit(solution)/shard_map/bring/pallas_call | solution.py:295
  11.5 0.0 collective-permute-done.2.refs_3_
  11.5 0.0 collective-permute-done.1.refs_2_
  11.5 0.5 %collective-permute-done.refs_1_ = bf16[56,768]{1,0:T(8,128)(2,1)S(1)} collective-permute-done((bf16[56,768]{1,0:T(8,128)(2,1)S(1)}, bf16[56,768]{1,0:T(8,128)(2,1)S(1)}, u32[]{:S(2)}, u32[]{:S(2)}) %collective-permute-start) | collective-permute-done | bytes 86048 | tf_op jit(solution)/shard_map/ppermute | solution.py:273
  12.0 0.6 %collective-permute-start.3 = (bf16[56,768]{1,0:T(8,128)(2,1)S(1)}, bf16[56,768]{1,0:T(8,128)(2,1)S(1)}, u32[]{:S(2)}, u32[]{:S(2)}) collective-permute-start(bf16[56,768]{1,0:T(8,128)(2,1)S(1)} %collective-permute-done.refs_1_), channel_id=1, source_target_pairs={{0,4},{1,5},{2,6},{3,7},{4,0},{5,1},{6,2},{7,3},{8,12},{9,13},{10,... | collective-permute-start | bytes 258056 | tf_op jit(solution)/shard_map/ppermute | solution.py:273
  12.6 0.5 %collective-permute-start.4 = (bf16[56,768]{1,0:T(8,128)(2,1)S(1)}, bf16[56,768]{1,0:T(8,128)(2,1)S(1)}, u32[]{:S(2)}, u32[]{:S(2)}) collective-permute-start(bf16[56,768]{1,0:T(8,128)(2,1)S(1)} %collective-permute-done.refs_1_), channel_id=1, source_target_pairs={{0,2},{1,3},{2,0},{3,1},{4,6},{5,7},{6,4},{7,5},{8,10},{9,11},{10,... | collective-permute-start | bytes 258056 | tf_op jit(solution)/shard_map/ppermute | solution.py:273
  13.1 1.5 %collective-permute-start.5 = (bf16[56,768]{1,0:T(8,128)(2,1)S(1)}, bf16[56,768]{1,0:T(8,128)(2,1)S(1)}, u32[]{:S(2)}, u32[]{:S(2)}) collective-permute-start(bf16[56,768]{1,0:T(8,128)(2,1)S(1)} %collective-permute-done.1.refs_2_), channel_id=1, source_target_pairs={{0,2},{1,3},{2,0},{3,1},{4,6},{5,7},{6,4},{7,5},{8,10},{9,11},{10,... | collective-permute-start | bytes 258056 | tf_op jit(solution)/shard_map/ppermute | solution.py:273
  14.6 1.9 %collective-permute-done.3.refs_0_.refs_4_ = bf16[56,768]{1,0:T(8,128)(2,1)S(1)} collective-permute-done((bf16[56,768]{1,0:T(8,128)(2,1)S(1)}, bf16[56,768]{1,0:T(8,128)(2,1)S(1)}, u32[]{:S(2)}, u32[]{:S(2)}) %collective-permute-start.3) | collective-permute-done | bytes 86048 | tf_op jit(solution)/shard_map/ppermute | solution.py:273
  16.5 0.5 %collective-permute-start.6 = (bf16[56,768]{1,0:T(8,128)(2,1)S(1)}, bf16[56,768]{1,0:T(8,128)(2,1)S(1)}, u32[]{:S(2)}, u32[]{:S(2)}) collective-permute-start(bf16[56,768]{1,0:T(8,128)(2,1)S(1)} %collective-permute-done.3.refs_0_.refs_4_), channel_id=1, source_target_pairs={{0,2},{1,3},{2,0},{3,1},{4,6},{5,7},{6,4},{7,5},{8,10},{9,11},{10,... | collective-permute-start | bytes 258056 | tf_op jit(solution)/shard_map/ppermute | solution.py:273
  17.0 0.1 collective-permute-start.7
  17.1 1.8 %collective-permute-done.5.refs_2_.refs_6_ = bf16[56,768]{1,0:T(8,128)(2,1)S(1)} collective-permute-done((bf16[56,768]{1,0:T(8,128)(2,1)S(1)}, bf16[56,768]{1,0:T(8,128)(2,1)S(1)}, u32[]{:S(2)}, u32[]{:S(2)}) %collective-permute-start.5) | collective-permute-done | bytes 86048 | tf_op jit(solution)/shard_map/ppermute | solution.py:273
  18.9 0.0 collective-permute-done.4.refs_1_.refs_5_
  18.9 2.1 %collective-permute-done.6.refs_3_.refs_7_ = bf16[56,768]{1,0:T(8,128)(2,1)S(1)} collective-permute-done((bf16[56,768]{1,0:T(8,128)(2,1)S(1)}, bf16[56,768]{1,0:T(8,128)(2,1)S(1)}, u32[]{:S(2)}, u32[]{:S(2)}) %collective-permute-start.6) | collective-permute-done | bytes 86048 | tf_op jit(solution)/shard_map/ppermute | solution.py:273
  21.0 0.1 collective-permute-start.8
  21.1 1.9 %keys.1.refs_5_ = bf16[256,4096]{1,0:T(8,128)(2,1)S(1)} custom-call(bf16[56,768]{1,0:T(8,128)(2,1)S(1)} %pack.1.refs_0_, bf16[56,768]{1,0:T(8,128)(2,1)S(1)} %collective-permute-done.refs_1_, bf16[56,768]{1,0:T(8,128)(2,1)S(1)} %collective-permute-done.1.refs_2_, bf16[56,768]{1,0:T(8,128)(2,1)S(1)} %collective-permute-done.2.refs_3_, ...), custom_call_target="tpu_custom_call" | custom-call | flops 1610612736 | bytes 12582912 | tf_op jit(solution)/shard_map/keys/pallas_call | solution.py:330
  23.0 0.0 collective-permute-done.7.refs_3_
  23.0 0.0 collective-permute-done.8.refs_4_
  23.0 6.0 %hidden.1 = (bf16[64,4224]{1,0:T(8,128)(2,1)S(1)}, bf16[2008,4096]{1,0:T(8,128)(2,1)S(1)}) custom-call(s32[1]{0:T(128)} %bitcast.pos_ref.refs_0_, bf16[128,768]{1,0:T(8,128)(2,1)S(1)} %collect.2.refs_1_, bf16[128,768]{1,0:T(8,128)(2,1)S(1)} %collect.3.refs_2_, bf16[128,768]{1,0:T(8,128)(2,1)S(1)} %collective-permute-done.7.refs_3_, ...), custom_call_target="tpu_custom_call" | custom-call | tf_op jit(solution)/shard_map/hidden/pallas_call | solution.py:343
  29.0 0.6 %collective-permute-start.9 = (bf16[64,4224]{1,0:T(8,128)(2,1)S(1)}, bf16[64,4224]{1,0:T(8,128)(2,1)S(1)}, u32[]{:S(2)}, u32[]{:S(2)}) collective-permute-start(bf16[64,4224]{1,0:T(8,128)(2,1)S(1)} %get-tuple-element.22.mine_ref), channel_id=1, source_target_pairs={{0,1},{1,0},{2,3},{3,2},{4,5},{5,4},{6,7},{7,6},{8,9},{9,8},{10,11... | collective-permute-start | bytes 1622024 | tf_op jit(solution)/shard_map/ppermute | solution.py:273
  29.6 1.6 %collective-permute-done.9.other_ref = bf16[64,4224]{1,0:T(8,128)(2,1)S(1)} collective-permute-done((bf16[64,4224]{1,0:T(8,128)(2,1)S(1)}, bf16[64,4224]{1,0:T(8,128)(2,1)S(1)}, u32[]{:S(2)}, u32[]{:S(2)}) %collective-permute-start.9) | collective-permute-done | bytes 540704 | tf_op jit(solution)/shard_map/ppermute | solution.py:273
  31.1 4.8 %logits.1 = f32[16,8,128]{2,1,0:T(8,128)S(1)} custom-call(s32[1]{0:T(128)} %bitcast.pos_ref.refs_0_, bf16[64,4224]{1,0:T(8,128)(2,1)S(1)} %get-tuple-element.22.mine_ref, bf16[64,4224]{1,0:T(8,128)(2,1)S(1)} %collective-permute-done.9.other_ref, bf16[2008,4096]{1,0:T(8,128)(2,1)S(1)} %get-tuple-element.23.head_ref, f32[1,128]{1,0:T(1,128)S(1)} %get-tuple-element.24.length_ref), custom_call_target="tpu_custom_call" | custom-call | tf_op jit(solution)/shard_map/logits/pallas_call | solution.py:364
  36.0 10.4 %all_to_all.5.stats_ref = f32[16,8,128]{2,1,0:T(8,128)S(1)} all-to-all(f32[16,8,128]{2,1,0:T(8,128)S(1)} %logits.1), channel_id=1, replica_groups=mesh['groups'=2,'dp'=16] {'dp'}, dimensions={0} | all-to-all | bytes 131072 | tf_op jit(solution)/shard_map/all_to_all | solution.py:377
  46.4 0.9 %finish.1 = f32[1,2,4]{2,1,0:T(2,128)} custom-call(f32[16,8,128]{2,1,0:T(8,128)S(1)} %all_to_all.5.stats_ref, bf16[64,4224]{1,0:T(8,128)(2,1)S(1)} %get-tuple-element.22.mine_ref), custom_call_target="tpu_custom_call" | custom-call | tf_op jit(solution)/shard_map/finish/pallas_call | solution.py:378
  (2 shorter events, 0.0 us)
Async XLA Ops:
  0.9 10.6 %collective-permute-start.2 = (bf16[56,768]{1,0:T(8,128)(2,1)S(1)}, bf16[56,768]{1,0:T(8,128)(2,1)S(1)}, u32[]{:S(2)}, u32[]{:S(2)}) collective-permute-start(bf16[56,768]{1,0:T(8,128)(2,1)S(1)} %pack.1.refs_0_), channel_id=1, source_target_pairs={{0,2},{1,3},{2,0},{3,1},{4,6},{5,7},{6,4},{7,5},{8,10},{9,11},{10,... | collective-permute-start | bytes 258056 | tf_op jit(solution)/shard_map/ppermute | solution.py:273
  3.9 7.6 %collective-permute-start.1 = (bf16[56,768]{1,0:T(8,128)(2,1)S(1)}, bf16[56,768]{1,0:T(8,128)(2,1)S(1)}, u32[]{:S(2)}, u32[]{:S(2)}) collective-permute-start(bf16[56,768]{1,0:T(8,128)(2,1)S(1)} %pack.1.refs_0_), channel_id=1, source_target_pairs={{0,4},{1,5},{2,6},{3,7},{4,0},{5,1},{6,2},{7,3},{8,12},{9,13},{10,... | collective-permute-start | bytes 258056 | tf_op jit(solution)/shard_map/ppermute | solution.py:273
  5.5 6.5 %collective-permute-start = (bf16[56,768]{1,0:T(8,128)(2,1)S(1)}, bf16[56,768]{1,0:T(8,128)(2,1)S(1)}, u32[]{:S(2)}, u32[]{:S(2)}) collective-permute-start(bf16[56,768]{1,0:T(8,128)(2,1)S(1)} %pack.1.refs_0_), channel_id=1, source_target_pairs={{0,12},{1,13},{2,14},{3,15},{4,8},{5,9},{6,10},{7,11},{8,4},{9,5},... | collective-permute-start | bytes 258056 | tf_op jit(solution)/shard_map/ppermute | solution.py:273
  12.0 4.5 %collective-permute-start.3 = (bf16[56,768]{1,0:T(8,128)(2,1)S(1)}, bf16[56,768]{1,0:T(8,128)(2,1)S(1)}, u32[]{:S(2)}, u32[]{:S(2)}) collective-permute-start(bf16[56,768]{1,0:T(8,128)(2,1)S(1)} %collective-permute-done.refs_1_), channel_id=1, source_target_pairs={{0,4},{1,5},{2,6},{3,7},{4,0},{5,1},{6,2},{7,3},{8,12},{9,13},{10,... | collective-permute-start | bytes 258056 | tf_op jit(solution)/shard_map/ppermute | solution.py:273
  12.6 6.3 %collective-permute-start.4 = (bf16[56,768]{1,0:T(8,128)(2,1)S(1)}, bf16[56,768]{1,0:T(8,128)(2,1)S(1)}, u32[]{:S(2)}, u32[]{:S(2)}) collective-permute-start(bf16[56,768]{1,0:T(8,128)(2,1)S(1)} %collective-permute-done.refs_1_), channel_id=1, source_target_pairs={{0,2},{1,3},{2,0},{3,1},{4,6},{5,7},{6,4},{7,5},{8,10},{9,11},{10,... | collective-permute-start | bytes 258056 | tf_op jit(solution)/shard_map/ppermute | solution.py:273
  13.1 5.8 %collective-permute-start.5 = (bf16[56,768]{1,0:T(8,128)(2,1)S(1)}, bf16[56,768]{1,0:T(8,128)(2,1)S(1)}, u32[]{:S(2)}, u32[]{:S(2)}) collective-permute-start(bf16[56,768]{1,0:T(8,128)(2,1)S(1)} %collective-permute-done.1.refs_2_), channel_id=1, source_target_pairs={{0,2},{1,3},{2,0},{3,1},{4,6},{5,7},{6,4},{7,5},{8,10},{9,11},{10,... | collective-permute-start | bytes 258056 | tf_op jit(solution)/shard_map/ppermute | solution.py:273
  16.5 4.5 %collective-permute-start.6 = (bf16[56,768]{1,0:T(8,128)(2,1)S(1)}, bf16[56,768]{1,0:T(8,128)(2,1)S(1)}, u32[]{:S(2)}, u32[]{:S(2)}) collective-permute-start(bf16[56,768]{1,0:T(8,128)(2,1)S(1)} %collective-permute-done.3.refs_0_.refs_4_), channel_id=1, source_target_pairs={{0,2},{1,3},{2,0},{3,1},{4,6},{5,7},{6,4},{7,5},{8,10},{9,11},{10,... | collective-permute-start | bytes 258056 | tf_op jit(solution)/shard_map/ppermute | solution.py:273
  17.0 5.9 %collective-permute-start.7 = (bf16[128,768]{1,0:T(8,128)(2,1)S(1)}, bf16[128,768]{1,0:T(8,128)(2,1)S(1)}, u32[]{:S(2)}, u32[]{:S(2)}) collective-permute-start(bf16[128,768]{1,0:T(8,128)(2,1)S(1)} %collect.2.refs_1_), channel_id=1, source_target_pairs={{0,1},{1,0},{2,3},{3,2},{4,5},{5,4},{6,7},{7,6},{8,9},{9,8},{10,11... | collective-permute-start | bytes 589832 | tf_op jit(solution)/shard_map/ppermute | solution.py:273
  21.0 2.0 %collective-permute-start.8 = (bf16[128,768]{1,0:T(8,128)(2,1)S(1)}, bf16[128,768]{1,0:T(8,128)(2,1)S(1)}, u32[]{:S(2)}, u32[]{:S(2)}) collective-permute-start(bf16[128,768]{1,0:T(8,128)(2,1)S(1)} %collect.3.refs_2_), channel_id=1, source_target_pairs={{0,1},{1,0},{2,3},{3,2},{4,5},{5,4},{6,7},{7,6},{8,9},{9,8},{10,11... | collective-permute-start | bytes 589832 | tf_op jit(solution)/shard_map/ppermute | solution.py:273
  29.0 2.1 %collective-permute-start.9 = (bf16[64,4224]{1,0:T(8,128)(2,1)S(1)}, bf16[64,4224]{1,0:T(8,128)(2,1)S(1)}, u32[]{:S(2)}, u32[]{:S(2)}) collective-permute-start(bf16[64,4224]{1,0:T(8,128)(2,1)S(1)} %get-tuple-element.22.mine_ref), channel_id=1, source_target_pairs={{0,1},{1,0},{2,3},{3,2},{4,5},{5,4},{6,7},{7,6},{8,9},{9,8},{10,11... | collective-permute-start | bytes 1622024 | tf_op jit(solution)/shard_map/ppermute | solution.py:273

commit v4 on v3

--- a/solution.py
+++ b/solution.py
@@ -20,6 +20,7 @@
 VMEM = pl.BlockSpec(memory_space=pltpu.VMEM)
 SMEM = pl.BlockSpec(memory_space=pltpu.SMEM)
 HBM = pl.BlockSpec(memory_space=pltpu.HBM)
+ANY = pl.BlockSpec(memory_space=pl.ANY)
 ROWS_BY_ROWS = (((1,), (1,)), ((), ()))
 
 
@@ -85,18 +86,30 @@
         copy.wait()
 
 
-def copies_of(src, dst, sem, parts):
-    total = src.shape[0]
+def cuts(total, parts):
     piece = -(-total // parts // 16) * 16
+    return [(i, min(total, i + piece)) for i in range(0, total, piece)]
+
+
+def copies_of(src, first, dst, sem):
     return [
-        pltpu.make_async_copy(src.at[i : min(total, i + piece)], dst.at[i : min(total, i + piece)], sem.at[i // piece])
-        for i in range(0, total, piece)
+        pltpu.make_async_copy(src.at[first + i : first + j], dst.at[i:j], sem.at[n])
+        for n, (i, j) in enumerate(cuts(dst.shape[0], sem.shape[0]))
     ]
 
 
-def collect_kernel(*refs):
-    *msgs, out_ref = refs
-    held = out_ref.shape[0] // len(msgs)
+def bring_head_kernel(after_ref, head_hbm, head_ref, done_ref, sem):
+    copies = copies_of(head_hbm, 0, head_ref, sem)
+    for copy in copies:
+        copy.start()
+    done_ref[...] = jnp.zeros_like(done_ref)
+    for copy in copies:
+        copy.wait()
+
+
+def collect_kernel(count, *refs):
+    msgs, out_ref = refs[:count], refs[-1]
+    held = out_ref.shape[0] // count
     for i, msg in enumerate(msgs):
         out_ref[i * held : (i + 1) * held, :] = msg[0:held, :]
 
@@ -115,7 +128,7 @@
 def hidden_kernel(order, prefix, cap_len, *refs):
     pos_ref, *cap_refs = refs[:5]
     keys, gain_ref, head_hbm, out_ref, head_ref, caps, query, mixed, bias, scores, weights, sem = refs[5:]
-    head_copies = copies_of(head_hbm, head_ref, sem, sem.shape[0])
+    head_copies = copies_of(head_hbm, head_hbm.shape[0] - head_ref.shape[0], head_ref, sem)
     for copy in head_copies:
         copy.start()
     blocks = len(order)
@@ -201,26 +214,32 @@
         copy.wait()
 
 
-def logits_kernel(order, pos_ref, mine_ref, other_ref, head_ref, length_ref, out_ref, states, logits):
+def logits_kernel(order, pos_ref, mine_ref, other_ref, first_ref, last_ref, length_ref, out_ref, states):
     half = mine_ref.shape[0]
-    vocab, model_width = head_ref.shape
+    model_width = states.shape[1]
     row_total = 2 * half
     states[0:half, :] = mine_ref[:, 0:model_width]
     states[half:, :] = other_ref[:, 0:model_width]
-    for start in range(0, vocab, TILE):
-        stop = min(vocab, start + TILE)
-        logits[start:stop, :] = dot_rows(head_ref[start:stop, :], states[...])
     digits = jnp.concatenate(
         [ref[:, model_width:].astype(jnp.float32) for ref in (mine_ref, other_ref)], 0
     ).T
-    ids = (digits[0:1] * DIGIT + digits[1:2]).astype(jnp.int32)
-    values = logits[...]
-    top = jnp.max(values, 0, keepdims=True)
-    total = jnp.sum(jnp.exp(values - top), 0, keepdims=True)
-    hit = iota((vocab, row_total), 0) == ids - pos_ref[0] * vocab
-    target = jnp.sum(jnp.where(hit, values, 0.0), 0, keepdims=True)
+    vocab = first_ref.shape[0] + last_ref.shape[0]
+    ids = (digits[0:1] * DIGIT + digits[1:2]).astype(jnp.int32) - pos_ref[0] * vocab
+    tops, totals, targets = [], [], []
+    before = 0
+    for ref in (first_ref, last_ref):
+        for i, j in cuts(ref.shape[0], -(-ref.shape[0] // TILE)):
+            values = dot_rows(ref[i:j, :], states[...])
+            top = jnp.max(values, 0, keepdims=True)
+            tops.append(top)
+            totals.append(jnp.sum(jnp.exp(values - top), 0, keepdims=True))
+            hit = iota(values.shape, 0) == ids - (before + i)
+            targets.append(jnp.sum(jnp.where(hit, values, 0.0), 0, keepdims=True))
+        before += ref.shape[0]
+    top = functools.reduce(jnp.maximum, tops)
+    total = sum(t * jnp.exp(m - top) for t, m in zip(totals, tops))
     packed = jnp.concatenate(
-        [top, total, target, length_ref[...], jnp.zeros((LANES - 4, row_total), jnp.float32)], 0
+        [top, total, sum(targets), length_ref[...], jnp.zeros((LANES - 4, row_total), jnp.float32)], 0
     ).T
     shards, rows = out_ref.shape[:2]
     for j in range(shards):
@@ -265,7 +284,7 @@
     row_total = blocks * pair_rows
     vocab = head_weight.shape[1]
     position = lax.axis_index("dp").astype(jnp.int32).reshape(1)
-    head_parts = 8
+    ahead = vocab * 3 // 8 // TILE * TILE
     heads, group = TILE // HEAD_DIM, LANES // prefix
     score_tiles = model_width // TILE * blocks // group
 
@@ -307,24 +326,38 @@
         cost_estimate=pl.CostEstimate(flops=0, bytes_accessed=4 * width * model_width, transcendentals=0),
         name="bring",
     )(position, caption_lengths, *(in_hbm(a) for a in (proj_weight, proj_bias, norm_gain.reshape(1, -1))))
-    got[12], got[4], got[2], length = lax.optimization_barrier((got[12], got[4], got[2], length))
+    got[12], length = lax.optimization_barrier((got[12], length))
     got[8] = swap(got[12], 4)
     for away in (12, 4, 8):
         got[away + 2] = swap(got[away], 2)
+    head_weight = in_hbm(head_weight.T)
+    head_first, done = pl.pallas_call(
+        bring_head_kernel,
+        out_shape=(
+            pltpu.VMEM((ahead, model_width), jnp.bfloat16),
+            pltpu.VMEM((8, LANES), jnp.float32),
+        ),
+        in_specs=[ANY, HBM],
+        out_specs=(VMEM, VMEM),
+        scratch_shapes=[pltpu.SemaphoreType.DMA((4,))],
+        compiler_params=pltpu.CompilerParams(vmem_limit_bytes=2 * MIB),
+        cost_estimate=pl.CostEstimate(flops=0, bytes_accessed=4 * ahead * model_width, transcendentals=0),
+        name="bring_head",
+    )(got[8], head_weight)
     order = (0, 12, 4, 2, 8, 14, 6, 10)
     mine = [got[away] for away in order]
 
-    def collect(msgs):
+    def collect(msgs, *after):
         return pl.pallas_call(
-            collect_kernel,
+            functools.partial(collect_kernel, len(msgs)),
             out_shape=jax.ShapeDtypeStruct((len(msgs) * held, width), jnp.bfloat16),
-            in_specs=[VMEM] * len(msgs),
+            in_specs=[VMEM] * len(msgs) + [ANY] * len(after),
             out_specs=VMEM,
             compiler_params=pltpu.CompilerParams(vmem_limit_bytes=2 * MIB),
             name="collect",
-        )(*msgs)
-
-    near, far = collect(mine[: blocks // 2]), collect(mine[blocks // 2 :])
+        )(*msgs, *after)
+
+    near, far = collect(mine[: blocks // 2]), collect(mine[blocks // 2 :], done)
     other_near, other_far = swap(near, 1), swap(far, 1)
 
     keys = pl.pallas_call(
@@ -340,11 +373,11 @@
         name="keys",
     )(*mine, weight, bias)
 
-    hidden, head = pl.pallas_call(
+    hidden, head_last = pl.pallas_call(
         functools.partial(hidden_kernel, order, prefix, cap_len),
         out_shape=(
             jax.ShapeDtypeStruct((row_total, model_width + LANES), jnp.bfloat16),
-            pltpu.VMEM((vocab, model_width), jnp.bfloat16),
+            pltpu.VMEM((vocab - ahead, model_width), jnp.bfloat16),
         ),
         in_specs=[SMEM] + [VMEM] * 6 + [HBM],
         out_specs=(VMEM, VMEM),
@@ -355,24 +388,21 @@
             pltpu.VMEM((heads * group * pair_rows, group * (prefix + pair_rows)), jnp.float32),
             pltpu.VMEM((score_tiles, heads * group * pair_rows, group * (prefix + pair_rows)), jnp.float32),
             pltpu.VMEM((score_tiles, heads * group * pair_rows, group * (prefix + pair_rows)), jnp.bfloat16),
-            pltpu.SemaphoreType.DMA((head_parts,)),
+            pltpu.SemaphoreType.DMA((8,)),
         ],
         compiler_params=pltpu.CompilerParams(vmem_limit_bytes=24 * MIB),
         name="hidden",
-    )(position, near, far, other_near, other_far, keys, gain, in_hbm(head_weight.T))
+    )(position, near, far, other_near, other_far, keys, gain, head_weight)
 
     stats = pl.pallas_call(
         functools.partial(logits_kernel, order),
         out_shape=jax.ShapeDtypeStruct((shards, pair_rows, LANES), jnp.float32),
-        in_specs=[SMEM, VMEM, VMEM, VMEM, VMEM],
+        in_specs=[SMEM] + [VMEM] * 5,
         out_specs=VMEM,
-        scratch_shapes=[
-            pltpu.VMEM((2 * row_total, model_width), jnp.bfloat16),
-            pltpu.VMEM((vocab, 2 * row_total), jnp.float32),
-        ],
+        scratch_shapes=[pltpu.VMEM((2 * row_total, model_width), jnp.bfloat16)],
         compiler_params=pltpu.CompilerParams(vmem_limit_bytes=16 * MIB),
         name="logits",
-    )(position, hidden, swap(hidden, 1), head, length)
+    )(position, hidden, swap(hidden, 1), head_first, head_last, length)
 
     stats = lax.all_to_all(stats, "dp", 0, 0, tiled=True)
     return pl.pallas_call(

time: 47.5 us -> 45.6 us (0.960)
  waiting for transfers between devices: 7.88 us -> 4.46 us
  starting transfers between devices: 10.9 us -> 12 us
  Pallas kernels: 17.3 us -> 18 us
    ppermute x10, waiting for transfers between devices: 7.88 us -> 4.46 us  [swap(): return lax.ppermute(a, 'dp', [(i, i ^ away) for i in range(shards)])]
    pallas_call x2 -> x3, Pallas kernels: 0.03 us -> 2.24 us  [the longest x1 2.21 us: paired(): pl.pallas_call(bring_head_kernel, out_shape=(pltpu.VMEM((ahead, model_wid...]
    pallas_call x1, Pallas kernels: 6.04 us -> 4.7 us  [paired(): pl.pallas_call(functools.partial(hidden_kernel, order, prefix, cap_len),...]
    ppermute x10, starting transfers between devices: 10.9 us -> 12 us  [swap(): return lax.ppermute(a, 'dp', [(i, i ^ away) for i in range(shards)])]
  transfers between devices with their start and end apart: 10 -> 10, of which waited for: 5 -> 4; matrix products, arithmetic and copies ran while one was open for 0% -> 0% of each run, Pallas kernels for 10% -> 15%
where the time goes in v4:
time: 45.6 us; the launch traced here: 45.3 us
  Pallas kernels  18 us (39%)
  starting transfers between devices  12 us (26%)
  blocking collectives  10.1 us (22%)
  waiting for transfers between devices  4.46 us (10%)
  between operations  0.75 us (2%)
    ppermute x10, starting transfers between devices, swap(): return lax.ppermute(a, 'dp', [(i, i ^ away) for i in range(shards)])  12 us
    all_to_all x1, blocking collectives, paired(): stats = lax.all_to_all(stats, 'dp', 0, 0, tiled=True)  10.1 us
    pallas_call x1, Pallas kernels, paired(): pl.pallas_call(functools.partial(hidden_kernel, order, prefix, cap_len),...  4.7 us
    pallas_call x1, Pallas kernels, paired(): pl.pallas_call(functools.partial(logits_kernel, order), out_shape=jax.Sha...  4.61 us
    ppermute x10, waiting for transfers between devices, swap(): return lax.ppermute(a, 'dp', [(i, i ^ away) for i in range(shards)])  4.46 us
    pallas_call x1, Pallas kernels, paired(): pl.pallas_call(bring_kernel, out_shape=(pltpu.VMEM((width, model_width),...  2.85 us
    pallas_call x1, Pallas kernels, paired(): pl.pallas_call(bring_head_kernel, out_shape=(pltpu.VMEM((ahead, model_wid...  2.21 us
    pallas_call x1, Pallas kernels, paired(): pl.pallas_call(functools.partial(keys_kernel, blocks), out_shape=pltpu.VM...  1.85 us
  transfers between devices with their start and end apart: 10, of which 4 were waited for; matrix products, arithmetic and copies ran while one was open for 0% of the time, Pallas kernels for 15%

profile of v4, /device:TPU:0, one launch (start us, length us, event | category | flops | bytes accessed | tf_op | source)
XLA Modules:
  0.0 45.3 jit_solution(5175320640436787668)
XLA Ops:
  0.0 0.9 %pack.1.refs_0_ = bf16[56,768]{1,0:T(8,128)(2,1)S(1)} custom-call(s32[1,2]{1,0:T(1,128)} %cand_hbm.1, s32[1,4]{1,0:T(1,128)} %ids_hbm.1, bf16[1,32,768]{2,1,0:T(8,128)(2,1)} %rows_hbm.1, bf16[1,4,4096]{2,1,0:T(4,128)(2,1)} %states_hbm.1), custom_call_target="tpu_custom_call" | custom-call | tf_op jit(solution)/shard_map/pack/pallas_call | solution.py:294
  0.9 5.1 %collective-permute-start = (bf16[56,768]{1,0:T(8,128)(2,1)S(1)}, bf16[56,768]{1,0:T(8,128)(2,1)S(1)}, u32[]{:S(2)}, u32[]{:S(2)}) collective-permute-start(bf16[56,768]{1,0:T(8,128)(2,1)S(1)} %pack.1.refs_0_), channel_id=1, source_target_pairs={{0,12},{1,13},{2,14},{3,15},{4,8},{5,9},{6,10},{7,11},{8,4},{9,5},... | collective-permute-start | bytes 258056 | tf_op jit(solution)/shard_map/ppermute | solution.py:292
  6.0 0.0 collective-permute-start.1
  6.7 2.8 %bring.1 = (bf16[768,4096]{1,0:T(8,128)(2,1)S(1)}, f32[1,4096]{1,0:T(1,128)S(1)}, f32[1,4096]{1,0:T(1,128)S(1)}, f32[1,128]{1,0:T(1,128)S(1)}) custom-call(s32[1]{0:T(128)} %bitcast.pos_ref.refs_0_, s32[1]{0:T(128)S(6)} %copy.10.len_ref, bf16[768,4096]{1,0:T(8,128)(2,1)} %weight_hbm.1, bf16[4096]{0:T(1024)(128)(2,1)} %bias_hbm.1, f32[1,4096]{1,0:T(1,128)} %bitcast.5), custom_call_target="tpu_custom_call" | custom-call | bytes 12582912 | tf_op jit(solution)/shard_map/bring/pallas_call | solution.py:314
  9.5 0.0 collective-permute-done.refs_1_
  9.5 2.1 %collective-permute-start.3 = (bf16[56,768]{1,0:T(8,128)(2,1)S(1)}, bf16[56,768]{1,0:T(8,128)(2,1)S(1)}, u32[]{:S(2)}, u32[]{:S(2)}) collective-permute-start(bf16[56,768]{1,0:T(8,128)(2,1)S(1)} %collective-permute-done.refs_1_), channel_id=1, source_target_pairs={{0,4},{1,5},{2,6},{3,7},{4,0},{5,1},{6,2},{7,3},{8,12},{9,13},{10,... | collective-permute-start | bytes 258056 | tf_op jit(solution)/shard_map/ppermute | solution.py:292
  11.6 1.5 %collective-permute-start.2 = (bf16[56,768]{1,0:T(8,128)(2,1)S(1)}, bf16[56,768]{1,0:T(8,128)(2,1)S(1)}, u32[]{:S(2)}, u32[]{:S(2)}) collective-permute-start(bf16[56,768]{1,0:T(8,128)(2,1)S(1)} %pack.1.refs_0_), channel_id=1, source_target_pairs={{0,2},{1,3},{2,0},{3,1},{4,6},{5,7},{6,4},{7,5},{8,10},{9,11},{10,... | collective-permute-start | bytes 258056 | tf_op jit(solution)/shard_map/ppermute | solution.py:292
  13.1 0.5 %collective-permute-start.4 = (bf16[56,768]{1,0:T(8,128)(2,1)S(1)}, bf16[56,768]{1,0:T(8,128)(2,1)S(1)}, u32[]{:S(2)}, u32[]{:S(2)}) collective-permute-start(bf16[56,768]{1,0:T(8,128)(2,1)S(1)} %collective-permute-done.refs_1_), channel_id=1, source_target_pairs={{0,2},{1,3},{2,0},{3,1},{4,6},{5,7},{6,4},{7,5},{8,10},{9,11},{10,... | collective-permute-start | bytes 258056 | tf_op jit(solution)/shard_map/ppermute | solution.py:292
  13.7 0.0 collective-permute-done.1.refs_2_
  13.7 1.5 %collective-permute-start.5 = (bf16[56,768]{1,0:T(8,128)(2,1)S(1)}, bf16[56,768]{1,0:T(8,128)(2,1)S(1)}, u32[]{:S(2)}, u32[]{:S(2)}) collective-permute-start(bf16[56,768]{1,0:T(8,128)(2,1)S(1)} %collective-permute-done.1.refs_2_), channel_id=1, source_target_pairs={{0,2},{1,3},{2,0},{3,1},{4,6},{5,7},{6,4},{7,5},{8,10},{9,11},{10,... | collective-permute-start | bytes 258056 | tf_op jit(solution)/shard_map/ppermute | solution.py:292
  15.2 0.0 collective-permute-done.3.after_ref.refs_0_.refs_4_
  15.2 0.5 %collective-permute-start.6 = (bf16[56,768]{1,0:T(8,128)(2,1)S(1)}, bf16[56,768]{1,0:T(8,128)(2,1)S(1)}, u32[]{:S(2)}, u32[]{:S(2)}) collective-permute-start(bf16[56,768]{1,0:T(8,128)(2,1)S(1)} %collective-permute-done.3.after_ref.refs_0_.refs_4_), channel_id=1, source_target_pairs={{0,2},{1,3},{2,0},{3,1},{4,6},{5,7},{6,4},{7,5},{8,10},{9,11},{10,... | collective-permute-start | bytes 258056 | tf_op jit(solution)/shard_map/ppermute | solution.py:292
  15.7 1.3 %collective-permute-done.2.refs_3_ = bf16[56,768]{1,0:T(8,128)(2,1)S(1)} collective-permute-done((bf16[56,768]{1,0:T(8,128)(2,1)S(1)}, bf16[56,768]{1,0:T(8,128)(2,1)S(1)}, u32[]{:S(2)}, u32[]{:S(2)}) %collective-permute-start.2) | collective-permute-done | bytes 86048 | tf_op jit(solution)/shard_map/ppermute | solution.py:292
  17.0 0.1 collective-permute-start.7
  17.1 2.2 %bring_head.1 = (bf16[512,4096]{1,0:T(8,128)(2,1)S(1)}, f32[8,128]{1,0:T(8,128)S(1)}) custom-call(bf16[56,768]{1,0:T(8,128)(2,1)S(1)} %collective-permute-done.3.after_ref.refs_0_.refs_4_, bf16[2008,4096]{1,0:T(8,128)(2,1)} %bitcast.3), custom_call_target="tpu_custom_call" | custom-call | bytes 8388608 | tf_op jit(solution)/shard_map/bring_head/pallas_call | solution.py:334
  19.3 0.7 %collective-permute-done.5.refs_2_.refs_6_ = bf16[56,768]{1,0:T(8,128)(2,1)S(1)} collective-permute-done((bf16[56,768]{1,0:T(8,128)(2,1)S(1)}, bf16[56,768]{1,0:T(8,128)(2,1)S(1)}, u32[]{:S(2)}, u32[]{:S(2)}) %collective-permute-start.5) | collective-permute-done | bytes 86048 | tf_op jit(solution)/shard_map/ppermute | solution.py:292
  20.0 0.0 collective-permute-done.4.refs_1_.refs_5_
  20.0 0.9 %collective-permute-done.6.refs_3_.refs_7_ = bf16[56,768]{1,0:T(8,128)(2,1)S(1)} collective-permute-done((bf16[56,768]{1,0:T(8,128)(2,1)S(1)}, bf16[56,768]{1,0:T(8,128)(2,1)S(1)}, u32[]{:S(2)}, u32[]{:S(2)}) %collective-permute-start.6) | collective-permute-done | bytes 86048 | tf_op jit(solution)/shard_map/ppermute | solution.py:292
  20.9 0.1 collective-permute-start.8
  21.0 1.9 %keys.1.refs_5_ = bf16[256,4096]{1,0:T(8,128)(2,1)S(1)} custom-call(bf16[56,768]{1,0:T(8,128)(2,1)S(1)} %pack.1.refs_0_, bf16[56,768]{1,0:T(8,128)(2,1)S(1)} %collective-permute-done.refs_1_, bf16[56,768]{1,0:T(8,128)(2,1)S(1)} %collective-permute-done.1.refs_2_, bf16[56,768]{1,0:T(8,128)(2,1)S(1)} %collective-permute-done.2.refs_3_, ...), custom_call_target="tpu_custom_call" | custom-call | flops 1610612736 | bytes 12582912 | tf_op jit(solution)/shard_map/keys/pallas_call | solution.py:363
  22.8 0.0 collective-permute-done.7.refs_3_
  22.9 0.0 collective-permute-done.8.refs_4_
  22.9 4.7 %hidden.1 = (bf16[64,4224]{1,0:T(8,128)(2,1)S(1)}, bf16[1496,4096]{1,0:T(8,128)(2,1)S(1)}) custom-call(s32[1]{0:T(128)} %bitcast.pos_ref.refs_0_, bf16[128,768]{1,0:T(8,128)(2,1)S(1)} %collect.2.refs_1_, bf16[128,768]{1,0:T(8,128)(2,1)S(1)} %collect.3.refs_2_, bf16[128,768]{1,0:T(8,128)(2,1)S(1)} %collective-permute-done.7.refs_3_, ...), custom_call_target="tpu_custom_call" | custom-call | tf_op jit(solution)/shard_map/hidden/pallas_call | solution.py:376
  27.6 0.6 %collective-permute-start.9 = (bf16[64,4224]{1,0:T(8,128)(2,1)S(1)}, bf16[64,4224]{1,0:T(8,128)(2,1)S(1)}, u32[]{:S(2)}, u32[]{:S(2)}) collective-permute-start(bf16[64,4224]{1,0:T(8,128)(2,1)S(1)} %get-tuple-element.21.mine_ref), channel_id=1, source_target_pairs={{0,1},{1,0},{2,3},{3,2},{4,5},{5,4},{6,7},{7,6},{8,9},{9,8},{10,11... | collective-permute-start | bytes 1622024 | tf_op jit(solution)/shard_map/ppermute | solution.py:292
  28.1 1.6 %collective-permute-done.9.other_ref = bf16[64,4224]{1,0:T(8,128)(2,1)S(1)} collective-permute-done((bf16[64,4224]{1,0:T(8,128)(2,1)S(1)}, bf16[64,4224]{1,0:T(8,128)(2,1)S(1)}, u32[]{:S(2)}, u32[]{:S(2)}) %collective-permute-start.9) | collective-permute-done | bytes 540704 | tf_op jit(solution)/shard_map/ppermute | solution.py:292
  29.7 4.6 %logits.1 = f32[16,8,128]{2,1,0:T(8,128)S(1)} custom-call(s32[1]{0:T(128)} %bitcast.pos_ref.refs_0_, bf16[64,4224]{1,0:T(8,128)(2,1)S(1)} %get-tuple-element.21.mine_ref, bf16[64,4224]{1,0:T(8,128)(2,1)S(1)} %collective-permute-done.9.other_ref, bf16[512,4096]{1,0:T(8,128)(2,1)S(1)} %get-tuple-element.22.first_ref, ...), custom_call_target="tpu_custom_call" | custom-call | tf_op jit(solution)/shard_map/logits/pallas_call | solution.py:397
  34.3 10.1 %all_to_all.5.stats_ref = f32[16,8,128]{2,1,0:T(8,128)S(1)} all-to-all(f32[16,8,128]{2,1,0:T(8,128)S(1)} %logits.1), channel_id=1, replica_groups=mesh['groups'=2,'dp'=16] {'dp'}, dimensions={0} | all-to-all | bytes 131072 | tf_op jit(solution)/shard_map/all_to_all | solution.py:407
  44.4 0.9 %finish.1 = f32[1,2,4]{2,1,0:T(2,128)} custom-call(f32[16,8,128]{2,1,0:T(8,128)S(1)} %all_to_all.5.stats_ref, bf16[64,4224]{1,0:T(8,128)(2,1)S(1)} %get-tuple-element.21.mine_ref), custom_call_target="tpu_custom_call" | custom-call | tf_op jit(solution)/shard_map/finish/pallas_call | solution.py:408
  (2 shorter events, 0.0 us)
Async XLA Ops:
  0.9 8.6 %collective-permute-start = (bf16[56,768]{1,0:T(8,128)(2,1)S(1)}, bf16[56,768]{1,0:T(8,128)(2,1)S(1)}, u32[]{:S(2)}, u32[]{:S(2)}) collective-permute-start(bf16[56,768]{1,0:T(8,128)(2,1)S(1)} %pack.1.refs_0_), channel_id=1, source_target_pairs={{0,12},{1,13},{2,14},{3,15},{4,8},{5,9},{6,10},{7,11},{8,4},{9,5},... | collective-permute-start | bytes 258056 | tf_op jit(solution)/shard_map/ppermute | solution.py:292
  6.0 7.7 %collective-permute-start.1 = (bf16[56,768]{1,0:T(8,128)(2,1)S(1)}, bf16[56,768]{1,0:T(8,128)(2,1)S(1)}, u32[]{:S(2)}, u32[]{:S(2)}) collective-permute-start(bf16[56,768]{1,0:T(8,128)(2,1)S(1)} %pack.1.refs_0_), channel_id=1, source_target_pairs={{0,4},{1,5},{2,6},{3,7},{4,0},{5,1},{6,2},{7,3},{8,12},{9,13},{10,... | collective-permute-start | bytes 258056 | tf_op jit(solution)/shard_map/ppermute | solution.py:292
  9.5 5.6 %collective-permute-start.3 = (bf16[56,768]{1,0:T(8,128)(2,1)S(1)}, bf16[56,768]{1,0:T(8,128)(2,1)S(1)}, u32[]{:S(2)}, u32[]{:S(2)}) collective-permute-start(bf16[56,768]{1,0:T(8,128)(2,1)S(1)} %collective-permute-done.refs_1_), channel_id=1, source_target_pairs={{0,4},{1,5},{2,6},{3,7},{4,0},{5,1},{6,2},{7,3},{8,12},{9,13},{10,... | collective-permute-start | bytes 258056 | tf_op jit(solution)/shard_map/ppermute | solution.py:292
  11.6 5.4 %collective-permute-start.2 = (bf16[56,768]{1,0:T(8,128)(2,1)S(1)}, bf16[56,768]{1,0:T(8,128)(2,1)S(1)}, u32[]{:S(2)}, u32[]{:S(2)}) collective-permute-start(bf16[56,768]{1,0:T(8,128)(2,1)S(1)} %pack.1.refs_0_), channel_id=1, source_target_pairs={{0,2},{1,3},{2,0},{3,1},{4,6},{5,7},{6,4},{7,5},{8,10},{9,11},{10,... | collective-permute-start | bytes 258056 | tf_op jit(solution)/shard_map/ppermute | solution.py:292
  13.1 6.8 %collective-permute-start.4 = (bf16[56,768]{1,0:T(8,128)(2,1)S(1)}, bf16[56,768]{1,0:T(8,128)(2,1)S(1)}, u32[]{:S(2)}, u32[]{:S(2)}) collective-permute-start(bf16[56,768]{1,0:T(8,128)(2,1)S(1)} %collective-permute-done.refs_1_), channel_id=1, source_target_pairs={{0,2},{1,3},{2,0},{3,1},{4,6},{5,7},{6,4},{7,5},{8,10},{9,11},{10,... | collective-permute-start | bytes 258056 | tf_op jit(solution)/shard_map/ppermute | solution.py:292
  13.7 6.3 %collective-permute-start.5 = (bf16[56,768]{1,0:T(8,128)(2,1)S(1)}, bf16[56,768]{1,0:T(8,128)(2,1)S(1)}, u32[]{:S(2)}, u32[]{:S(2)}) collective-permute-start(bf16[56,768]{1,0:T(8,128)(2,1)S(1)} %collective-permute-done.1.refs_2_), channel_id=1, source_target_pairs={{0,2},{1,3},{2,0},{3,1},{4,6},{5,7},{6,4},{7,5},{8,10},{9,11},{10,... | collective-permute-start | bytes 258056 | tf_op jit(solution)/shard_map/ppermute | solution.py:292
  15.2 5.7 %collective-permute-start.6 = (bf16[56,768]{1,0:T(8,128)(2,1)S(1)}, bf16[56,768]{1,0:T(8,128)(2,1)S(1)}, u32[]{:S(2)}, u32[]{:S(2)}) collective-permute-start(bf16[56,768]{1,0:T(8,128)(2,1)S(1)} %collective-permute-done.3.after_ref.refs_0_.refs_4_), channel_id=1, source_target_pairs={{0,2},{1,3},{2,0},{3,1},{4,6},{5,7},{6,4},{7,5},{8,10},{9,11},{10,... | collective-permute-start | bytes 258056 | tf_op jit(solution)/shard_map/ppermute | solution.py:292
  17.0 5.9 %collective-permute-start.7 = (bf16[128,768]{1,0:T(8,128)(2,1)S(1)}, bf16[128,768]{1,0:T(8,128)(2,1)S(1)}, u32[]{:S(2)}, u32[]{:S(2)}) collective-permute-start(bf16[128,768]{1,0:T(8,128)(2,1)S(1)} %collect.2.refs_1_), channel_id=1, source_target_pairs={{0,1},{1,0},{2,3},{3,2},{4,5},{5,4},{6,7},{7,6},{8,9},{9,8},{10,11... | collective-permute-start | bytes 589832 | tf_op jit(solution)/shard_map/ppermute | solution.py:292
  20.9 2.0 %collective-permute-start.8 = (bf16[128,768]{1,0:T(8,128)(2,1)S(1)}, bf16[128,768]{1,0:T(8,128)(2,1)S(1)}, u32[]{:S(2)}, u32[]{:S(2)}) collective-permute-start(bf16[128,768]{1,0:T(8,128)(2,1)S(1)} %collect.3.refs_2_), channel_id=1, source_target_pairs={{0,1},{1,0},{2,3},{3,2},{4,5},{5,4},{6,7},{7,6},{8,9},{9,8},{10,11... | collective-permute-start | bytes 589832 | tf_op jit(solution)/shard_map/ppermute | solution.py:292
  27.6 2.1 %collective-permute-start.9 = (bf16[64,4224]{1,0:T(8,128)(2,1)S(1)}, bf16[64,4224]{1,0:T(8,128)(2,1)S(1)}, u32[]{:S(2)}, u32[]{:S(2)}) collective-permute-start(bf16[64,4224]{1,0:T(8,128)(2,1)S(1)} %get-tuple-element.21.mine_ref), channel_id=1, source_target_pairs={{0,1},{1,0},{2,3},{3,2},{4,5},{5,4},{6,7},{7,6},{8,9},{9,8},{10,11... | collective-permute-start | bytes 1622024 | tf_op jit(solution)/shard_map/ppermute | solution.py:292

commit v5 on v4

--- a/solution.py
+++ b/solution.py
@@ -9,6 +9,7 @@
 
 HEAD_DIM = 64
 LANES = 128
+SUBLANES = 8
 TILE = 256
 DIGIT = 256
 MIB = 1 << 20
@@ -238,36 +239,40 @@
         before += ref.shape[0]
     top = functools.reduce(jnp.maximum, tops)
     total = sum(t * jnp.exp(m - top) for t, m in zip(totals, tops))
-    packed = jnp.concatenate(
-        [top, total, sum(targets), length_ref[...], jnp.zeros((LANES - 4, row_total), jnp.float32)], 0
-    ).T
-    shards, rows = out_ref.shape[:2]
+    shards, _, width = out_ref.shape
+    rows = row_total // shards
+    field = iota((SUBLANES, width), 1) // rows
+    halves = []
+    for start in range(0, shards, SUBLANES):
+        half = jnp.zeros((SUBLANES, width), jnp.float32)
+        for s, values in enumerate((top, total, sum(targets), length_ref[...])):
+            shift = (s + 1 + start) * rows % width
+            spread = jnp.broadcast_to(pltpu.roll(values, shift, 1) if shift else values, half.shape)
+            half = jnp.where(field == s, pltpu.roll(spread, 0, 1, stride=rows, stride_axis=0), half)
+        halves.append(half)
+    packed = jnp.concatenate(halves, 0)
     for j in range(shards):
         away = order[j % len(order)] + j // len(order)
-        out_ref[pos_ref[0] ^ away] = packed[j * rows : (j + 1) * rows]
+        out_ref[pos_ref[0] ^ away] = packed[shards - 1 - j : shards - j]
 
 
 def finish_kernel(stats_ref, mine_ref, out_ref):
-    stats = stats_ref[...]
-    shards, rows, _ = stats.shape
-    cap_len = out_ref.shape[2]
-    model_width = mine_ref.shape[1] - LANES
-    lane = iota((rows, LANES), 1)
-    top = jnp.max(stats, 0)[:, 0:1]
-    total = jnp.zeros((rows, 1), jnp.float32)
-    target = jnp.zeros((rows, 1), jnp.float32)
-    length = jnp.zeros((rows, 1), jnp.float32)
-    cand = mine_ref[0:16, model_width:].astype(jnp.float32)[0:rows, 2:3]
-    for e in range(shards):
-        total += stats[e][:, 1:2] * jnp.exp(stats[e][:, 0:1] - top)
-        target += stats[e][:, 2:3]
-        length += jnp.where(cand == e, stats[e][:, 3:4], 0.0)
-    loglik = target - (top + jnp.log(total))
-    token = iota((rows, LANES), 0) % cap_len
-    kept = (token == lane) & (token.astype(jnp.float32) < length)
-    spread = jnp.where(kept, loglik, 0.0)
-    for k in range(out_ref.shape[1]):
-        out_ref[0, k : k + 1, :] = jnp.sum(spread[k * cap_len : (k + 1) * cap_len], 0, keepdims=True)[:, 0:cap_len]
+    shards, _, width = stats_ref.shape
+    _, top_count, cap_len = out_ref.shape
+    rows = top_count * cap_len
+    tops = jnp.concatenate([stats_ref[e] for e in range(shards)], 0)
+    totals, targets, lengths = (pltpu.roll(tops, width - s * rows, 1) for s in (1, 2, 3))
+    marks = mine_ref[0:16, mine_ref.shape[1] - width :].astype(jnp.float32)
+    cand = jnp.where(iota(marks.shape, 0) == iota(marks.shape, 1), marks[:, 2:3], 0.0)
+    cand = jnp.sum(cand, 0, keepdims=True).astype(jnp.int32)
+    length = jnp.sum(jnp.where(iota(tops.shape, 0) == cand, lengths, 0.0), 0, keepdims=True)
+    top = jnp.max(tops, 0, keepdims=True)
+    total = jnp.sum(totals * jnp.exp(tops - top), 0, keepdims=True)
+    loglik = jnp.sum(targets, 0, keepdims=True) - (top + jnp.log(total))
+    token = (iota(loglik.shape, 1) % cap_len).astype(jnp.float32)
+    loglik = jnp.where(token < length, loglik, 0.0)
+    for k in range(top_count):
+        out_ref[0, k : k + 1, :] = loglik[:, k * cap_len : (k + 1) * cap_len]
 
 
 def paired(
@@ -284,7 +289,7 @@
     row_total = blocks * pair_rows
     vocab = head_weight.shape[1]
     position = lax.axis_index("dp").astype(jnp.int32).reshape(1)
-    ahead = vocab * 3 // 8 // TILE * TILE
+    ahead = vocab // 2 // TILE * TILE + TILE
     heads, group = TILE // HEAD_DIM, LANES // prefix
     score_tiles = model_width // TILE * blocks // group
 
@@ -309,7 +314,7 @@
     )(*(in_hbm(a) for a in (candidates, caption_ids, query_rows, caption_states)))
 
     got = {0: message}
-    for away in (12, 4, 2):
+    for away in (12, 8, 4, 2):
         got[away] = swap(message, away)
     weight, bias, gain, length = pl.pallas_call(
         bring_kernel,
@@ -326,9 +331,9 @@
         cost_estimate=pl.CostEstimate(flops=0, bytes_accessed=4 * width * model_width, transcendentals=0),
         name="bring",
     )(position, caption_lengths, *(in_hbm(a) for a in (proj_weight, proj_bias, norm_gain.reshape(1, -1))))
+    got[6] = swap(got[4], 2)
     got[12], length = lax.optimization_barrier((got[12], length))
-    got[8] = swap(got[12], 4)
-    for away in (12, 4, 8):
+    for away in (12, 8):
         got[away + 2] = swap(got[away], 2)
     head_weight = in_hbm(head_weight.T)
     head_first, done = pl.pallas_call(
@@ -344,7 +349,7 @@
         cost_estimate=pl.CostEstimate(flops=0, bytes_accessed=4 * ahead * model_width, transcendentals=0),
         name="bring_head",
     )(got[8], head_weight)
-    order = (0, 12, 4, 2, 8, 14, 6, 10)
+    order = (0, 2, 4, 6, 8, 12, 10, 14)
     mine = [got[away] for away in order]
 
     def collect(msgs, *after):
@@ -396,7 +401,7 @@
 
     stats = pl.pallas_call(
         functools.partial(logits_kernel, order),
-        out_shape=jax.ShapeDtypeStruct((shards, pair_rows, LANES), jnp.float32),
+        out_shape=jax.ShapeDtypeStruct((shards, 1, LANES), jnp.float32),
         in_specs=[SMEM] + [VMEM] * 5,
         out_specs=VMEM,
         scratch_shapes=[pltpu.VMEM((2 * row_total, model_width), jnp.bfloat16)],

time: 45.6 us -> 43.8 us (0.961)
  waiting for transfers between devices: 4.46 us -> 2.3 us
  blocking collectives: 10.1 us -> 10.7 us
    ppermute x10, waiting for transfers between devices: 4.46 us -> 2.3 us  [swap(): return lax.ppermute(a, 'dp', [(i, i ^ away) for i in range(shards)])]
    pallas_call x1, Pallas kernels: 2.21 us -> 3.5 us  [paired(): pl.pallas_call(bring_head_kernel, out_shape=(pltpu.VMEM((ahead, model_wid...]
    pallas_call x1, Pallas kernels: 4.7 us -> 3.45 us  [paired(): pl.pallas_call(functools.partial(hidden_kernel, order, prefix, cap_len),...]
    all_to_all x1, blocking collectives: 10.1 us -> 10.7 us  [paired(): stats = lax.all_to_all(stats, 'dp', 0, 0, tiled=True)]
  transfers between devices with their start and end apart: 10 -> 10, of which waited for: 4 -> 3; matrix products, arithmetic and copies ran while one was open for 0% -> 0% of each run, Pallas kernels for 15% -> 19%
where the time goes in v5:
time: 43.8 us; the launch traced here: 43.5 us
  Pallas kernels  17.9 us (41%)
  starting transfers between devices  11.8 us (27%)
  blocking collectives  10.7 us (24%)
  waiting for transfers between devices  2.3 us (5%)
  between operations  0.77 us (2%)
    ppermute x10, starting transfers between devices, swap(): return lax.ppermute(a, 'dp', [(i, i ^ away) for i in range(shards)])  11.8 us
    all_to_all x1, blocking collectives, paired(): stats = lax.all_to_all(stats, 'dp', 0, 0, tiled=True)  10.7 us
    pallas_call x1, Pallas kernels, paired(): pl.pallas_call(functools.partial(logits_kernel, order), out_shape=jax.Sha...  4.66 us
    pallas_call x1, Pallas kernels, paired(): pl.pallas_call(bring_head_kernel, out_shape=(pltpu.VMEM((ahead, model_wid...  3.5 us
    pallas_call x1, Pallas kernels, paired(): pl.pallas_call(functools.partial(hidden_kernel, order, prefix, cap_len),...  3.45 us
    pallas_call x1, Pallas kernels, paired(): pl.pallas_call(bring_kernel, out_shape=(pltpu.VMEM((width, model_width),...  2.85 us
    ppermute x10, waiting for transfers between devices, swap(): return lax.ppermute(a, 'dp', [(i, i ^ away) for i in range(shards)])  2.3 us
    pallas_call x1, Pallas kernels, paired(): pl.pallas_call(functools.partial(keys_kernel, blocks), out_shape=pltpu.VM...  1.85 us
  transfers between devices with their start and end apart: 10, of which 3 were waited for; matrix products, arithmetic and copies ran while one was open for 0% of the time, Pallas kernels for 19%

profile of v5, /device:TPU:0, one launch (start us, length us, event | category | flops | bytes accessed | tf_op | source)
XLA Modules:
  0.0 43.5 jit_solution(3123446542852409448)
XLA Ops:
  0.0 0.9 %pack.1.refs_0_ = bf16[56,768]{1,0:T(8,128)(2,1)S(1)} custom-call(s32[1,2]{1,0:T(1,128)} %cand_hbm.1, s32[1,4]{1,0:T(1,128)} %ids_hbm.1, bf16[1,32,768]{2,1,0:T(8,128)(2,1)} %rows_hbm.1, bf16[1,4,4096]{2,1,0:T(4,128)(2,1)} %states_hbm.1), custom_call_target="tpu_custom_call" | custom-call | tf_op jit(solution)/shard_map/pack/pallas_call | solution.py:299
  0.9 5.1 %collective-permute-start.4 = (bf16[56,768]{1,0:T(8,128)(2,1)S(1)}, bf16[56,768]{1,0:T(8,128)(2,1)S(1)}, u32[]{:S(2)}, u32[]{:S(2)}) collective-permute-start(bf16[56,768]{1,0:T(8,128)(2,1)S(1)} %pack.1.refs_0_), channel_id=1, source_target_pairs={{0,12},{1,13},{2,14},{3,15},{4,8},{5,9},{6,10},{7,11},{8,4},{9,5},... | collective-permute-start | bytes 258056 | tf_op jit(solution)/shard_map/ppermute | solution.py:297
  6.0 0.0 collective-permute-start.1
  6.0 0.6 %collective-permute-start.3 = (bf16[56,768]{1,0:T(8,128)(2,1)S(1)}, bf16[56,768]{1,0:T(8,128)(2,1)S(1)}, u32[]{:S(2)}, u32[]{:S(2)}) collective-permute-start(bf16[56,768]{1,0:T(8,128)(2,1)S(1)} %pack.1.refs_0_), channel_id=1, source_target_pairs={{0,8},{1,9},{2,10},{3,11},{4,12},{5,13},{6,14},{7,15},{8,0},{9,1},... | collective-permute-start | bytes 258056 | tf_op jit(solution)/shard_map/ppermute | solution.py:297
  6.6 1.7 %collective-permute-start = (bf16[56,768]{1,0:T(8,128)(2,1)S(1)}, bf16[56,768]{1,0:T(8,128)(2,1)S(1)}, u32[]{:S(2)}, u32[]{:S(2)}) collective-permute-start(bf16[56,768]{1,0:T(8,128)(2,1)S(1)} %pack.1.refs_0_), channel_id=1, source_target_pairs={{0,2},{1,3},{2,0},{3,1},{4,6},{5,7},{6,4},{7,5},{8,10},{9,11},{10,... | collective-permute-start | bytes 258056 | tf_op jit(solution)/shard_map/ppermute | solution.py:297
  9.0 2.8 %bring.1 = (bf16[768,4096]{1,0:T(8,128)(2,1)S(1)}, f32[1,4096]{1,0:T(1,128)S(1)}, f32[1,4096]{1,0:T(1,128)S(1)}, f32[1,128]{1,0:T(1,128)S(1)}) custom-call(s32[1]{0:T(128)} %bitcast.pos_ref.refs_0_, s32[1]{0:T(128)S(6)} %copy.10.len_ref, bf16[768,4096]{1,0:T(8,128)(2,1)} %weight_hbm.1, bf16[4096]{0:T(1024)(128)(2,1)} %bias_hbm.1, f32[1,4096]{1,0:T(1,128)} %bitcast.5), custom_call_target="tpu_custom_call" | custom-call | bytes 12582912 | tf_op jit(solution)/shard_map/bring/pallas_call | solution.py:319
  11.8 0.0 collective-permute-done.4.refs_1_.refs_5_
  11.8 0.4 collective-permute-done.1.refs_2_
  12.2 1.6 %collective-permute-start.2 = (bf16[56,768]{1,0:T(8,128)(2,1)S(1)}, bf16[56,768]{1,0:T(8,128)(2,1)S(1)}, u32[]{:S(2)}, u32[]{:S(2)}) collective-permute-start(bf16[56,768]{1,0:T(8,128)(2,1)S(1)} %collective-permute-done.1.refs_2_), channel_id=1, source_target_pairs={{0,2},{1,3},{2,0},{3,1},{4,6},{5,7},{6,4},{7,5},{8,10},{9,11},{10,... | collective-permute-start | bytes 258056 | tf_op jit(solution)/shard_map/ppermute | solution.py:297
  13.8 0.0 collective-permute-done.3.after_ref.refs_0_.refs_4_
  13.8 0.9 %collective-permute-start.5 = (bf16[56,768]{1,0:T(8,128)(2,1)S(1)}, bf16[56,768]{1,0:T(8,128)(2,1)S(1)}, u32[]{:S(2)}, u32[]{:S(2)}) collective-permute-start(bf16[56,768]{1,0:T(8,128)(2,1)S(1)} %collective-permute-done.3.after_ref.refs_0_.refs_4_), channel_id=1, source_target_pairs={{0,2},{1,3},{2,0},{3,1},{4,6},{5,7},{6,4},{7,5},{8,10},{9,11},{10,... | collective-permute-start | bytes 258056 | tf_op jit(solution)/shard_map/ppermute | solution.py:297
  14.7 1.1 %collective-permute-start.6 = (bf16[56,768]{1,0:T(8,128)(2,1)S(1)}, bf16[56,768]{1,0:T(8,128)(2,1)S(1)}, u32[]{:S(2)}, u32[]{:S(2)}) collective-permute-start(bf16[56,768]{1,0:T(8,128)(2,1)S(1)} %collective-permute-done.4.refs_1_.refs_5_), channel_id=1, source_target_pairs={{0,2},{1,3},{2,0},{3,1},{4,6},{5,7},{6,4},{7,5},{8,10},{9,11},{10,... | collective-permute-start | bytes 258056 | tf_op jit(solution)/shard_map/ppermute | solution.py:297
  15.9 3.5 %bring_head.1 = (bf16[1024,4096]{1,0:T(8,128)(2,1)S(1)}, f32[8,128]{1,0:T(8,128)S(1)}) custom-call(bf16[56,768]{1,0:T(8,128)(2,1)S(1)} %collective-permute-done.3.after_ref.refs_0_.refs_4_, bf16[2008,4096]{1,0:T(8,128)(2,1)} %bitcast.3), custom_call_target="tpu_custom_call" | custom-call | bytes 16777216 | tf_op jit(solution)/shard_map/bring_head/pallas_call | solution.py:339
  19.4 0.0 collective-permute-done.refs_1_
  19.4 0.0 collective-permute-done.2.refs_3_
  19.4 0.1 collective-permute-start.7
  19.5 0.0 collective-permute-done.5.refs_2_.refs_6_
  19.5 0.1 collective-permute-done.6.refs_3_.refs_7_
  19.6 0.5 %collective-permute-start.8 = (bf16[128,768]{1,0:T(8,128)(2,1)S(1)}, bf16[128,768]{1,0:T(8,128)(2,1)S(1)}, u32[]{:S(2)}, u32[]{:S(2)}) collective-permute-start(bf16[128,768]{1,0:T(8,128)(2,1)S(1)} %collect.3.refs_2_), channel_id=1, source_target_pairs={{0,1},{1,0},{2,3},{3,2},{4,5},{5,4},{6,7},{7,6},{8,9},{9,8},{10,11... | collective-permute-start | bytes 589832 | tf_op jit(solution)/shard_map/ppermute | solution.py:297
  20.1 1.8 %keys.1.refs_5_ = bf16[256,4096]{1,0:T(8,128)(2,1)S(1)} custom-call(bf16[56,768]{1,0:T(8,128)(2,1)S(1)} %pack.1.refs_0_, bf16[56,768]{1,0:T(8,128)(2,1)S(1)} %collective-permute-done.refs_1_, bf16[56,768]{1,0:T(8,128)(2,1)S(1)} %collective-permute-done.1.refs_2_, bf16[56,768]{1,0:T(8,128)(2,1)S(1)} %collective-permute-done.2.refs_3_, ...), custom_call_target="tpu_custom_call" | custom-call | flops 1610612736 | bytes 12582912 | tf_op jit(solution)/shard_map/keys/pallas_call | solution.py:368
  21.9 0.0 collective-permute-done.7.refs_3_
  21.9 0.0 collective-permute-done.8.refs_4_
  21.9 3.5 %hidden.1 = (bf16[64,4224]{1,0:T(8,128)(2,1)S(1)}, bf16[984,4096]{1,0:T(8,128)(2,1)S(1)}) custom-call(s32[1]{0:T(128)} %bitcast.pos_ref.refs_0_, bf16[128,768]{1,0:T(8,128)(2,1)S(1)} %collect.2.refs_1_, bf16[128,768]{1,0:T(8,128)(2,1)S(1)} %collect.3.refs_2_, bf16[128,768]{1,0:T(8,128)(2,1)S(1)} %collective-permute-done.7.refs_3_, ...), custom_call_target="tpu_custom_call" | custom-call | tf_op jit(solution)/shard_map/hidden/pallas_call | solution.py:381
  25.4 0.1 collective-permute-start.9
  25.5 1.9 %collective-permute-done.9.other_ref = bf16[64,4224]{1,0:T(8,128)(2,1)S(1)} collective-permute-done((bf16[64,4224]{1,0:T(8,128)(2,1)S(1)}, bf16[64,4224]{1,0:T(8,128)(2,1)S(1)}, u32[]{:S(2)}, u32[]{:S(2)}) %collective-permute-start.9) | collective-permute-done | bytes 540704 | tf_op jit(solution)/shard_map/ppermute | solution.py:297
  27.4 4.7 %logits.1 = f32[16,1,128]{2,1,0:T(1,128)S(1)} custom-call(s32[1]{0:T(128)} %bitcast.pos_ref.refs_0_, bf16[64,4224]{1,0:T(8,128)(2,1)S(1)} %get-tuple-element.21.mine_ref, bf16[64,4224]{1,0:T(8,128)(2,1)S(1)} %collective-permute-done.9.other_ref, bf16[1024,4096]{1,0:T(8,128)(2,1)S(1)} %get-tuple-element.22.first_ref, ...), custom_call_target="tpu_custom_call" | custom-call | tf_op jit(solution)/shard_map/logits/pallas_call | solution.py:402
  32.1 10.7 %all_to_all.5.stats_ref = f32[16,1,128]{2,1,0:T(1,128)S(1)} all-to-all(f32[16,1,128]{2,1,0:T(1,128)S(1)} %logits.1), channel_id=1, replica_groups=mesh['groups'=2,'dp'=16] {'dp'}, dimensions={0} | all-to-all | bytes 16384 | tf_op jit(solution)/shard_map/all_to_all | solution.py:412
  42.8 0.7 %finish.1 = f32[1,2,4]{2,1,0:T(2,128)} custom-call(f32[16,1,128]{2,1,0:T(1,128)S(1)} %all_to_all.5.stats_ref, bf16[64,4224]{1,0:T(8,128)(2,1)S(1)} %get-tuple-element.21.mine_ref), custom_call_target="tpu_custom_call" | custom-call | tf_op jit(solution)/shard_map/finish/pallas_call | solution.py:413
  (2 shorter events, 0.0 us)
Async XLA Ops:
  0.9 10.9 %collective-permute-start.4 = (bf16[56,768]{1,0:T(8,128)(2,1)S(1)}, bf16[56,768]{1,0:T(8,128)(2,1)S(1)}, u32[]{:S(2)}, u32[]{:S(2)}) collective-permute-start(bf16[56,768]{1,0:T(8,128)(2,1)S(1)} %pack.1.refs_0_), channel_id=1, source_target_pairs={{0,12},{1,13},{2,14},{3,15},{4,8},{5,9},{6,10},{7,11},{8,4},{9,5},... | collective-permute-start | bytes 258056 | tf_op jit(solution)/shard_map/ppermute | solution.py:297
  6.0 6.2 %collective-permute-start.1 = (bf16[56,768]{1,0:T(8,128)(2,1)S(1)}, bf16[56,768]{1,0:T(8,128)(2,1)S(1)}, u32[]{:S(2)}, u32[]{:S(2)}) collective-permute-start(bf16[56,768]{1,0:T(8,128)(2,1)S(1)} %pack.1.refs_0_), channel_id=1, source_target_pairs={{0,4},{1,5},{2,6},{3,7},{4,0},{5,1},{6,2},{7,3},{8,12},{9,13},{10,... | collective-permute-start | bytes 258056 | tf_op jit(solution)/shard_map/ppermute | solution.py:297
  6.0 7.8 %collective-permute-start.3 = (bf16[56,768]{1,0:T(8,128)(2,1)S(1)}, bf16[56,768]{1,0:T(8,128)(2,1)S(1)}, u32[]{:S(2)}, u32[]{:S(2)}) collective-permute-start(bf16[56,768]{1,0:T(8,128)(2,1)S(1)} %pack.1.refs_0_), channel_id=1, source_target_pairs={{0,8},{1,9},{2,10},{3,11},{4,12},{5,13},{6,14},{7,15},{8,0},{9,1},... | collective-permute-start | bytes 258056 | tf_op jit(solution)/shard_map/ppermute | solution.py:297
  6.6 12.7 %collective-permute-start = (bf16[56,768]{1,0:T(8,128)(2,1)S(1)}, bf16[56,768]{1,0:T(8,128)(2,1)S(1)}, u32[]{:S(2)}, u32[]{:S(2)}) collective-permute-start(bf16[56,768]{1,0:T(8,128)(2,1)S(1)} %pack.1.refs_0_), channel_id=1, source_target_pairs={{0,2},{1,3},{2,0},{3,1},{4,6},{5,7},{6,4},{7,5},{8,10},{9,11},{10,... | collective-permute-start | bytes 258056 | tf_op jit(solution)/shard_map/ppermute | solution.py:297
  12.2 7.2 %collective-permute-start.2 = (bf16[56,768]{1,0:T(8,128)(2,1)S(1)}, bf16[56,768]{1,0:T(8,128)(2,1)S(1)}, u32[]{:S(2)}, u32[]{:S(2)}) collective-permute-start(bf16[56,768]{1,0:T(8,128)(2,1)S(1)} %collective-permute-done.1.refs_2_), channel_id=1, source_target_pairs={{0,2},{1,3},{2,0},{3,1},{4,6},{5,7},{6,4},{7,5},{8,10},{9,11},{10,... | collective-permute-start | bytes 258056 | tf_op jit(solution)/shard_map/ppermute | solution.py:297
  13.8 5.7 %collective-permute-start.5 = (bf16[56,768]{1,0:T(8,128)(2,1)S(1)}, bf16[56,768]{1,0:T(8,128)(2,1)S(1)}, u32[]{:S(2)}, u32[]{:S(2)}) collective-permute-start(bf16[56,768]{1,0:T(8,128)(2,1)S(1)} %collective-permute-done.3.after_ref.refs_0_.refs_4_), channel_id=1, source_target_pairs={{0,2},{1,3},{2,0},{3,1},{4,6},{5,7},{6,4},{7,5},{8,10},{9,11},{10,... | collective-permute-start | bytes 258056 | tf_op jit(solution)/shard_map/ppermute | solution.py:297
  14.7 4.8 %collective-permute-start.6 = (bf16[56,768]{1,0:T(8,128)(2,1)S(1)}, bf16[56,768]{1,0:T(8,128)(2,1)S(1)}, u32[]{:S(2)}, u32[]{:S(2)}) collective-permute-start(bf16[56,768]{1,0:T(8,128)(2,1)S(1)} %collective-permute-done.4.refs_1_.refs_5_), channel_id=1, source_target_pairs={{0,2},{1,3},{2,0},{3,1},{4,6},{5,7},{6,4},{7,5},{8,10},{9,11},{10,... | collective-permute-start | bytes 258056 | tf_op jit(solution)/shard_map/ppermute | solution.py:297
  19.4 2.5 %collective-permute-start.7 = (bf16[128,768]{1,0:T(8,128)(2,1)S(1)}, bf16[128,768]{1,0:T(8,128)(2,1)S(1)}, u32[]{:S(2)}, u32[]{:S(2)}) collective-permute-start(bf16[128,768]{1,0:T(8,128)(2,1)S(1)} %collect.2.refs_1_), channel_id=1, source_target_pairs={{0,1},{1,0},{2,3},{3,2},{4,5},{5,4},{6,7},{7,6},{8,9},{9,8},{10,11... | collective-permute-start | bytes 589832 | tf_op jit(solution)/shard_map/ppermute | solution.py:297
  19.6 2.4 %collective-permute-start.8 = (bf16[128,768]{1,0:T(8,128)(2,1)S(1)}, bf16[128,768]{1,0:T(8,128)(2,1)S(1)}, u32[]{:S(2)}, u32[]{:S(2)}) collective-permute-start(bf16[128,768]{1,0:T(8,128)(2,1)S(1)} %collect.3.refs_2_), channel_id=1, source_target_pairs={{0,1},{1,0},{2,3},{3,2},{4,5},{5,4},{6,7},{7,6},{8,9},{9,8},{10,11... | collective-permute-start | bytes 589832 | tf_op jit(solution)/shard_map/ppermute | solution.py:297
  25.4 2.0 %collective-permute-start.9 = (bf16[64,4224]{1,0:T(8,128)(2,1)S(1)}, bf16[64,4224]{1,0:T(8,128)(2,1)S(1)}, u32[]{:S(2)}, u32[]{:S(2)}) collective-permute-start(bf16[64,4224]{1,0:T(8,128)(2,1)S(1)} %get-tuple-element.21.mine_ref), channel_id=1, source_target_pairs={{0,1},{1,0},{2,3},{3,2},{4,5},{5,4},{6,7},{7,6},{8,9},{9,8},{10,11... | collective-permute-start | bytes 1622024 | tf_op jit(solution)/shard_map/ppermute | solution.py:297

commit v6 on v5

--- a/solution.py
+++ b/solution.py
@@ -21,7 +21,6 @@
 VMEM = pl.BlockSpec(memory_space=pltpu.VMEM)
 SMEM = pl.BlockSpec(memory_space=pltpu.SMEM)
 HBM = pl.BlockSpec(memory_space=pltpu.HBM)
-ANY = pl.BlockSpec(memory_space=pl.ANY)
 ROWS_BY_ROWS = (((1,), (1,)), ((), ()))
 
 
@@ -31,6 +30,10 @@
 
 def in_hbm(a):
     return pltpu.with_memory_space_constraint(a, pltpu.HBM)
+
+
+def in_vmem(a):
+    return pltpu.with_memory_space_constraint(a, pltpu.VMEM)
 
 
 def dot(a, b):
@@ -75,16 +78,9 @@
     out_ref[held:, :] = rows[0]
 
 
-def bring_kernel(pos_ref, len_ref, weight_hbm, bias_hbm, gain_hbm, weight_ref, bias_ref, gain_ref, length_ref, bias, sem):
-    pairs = ((bias_hbm, bias), (gain_hbm, gain_ref), (weight_hbm, weight_ref))
-    copies = [pltpu.make_async_copy(src, dst, sem.at[i]) for i, (src, dst) in enumerate(pairs)]
-    for copy in copies:
-        copy.start()
+def length_kernel(pos_ref, len_ref, *refs):
+    length_ref = refs[-1]
     length_ref[...] = jnp.full(length_ref.shape, len_ref[0].astype(jnp.float32))
-    copies[0].wait()
-    bias_ref[...] = bias[...].astype(jnp.float32).reshape(bias_ref.shape)
-    for copy in copies[1:]:
-        copy.wait()
 
 
 def cuts(total, parts):
@@ -92,25 +88,9 @@
     return [(i, min(total, i + piece)) for i in range(0, total, piece)]
 
 
-def copies_of(src, first, dst, sem):
-    return [
-        pltpu.make_async_copy(src.at[first + i : first + j], dst.at[i:j], sem.at[n])
-        for n, (i, j) in enumerate(cuts(dst.shape[0], sem.shape[0]))
-    ]
-
-
-def bring_head_kernel(after_ref, head_hbm, head_ref, done_ref, sem):
-    copies = copies_of(head_hbm, 0, head_ref, sem)
-    for copy in copies:
-        copy.start()
-    done_ref[...] = jnp.zeros_like(done_ref)
-    for copy in copies:
-        copy.wait()
-
-
-def collect_kernel(count, *refs):
-    msgs, out_ref = refs[:count], refs[-1]
-    held = out_ref.shape[0] // count
+def collect_kernel(*refs):
+    *msgs, out_ref = refs
+    held = out_ref.shape[0] // len(msgs)
     for i, msg in enumerate(msgs):
         out_ref[i * held : (i + 1) * held, :] = msg[0:held, :]
 
@@ -121,6 +101,7 @@
     for j, msg in enumerate(msgs):
         rows[j * prefix : (j + 1) * prefix, :] = msg[msg.shape[0] - prefix :, :]
     step = 512
+    bias = bias[...].astype(jnp.float32).reshape(1, keys.shape[1])
     for i in range(0, keys.shape[1], step):
         summed = dot(rows[...], weight[:, i : i + step])
         keys[:, i : i + step] = (summed + bias[:, i : i + step]).astype(jnp.bfloat16)
@@ -128,10 +109,7 @@
 
 def hidden_kernel(order, prefix, cap_len, *refs):
     pos_ref, *cap_refs = refs[:5]
-    keys, gain_ref, head_hbm, out_ref, head_ref, caps, query, mixed, bias, scores, weights, sem = refs[5:]
-    head_copies = copies_of(head_hbm, head_hbm.shape[0] - head_ref.shape[0], head_ref, sem)
-    for copy in head_copies:
-        copy.start()
+    keys, gain_ref, out_ref, caps, query, mixed, bias, scores, weights = refs[5:]
     blocks = len(order)
     width = caps.shape[1]
     model_width = mixed.shape[1]
@@ -211,11 +189,9 @@
     out_ref[:, 0:model_width] = (mixed[...] * scale * gain_ref[...]).astype(jnp.bfloat16)
     marks = query[:, model_width:]
     out_ref[:, model_width:] = jnp.where(iota(marks.shape, 1) == 2, found.astype(jnp.bfloat16), marks)
-    for copy in head_copies:
-        copy.wait()
-
-
-def logits_kernel(order, pos_ref, mine_ref, other_ref, first_ref, last_ref, length_ref, out_ref, states):
+
+
+def logits_kernel(order, pos_ref, mine_ref, other_ref, head_ref, length_ref, out_ref, states):
     half = mine_ref.shape[0]
     model_width = states.shape[1]
     row_total = 2 * half
@@ -224,19 +200,16 @@
     digits = jnp.concatenate(
         [ref[:, model_width:].astype(jnp.float32) for ref in (mine_ref, other_ref)], 0
     ).T
-    vocab = first_ref.shape[0] + last_ref.shape[0]
+    vocab = head_ref.shape[0]
     ids = (digits[0:1] * DIGIT + digits[1:2]).astype(jnp.int32) - pos_ref[0] * vocab
     tops, totals, targets = [], [], []
-    before = 0
-    for ref in (first_ref, last_ref):
-        for i, j in cuts(ref.shape[0], -(-ref.shape[0] // TILE)):
-            values = dot_rows(ref[i:j, :], states[...])
-            top = jnp.max(values, 0, keepdims=True)
-            tops.append(top)
-            totals.append(jnp.sum(jnp.exp(values - top), 0, keepdims=True))
-            hit = iota(values.shape, 0) == ids - (before + i)
-            targets.append(jnp.sum(jnp.where(hit, values, 0.0), 0, keepdims=True))
-        before += ref.shape[0]
+    for i, j in cuts(vocab, -(-vocab // TILE)):
+        values = dot_rows(head_ref[i:j, :], states[...])
+        top = jnp.max(values, 0, keepdims=True)
+        tops.append(top)
+        totals.append(jnp.sum(jnp.exp(values - top), 0, keepdims=True))
+        hit = iota(values.shape, 0) == ids - i
+        targets.append(jnp.sum(jnp.where(hit, values, 0.0), 0, keepdims=True))
     top = functools.reduce(jnp.maximum, tops)
     total = sum(t * jnp.exp(m - top) for t, m in zip(totals, tops))
     shards, _, width = out_ref.shape
@@ -287,9 +260,7 @@
     piece_rows = cap_len * -(-model_width // width)
     held = -(-piece_rows // 16) * 16
     row_total = blocks * pair_rows
-    vocab = head_weight.shape[1]
     position = lax.axis_index("dp").astype(jnp.int32).reshape(1)
-    ahead = vocab // 2 // TILE * TILE + TILE
     heads, group = TILE // HEAD_DIM, LANES // prefix
     score_tiles = model_width // TILE * blocks // group
 
@@ -316,53 +287,32 @@
     got = {0: message}
     for away in (12, 8, 4, 2):
         got[away] = swap(message, away)
-    weight, bias, gain, length = pl.pallas_call(
-        bring_kernel,
-        out_shape=(
-            pltpu.VMEM((width, model_width), jnp.bfloat16),
-            pltpu.VMEM((1, model_width), jnp.float32),
-            pltpu.VMEM((1, model_width), jnp.float32),
-            pltpu.VMEM((1, LANES), jnp.float32),
-        ),
-        in_specs=[SMEM] * 2 + [HBM] * 3,
-        out_specs=(VMEM,) * 4,
-        scratch_shapes=[pltpu.VMEM((model_width,), jnp.bfloat16), pltpu.SemaphoreType.DMA((3,))],
-        compiler_params=pltpu.CompilerParams(vmem_limit_bytes=2 * MIB),
-        cost_estimate=pl.CostEstimate(flops=0, bytes_accessed=4 * width * model_width, transcendentals=0),
-        name="bring",
-    )(position, caption_lengths, *(in_hbm(a) for a in (proj_weight, proj_bias, norm_gain.reshape(1, -1))))
+    length = pl.pallas_call(
+        length_kernel,
+        out_shape=jax.ShapeDtypeStruct((1, LANES), jnp.float32),
+        in_specs=[SMEM, SMEM] + [HBM] * 3,
+        out_specs=VMEM,
+        compiler_params=pltpu.CompilerParams(vmem_limit_bytes=MIB),
+        name="length",
+    )(position, caption_lengths, in_hbm(head_weight.T), in_hbm(head_weight.T), in_hbm(proj_weight))
     got[6] = swap(got[4], 2)
-    got[12], length = lax.optimization_barrier((got[12], length))
-    for away in (12, 8):
-        got[away + 2] = swap(got[away], 2)
-    head_weight = in_hbm(head_weight.T)
-    head_first, done = pl.pallas_call(
-        bring_head_kernel,
-        out_shape=(
-            pltpu.VMEM((ahead, model_width), jnp.bfloat16),
-            pltpu.VMEM((8, LANES), jnp.float32),
-        ),
-        in_specs=[ANY, HBM],
-        out_specs=(VMEM, VMEM),
-        scratch_shapes=[pltpu.SemaphoreType.DMA((4,))],
-        compiler_params=pltpu.CompilerParams(vmem_limit_bytes=2 * MIB),
-        cost_estimate=pl.CostEstimate(flops=0, bytes_accessed=4 * ahead * model_width, transcendentals=0),
-        name="bring_head",
-    )(got[8], head_weight)
+    got[14] = swap(got[12], 2)
+    got[8], got[2], got[6], length = lax.optimization_barrier((got[8], got[2], got[6], length))
+    got[10] = swap(got[8], 2)
     order = (0, 2, 4, 6, 8, 12, 10, 14)
     mine = [got[away] for away in order]
 
-    def collect(msgs, *after):
+    def collect(msgs):
         return pl.pallas_call(
-            functools.partial(collect_kernel, len(msgs)),
+            collect_kernel,
             out_shape=jax.ShapeDtypeStruct((len(msgs) * held, width), jnp.bfloat16),
-            in_specs=[VMEM] * len(msgs) + [ANY] * len(after),
+            in_specs=[VMEM] * len(msgs),
             out_specs=VMEM,
             compiler_params=pltpu.CompilerParams(vmem_limit_bytes=2 * MIB),
             name="collect",
-        )(*msgs, *after)
-
-    near, far = collect(mine[: blocks // 2]), collect(mine[blocks // 2 :], done)
+        )(*msgs)
+
+    near, far = collect(mine[: blocks // 2]), collect(mine[blocks // 2 :])
     other_near, other_far = swap(near, 1), swap(far, 1)
 
     keys = pl.pallas_call(
@@ -376,16 +326,13 @@
             flops=2 * blocks * prefix * width * model_width, bytes_accessed=4 * width * model_width, transcendentals=0
         ),
         name="keys",
-    )(*mine, weight, bias)
-
-    hidden, head_last = pl.pallas_call(
+    )(*mine, in_vmem(proj_weight), in_vmem(proj_bias))
+
+    hidden = pl.pallas_call(
         functools.partial(hidden_kernel, order, prefix, cap_len),
-        out_shape=(
-            jax.ShapeDtypeStruct((row_total, model_width + LANES), jnp.bfloat16),
-            pltpu.VMEM((vocab - ahead, model_width), jnp.bfloat16),
-        ),
-        in_specs=[SMEM] + [VMEM] * 6 + [HBM],
-        out_specs=(VMEM, VMEM),
+        out_shape=jax.ShapeDtypeStruct((row_total, model_width + LANES), jnp.bfloat16),
+        in_specs=[SMEM] + [VMEM] * 6,
+        out_specs=VMEM,
         scratch_shapes=[
             pltpu.VMEM((2 * blocks * held, width), jnp.bfloat16),
             pltpu.VMEM((row_total, model_width + LANES), jnp.bfloat16),
@@ -393,21 +340,20 @@
             pltpu.VMEM((heads * group * pair_rows, group * (prefix + pair_rows)), jnp.float32),
             pltpu.VMEM((score_tiles, heads * group * pair_rows, group * (prefix + pair_rows)), jnp.float32),
             pltpu.VMEM((score_tiles, heads * group * pair_rows, group * (prefix + pair_rows)), jnp.bfloat16),
-            pltpu.SemaphoreType.DMA((8,)),
         ],
-        compiler_params=pltpu.CompilerParams(vmem_limit_bytes=24 * MIB),
+        compiler_params=pltpu.CompilerParams(vmem_limit_bytes=16 * MIB),
         name="hidden",
-    )(position, near, far, other_near, other_far, keys, gain, head_weight)
+    )(position, near, far, other_near, other_far, keys, in_vmem(norm_gain.reshape(1, -1)))
 
     stats = pl.pallas_call(
         functools.partial(logits_kernel, order),
         out_shape=jax.ShapeDtypeStruct((shards, 1, LANES), jnp.float32),
-        in_specs=[SMEM] + [VMEM] * 5,
+        in_specs=[SMEM] + [VMEM] * 4,
         out_specs=VMEM,
         scratch_shapes=[pltpu.VMEM((2 * row_total, model_width), jnp.bfloat16)],
         compiler_params=pltpu.CompilerParams(vmem_limit_bytes=16 * MIB),
         name="logits",
-    )(position, hidden, swap(hidden, 1), head_first, head_last, length)
+    )(position, hidden, swap(hidden, 1), in_vmem(head_weight.T), length)
 
     stats = lax.all_to_all(stats, "dp", 0, 0, tiled=True)
     return pl.pallas_call(

time: 43.8 us -> 42.9 us (0.979)
  Pallas kernels: 17.9 us -> 11.3 us
  waiting for transfers between devices: 2.3 us -> 8.01 us
    pallas_call x4 -> x3, Pallas kernels: 6.38 us -> 0.03 us  [the longest x2 0.03 us: collect(): pl.pallas_call(collect_kernel, out_shape=jax.ShapeDtypeStruct((len(msgs)...]
    ppermute x10, waiting for transfers between devices: 2.3 us -> 8.01 us  [swap(): return lax.ppermute(a, 'dp', [(i, i ^ away) for i in range(shards)])]
  transfers between devices with their start and end apart: 10 -> 10, of which waited for: 3 -> 5; matrix products, arithmetic and copies ran while one was open for 0% -> 0% of each run, Pallas kernels for 19% -> 4%
where the time goes in v6:
time: 42.9 us; the launch traced here: 42.7 us
  starting transfers between devices  11.4 us (27%)
  Pallas kernels  11.3 us (26%)
  blocking collectives  11.1 us (26%)
  waiting for transfers between devices  8.01 us (19%)
  between operations  0.83 us (2%)
    ppermute x10, starting transfers between devices, swap(): return lax.ppermute(a, 'dp', [(i, i ^ away) for i in range(shards)])  11.4 us
    all_to_all x1, blocking collectives, paired(): stats = lax.all_to_all(stats, 'dp', 0, 0, tiled=True)  11.1 us
    ppermute x10, waiting for transfers between devices, swap(): return lax.ppermute(a, 'dp', [(i, i ^ away) for i in range(shards)])  8.01 us
    pallas_call x1, Pallas kernels, paired(): pl.pallas_call(functools.partial(logits_kernel, order), out_shape=jax.Sha...  4.67 us
    pallas_call x1, Pallas kernels, paired(): pl.pallas_call(functools.partial(hidden_kernel, order, prefix, cap_len),...  3.16 us
    pallas_call x1, Pallas kernels, paired(): pl.pallas_call(functools.partial(keys_kernel, blocks), out_shape=pltpu.VM...  1.84 us
    pallas_call x1, Pallas kernels, paired(): pl.pallas_call(pack_kernel, out_shape=jax.ShapeDtypeStruct((piece_rows +...  0.88 us
  transfers between devices with their start and end apart: 10, of which 5 were waited for; matrix products, arithmetic and copies ran while one was open for 0% of the time, Pallas kernels for 4%

profile of v6, /device:TPU:0, one launch (start us, length us, event | category | flops | bytes accessed | tf_op | source)
XLA Modules:
  0.0 42.7 jit_solution(5874492003950150129)
XLA Ops:
  0.0 0.9 %pack.1.refs_0_ = bf16[56,768]{1,0:T(8,128)(2,1)S(1)} custom-call(s32[1,2]{1,0:T(1,128)} %cand_hbm.1, s32[1,4]{1,0:T(1,128)} %ids_hbm.1, bf16[1,32,768]{2,1,0:T(8,128)(2,1)} %rows_hbm.1, bf16[1,4,4096]{2,1,0:T(4,128)(2,1)} %states_hbm.1), custom_call_target="tpu_custom_call" | custom-call | tf_op jit(solution)/shard_map/pack/pallas_call | solution.py:270
  0.9 3.1 %collective-permute-start.2 = (bf16[56,768]{1,0:T(8,128)(2,1)S(1)}, bf16[56,768]{1,0:T(8,128)(2,1)S(1)}, u32[]{:S(2)}, u32[]{:S(2)}) collective-permute-start(bf16[56,768]{1,0:T(8,128)(2,1)S(1)} %pack.1.refs_0_), channel_id=1, source_target_pairs={{0,4},{1,5},{2,6},{3,7},{4,0},{5,1},{6,2},{7,3},{8,12},{9,13},{10,... | collective-permute-start | bytes 258056 | tf_op jit(solution)/shard_map/ppermute | solution.py:268
  4.0 2.5 %collective-permute-start.4 = (bf16[56,768]{1,0:T(8,128)(2,1)S(1)}, bf16[56,768]{1,0:T(8,128)(2,1)S(1)}, u32[]{:S(2)}, u32[]{:S(2)}) collective-permute-start(bf16[56,768]{1,0:T(8,128)(2,1)S(1)} %pack.1.refs_0_), channel_id=1, source_target_pairs={{0,12},{1,13},{2,14},{3,15},{4,8},{5,9},{6,10},{7,11},{8,4},{9,5},... | collective-permute-start | bytes 258056 | tf_op jit(solution)/shard_map/ppermute | solution.py:268
  6.5 0.1 collective-permute-start
  6.6 1.5 %collective-permute-start.1 = (bf16[56,768]{1,0:T(8,128)(2,1)S(1)}, bf16[56,768]{1,0:T(8,128)(2,1)S(1)}, u32[]{:S(2)}, u32[]{:S(2)}) collective-permute-start(bf16[56,768]{1,0:T(8,128)(2,1)S(1)} %pack.1.refs_0_), channel_id=1, source_target_pairs={{0,2},{1,3},{2,0},{3,1},{4,6},{5,7},{6,4},{7,5},{8,10},{9,11},{10,... | collective-permute-start | bytes 258056 | tf_op jit(solution)/shard_map/ppermute | solution.py:268
  8.1 0.0 collective-permute-done.2.refs_2_
  8.1 0.5 %collective-permute-start.3 = (bf16[56,768]{1,0:T(8,128)(2,1)S(1)}, bf16[56,768]{1,0:T(8,128)(2,1)S(1)}, u32[]{:S(2)}, u32[]{:S(2)}) collective-permute-start(bf16[56,768]{1,0:T(8,128)(2,1)S(1)} %collective-permute-done.2.refs_2_), channel_id=1, source_target_pairs={{0,2},{1,3},{2,0},{3,1},{4,6},{5,7},{6,4},{7,5},{8,10},{9,11},{10,... | collective-permute-start | bytes 258056 | tf_op jit(solution)/shard_map/ppermute | solution.py:268
  9.2 0.0 copy-start
  9.3 0.0 copy-start.2
  9.3 0.0 slice-start
  9.3 0.0 slice-start.1
  9.3 0.0 slice-start.2
  9.3 0.0 copy-start.1
  9.3 0.0 slice-start.3
  9.3 2.4 %collective-permute-done.4.refs_1_.refs_5_ = bf16[56,768]{1,0:T(8,128)(2,1)S(1)} collective-permute-done((bf16[56,768]{1,0:T(8,128)(2,1)S(1)}, bf16[56,768]{1,0:T(8,128)(2,1)S(1)}, u32[]{:S(2)}, u32[]{:S(2)}) %collective-permute-start.4) | collective-permute-done | bytes 86048 | tf_op jit(solution)/shard_map/ppermute | solution.py:268
  11.7 1.5 %collective-permute-start.6 = (bf16[56,768]{1,0:T(8,128)(2,1)S(1)}, bf16[56,768]{1,0:T(8,128)(2,1)S(1)}, u32[]{:S(2)}, u32[]{:S(2)}) collective-permute-start(bf16[56,768]{1,0:T(8,128)(2,1)S(1)} %collective-permute-done.4.refs_1_.refs_5_), channel_id=1, source_target_pairs={{0,2},{1,3},{2,0},{3,1},{4,6},{5,7},{6,4},{7,5},{8,10},{9,11},{10,... | collective-permute-start | bytes 258056 | tf_op jit(solution)/shard_map/ppermute | solution.py:268
  13.2 1.2 %collective-permute-done.refs_0_.refs_4_ = bf16[56,768]{1,0:T(8,128)(2,1)S(1)} collective-permute-done((bf16[56,768]{1,0:T(8,128)(2,1)S(1)}, bf16[56,768]{1,0:T(8,128)(2,1)S(1)}, u32[]{:S(2)}, u32[]{:S(2)}) %collective-permute-start) | collective-permute-done | bytes 86048 | tf_op jit(solution)/shard_map/ppermute | solution.py:268
  14.4 0.0 collective-permute-done.1.refs_1_
  14.4 0.0 collective-permute-done.3.refs_3_
  14.4 1.5 %collective-permute-start.5 = (bf16[56,768]{1,0:T(8,128)(2,1)S(1)}, bf16[56,768]{1,0:T(8,128)(2,1)S(1)}, u32[]{:S(2)}, u32[]{:S(2)}) collective-permute-start(bf16[56,768]{1,0:T(8,128)(2,1)S(1)} %collective-permute-done.refs_0_.refs_4_), channel_id=1, source_target_pairs={{0,2},{1,3},{2,0},{3,1},{4,6},{5,7},{6,4},{7,5},{8,10},{9,11},{10,... | collective-permute-start | bytes 258056 | tf_op jit(solution)/shard_map/ppermute | solution.py:268
  16.0 0.1 collective-permute-start.7
  16.1 0.1 collective-permute-done.6.refs_3_.refs_7_
  16.2 2.7 %collective-permute-done.5.refs_2_.refs_6_ = bf16[56,768]{1,0:T(8,128)(2,1)S(1)} collective-permute-done((bf16[56,768]{1,0:T(8,128)(2,1)S(1)}, bf16[56,768]{1,0:T(8,128)(2,1)S(1)}, u32[]{:S(2)}, u32[]{:S(2)}) %collective-permute-start.5) | collective-permute-done | bytes 86048 | tf_op jit(solution)/shard_map/ppermute | solution.py:268
  18.9 0.1 collective-permute-start.8
  19.0 1.8 %keys.1.refs_5_ = bf16[256,4096]{1,0:T(8,128)(2,1)S(1)} custom-call(bf16[56,768]{1,0:T(8,128)(2,1)S(1)} %pack.1.refs_0_, bf16[56,768]{1,0:T(8,128)(2,1)S(1)} %collective-permute-done.1.refs_1_, bf16[56,768]{1,0:T(8,128)(2,1)S(1)} %collective-permute-done.2.refs_2_, bf16[56,768]{1,0:T(8,128)(2,1)S(1)} %collective-permute-done.3.refs_3_, ...), custom_call_target="tpu_custom_call" | custom-call | flops 1610612736 | bytes 12582912 | tf_op jit(solution)/shard_map/keys/pallas_call | solution.py:318
  20.9 0.0 collective-permute-done.8.refs_4_
  20.9 3.2 %hidden.1.mine_ref = bf16[64,4224]{1,0:T(8,128)(2,1)S(1)} custom-call(s32[1]{0:T(128)} %bitcast.pos_ref.refs_0_, bf16[128,768]{1,0:T(8,128)(2,1)S(1)} %collect.2.refs_1_, bf16[128,768]{1,0:T(8,128)(2,1)S(1)} %collect.3.refs_2_, bf16[128,768]{1,0:T(8,128)(2,1)S(1)} %collective-permute-done.7.refs_3_, bf16[128,768]{1,0:T(8,128)(2,1)S(1)} %collective-permute-done.8.refs_4_, ...), custom_call_target="tpu_custom_call" | custom-call | tf_op jit(solution)/shard_map/hidden/pallas_call | solution.py:331
  24.1 0.5 %collective-permute-start.9 = (bf16[64,4224]{1,0:T(8,128)(2,1)S(1)}, bf16[64,4224]{1,0:T(8,128)(2,1)S(1)}, u32[]{:S(2)}, u32[]{:S(2)}) collective-permute-start(bf16[64,4224]{1,0:T(8,128)(2,1)S(1)} %hidden.1.mine_ref), channel_id=1, source_target_pairs={{0,1},{1,0},{2,3},{3,2},{4,5},{5,4},{6,7},{7,6},{8,9},{9,8},{10,11... | collective-permute-start | bytes 1622024 | tf_op jit(solution)/shard_map/ppermute | solution.py:268
  24.6 1.6 %collective-permute-done.9.other_ref = bf16[64,4224]{1,0:T(8,128)(2,1)S(1)} collective-permute-done((bf16[64,4224]{1,0:T(8,128)(2,1)S(1)}, bf16[64,4224]{1,0:T(8,128)(2,1)S(1)}, u32[]{:S(2)}, u32[]{:S(2)}) %collective-permute-start.9) | collective-permute-done | bytes 540704 | tf_op jit(solution)/shard_map/ppermute | solution.py:268
  26.2 4.7 %logits.1 = f32[16,1,128]{2,1,0:T(1,128)S(1)} custom-call(s32[1]{0:T(128)} %bitcast.pos_ref.refs_0_, bf16[64,4224]{1,0:T(8,128)(2,1)S(1)} %hidden.1.mine_ref, bf16[64,4224]{1,0:T(8,128)(2,1)S(1)} %collective-permute-done.9.other_ref, bf16[2008,4096]{1,0:T(8,128)(2,1)S(1)} %bitcast.7, f32[1,128]{1,0:T(1,128)S(1)} %length.1.length_ref), custom_call_target="tpu_custom_call" | custom-call | tf_op jit(solution)/shard_map/logits/pallas_call | solution.py:348
  30.9 11.1 %all_to_all.5.stats_ref = f32[16,1,128]{2,1,0:T(1,128)S(1)} all-to-all(f32[16,1,128]{2,1,0:T(1,128)S(1)} %logits.1), channel_id=1, replica_groups=mesh['groups'=2,'dp'=16] {'dp'}, dimensions={0} | all-to-all | bytes 16384 | tf_op jit(solution)/shard_map/all_to_all | solution.py:358
  42.0 0.7 %finish.1 = f32[1,2,4]{2,1,0:T(2,128)} custom-call(f32[16,1,128]{2,1,0:T(1,128)S(1)} %all_to_all.5.stats_ref, bf16[64,4224]{1,0:T(8,128)(2,1)S(1)} %hidden.1.mine_ref), custom_call_target="tpu_custom_call" | custom-call | tf_op jit(solution)/shard_map/finish/pallas_call | solution.py:359
  (12 shorter events, 0.1 us)
Async XLA Ops:
  0.9 7.2 %collective-permute-start.2 = (bf16[56,768]{1,0:T(8,128)(2,1)S(1)}, bf16[56,768]{1,0:T(8,128)(2,1)S(1)}, u32[]{:S(2)}, u32[]{:S(2)}) collective-permute-start(bf16[56,768]{1,0:T(8,128)(2,1)S(1)} %pack.1.refs_0_), channel_id=1, source_target_pairs={{0,4},{1,5},{2,6},{3,7},{4,0},{5,1},{6,2},{7,3},{8,12},{9,13},{10,... | collective-permute-start | bytes 258056 | tf_op jit(solution)/shard_map/ppermute | solution.py:268
  4.0 7.7 %collective-permute-start.4 = (bf16[56,768]{1,0:T(8,128)(2,1)S(1)}, bf16[56,768]{1,0:T(8,128)(2,1)S(1)}, u32[]{:S(2)}, u32[]{:S(2)}) collective-permute-start(bf16[56,768]{1,0:T(8,128)(2,1)S(1)} %pack.1.refs_0_), channel_id=1, source_target_pairs={{0,12},{1,13},{2,14},{3,15},{4,8},{5,9},{6,10},{7,11},{8,4},{9,5},... | collective-permute-start | bytes 258056 | tf_op jit(solution)/shard_map/ppermute | solution.py:268
  6.5 8.0 %collective-permute-start = (bf16[56,768]{1,0:T(8,128)(2,1)S(1)}, bf16[56,768]{1,0:T(8,128)(2,1)S(1)}, u32[]{:S(2)}, u32[]{:S(2)}) collective-permute-start(bf16[56,768]{1,0:T(8,128)(2,1)S(1)} %pack.1.refs_0_), channel_id=1, source_target_pairs={{0,8},{1,9},{2,10},{3,11},{4,12},{5,13},{6,14},{7,15},{8,0},{9,1},... | collective-permute-start | bytes 258056 | tf_op jit(solution)/shard_map/ppermute | solution.py:268
  6.6 7.9 %collective-permute-start.1 = (bf16[56,768]{1,0:T(8,128)(2,1)S(1)}, bf16[56,768]{1,0:T(8,128)(2,1)S(1)}, u32[]{:S(2)}, u32[]{:S(2)}) collective-permute-start(bf16[56,768]{1,0:T(8,128)(2,1)S(1)} %pack.1.refs_0_), channel_id=1, source_target_pairs={{0,2},{1,3},{2,0},{3,1},{4,6},{5,7},{6,4},{7,5},{8,10},{9,11},{10,... | collective-permute-start | bytes 258056 | tf_op jit(solution)/shard_map/ppermute | solution.py:268
  8.1 6.3 %collective-permute-start.3 = (bf16[56,768]{1,0:T(8,128)(2,1)S(1)}, bf16[56,768]{1,0:T(8,128)(2,1)S(1)}, u32[]{:S(2)}, u32[]{:S(2)}) collective-permute-start(bf16[56,768]{1,0:T(8,128)(2,1)S(1)} %collective-permute-done.2.refs_2_), channel_id=1, source_target_pairs={{0,2},{1,3},{2,0},{3,1},{4,6},{5,7},{6,4},{7,5},{8,10},{9,11},{10,... | collective-permute-start | bytes 258056 | tf_op jit(solution)/shard_map/ppermute | solution.py:268
  9.2 9.8 %copy-start = (bf16[768,4096]{1,0:T(8,128)(2,1)S(1)}, bf16[768,4096]{1,0:T(8,128)(2,1)}, u32[]{:S(2)}) copy-start(bf16[768,4096]{1,0:T(8,128)(2,1)} %refs_8_.1) | copy-start | bytes 18874372
  9.3 9.8 %copy-start.2 = (bf16[4096]{0:T(1024)(128)(2,1)S(1)}, bf16[4096]{0:T(1024)(128)(2,1)}, u32[]{:S(2)}) copy-start(bf16[4096]{0:T(1024)(128)(2,1)} %refs_9_.1) | copy-start | bytes 24580
  9.3 16.9 %slice-start = ((s8[16449536]{0:T(1024)(128)(4,1)}), s8[4194304]{0:T(1024)(128)(4,1)S(1)}, s32[]{:S(2)}) async-start(s8[16449536]{0:T(1024)(128)(4,1)} %bitcast.5), calls=%async_computation.1 | async-start | bytes 8388608
  9.3 16.9 %slice-start.1 = ((s8[16449536]{0:T(1024)(128)(4,1)}), s8[4194304]{0:T(1024)(128)(4,1)S(1)}, s32[]{:S(2)}) async-start(s8[16449536]{0:T(1024)(128)(4,1)} %bitcast.5), calls=%async_computation.2 | async-start | bytes 8388608
  9.3 16.9 %slice-start.2 = ((s8[16449536]{0:T(1024)(128)(4,1)}), s8[4194304]{0:T(1024)(128)(4,1)S(1)}, s32[]{:S(2)}) async-start(s8[16449536]{0:T(1024)(128)(4,1)} %bitcast.5), calls=%async_computation.3 | async-start | bytes 8388608
  9.3 11.6 %copy-start.1 = (f32[4096]{0:T(1024)S(1)}, f32[4096]{0:T(1024)}, u32[]{:S(2)}) copy-start(f32[4096]{0:T(1024)} %param.16) | copy-start | bytes 49156
  9.3 16.9 %slice-start.3 = ((s8[16449536]{0:T(1024)(128)(4,1)}), s8[3866624]{0:T(1024)(128)(4,1)S(1)}, s32[]{:S(2)}) async-start(s8[16449536]{0:T(1024)(128)(4,1)} %bitcast.5), calls=%async_computation.4 | async-start | bytes 7733248
  11.7 4.5 %collective-permute-start.6 = (bf16[56,768]{1,0:T(8,128)(2,1)S(1)}, bf16[56,768]{1,0:T(8,128)(2,1)S(1)}, u32[]{:S(2)}, u32[]{:S(2)}) collective-permute-start(bf16[56,768]{1,0:T(8,128)(2,1)S(1)} %collective-permute-done.4.refs_1_.refs_5_), channel_id=1, source_target_pairs={{0,2},{1,3},{2,0},{3,1},{4,6},{5,7},{6,4},{7,5},{8,10},{9,11},{10,... | collective-permute-start | bytes 258056 | tf_op jit(solution)/shard_map/ppermute | solution.py:268
  14.4 4.5 %collective-permute-start.5 = (bf16[56,768]{1,0:T(8,128)(2,1)S(1)}, bf16[56,768]{1,0:T(8,128)(2,1)S(1)}, u32[]{:S(2)}, u32[]{:S(2)}) collective-permute-start(bf16[56,768]{1,0:T(8,128)(2,1)S(1)} %collective-permute-done.refs_0_.refs_4_), channel_id=1, source_target_pairs={{0,2},{1,3},{2,0},{3,1},{4,6},{5,7},{6,4},{7,5},{8,10},{9,11},{10,... | collective-permute-start | bytes 258056 | tf_op jit(solution)/shard_map/ppermute | solution.py:268
  16.0 4.9 %collective-permute-start.7 = (bf16[128,768]{1,0:T(8,128)(2,1)S(1)}, bf16[128,768]{1,0:T(8,128)(2,1)S(1)}, u32[]{:S(2)}, u32[]{:S(2)}) collective-permute-start(bf16[128,768]{1,0:T(8,128)(2,1)S(1)} %collect.2.refs_1_), channel_id=1, source_target_pairs={{0,1},{1,0},{2,3},{3,2},{4,5},{5,4},{6,7},{7,6},{8,9},{9,8},{10,11... | collective-permute-start | bytes 589832 | tf_op jit(solution)/shard_map/ppermute | solution.py:268
  18.9 2.0 %collective-permute-start.8 = (bf16[128,768]{1,0:T(8,128)(2,1)S(1)}, bf16[128,768]{1,0:T(8,128)(2,1)S(1)}, u32[]{:S(2)}, u32[]{:S(2)}) collective-permute-start(bf16[128,768]{1,0:T(8,128)(2,1)S(1)} %collect.3.refs_2_), channel_id=1, source_target_pairs={{0,1},{1,0},{2,3},{3,2},{4,5},{5,4},{6,7},{7,6},{8,9},{9,8},{10,11... | collective-permute-start | bytes 589832 | tf_op jit(solution)/shard_map/ppermute | solution.py:268
  24.1 2.1 %collective-permute-start.9 = (bf16[64,4224]{1,0:T(8,128)(2,1)S(1)}, bf16[64,4224]{1,0:T(8,128)(2,1)S(1)}, u32[]{:S(2)}, u32[]{:S(2)}) collective-permute-start(bf16[64,4224]{1,0:T(8,128)(2,1)S(1)} %hidden.1.mine_ref), channel_id=1, source_target_pairs={{0,1},{1,0},{2,3},{3,2},{4,5},{5,4},{6,7},{7,6},{8,9},{9,8},{10,11... | collective-permute-start | bytes 1622024 | tf_op jit(solution)/shard_map/ppermute | solution.py:268

commit v7 on v6

--- a/solution.py
+++ b/solution.py
@@ -285,7 +285,7 @@
     )(*(in_hbm(a) for a in (candidates, caption_ids, query_rows, caption_states)))
 
     got = {0: message}
-    for away in (12, 8, 4, 2):
+    for away in (12, 2, 4):
         got[away] = swap(message, away)
     length = pl.pallas_call(
         length_kernel,
@@ -295,11 +295,11 @@
         compiler_params=pltpu.CompilerParams(vmem_limit_bytes=MIB),
         name="length",
     )(position, caption_lengths, in_hbm(head_weight.T), in_hbm(head_weight.T), in_hbm(proj_weight))
-    got[6] = swap(got[4], 2)
-    got[14] = swap(got[12], 2)
-    got[8], got[2], got[6], length = lax.optimization_barrier((got[8], got[2], got[6], length))
-    got[10] = swap(got[8], 2)
-    order = (0, 2, 4, 6, 8, 12, 10, 14)
+    got[10] = swap(message, 10)
+    got[6] = swap(message, 6)
+    got[12], length = lax.optimization_barrier((got[12], length))
+    got[8], got[14] = swap(got[12], 4), swap(got[12], 2)
+    order = (0, 2, 4, 12, 10, 6, 8, 14)
     mine = [got[away] for away in order]
 
     def collect(msgs):

time: 42.9 us -> 40.7 us (0.949)
  waiting for transfers between devices: 8.01 us -> 5.34 us
  starting transfers between devices: 11.4 us -> 12.2 us
    ppermute x10, waiting for transfers between devices: 8.01 us -> 5.34 us  [swap(): return lax.ppermute(a, 'dp', [(i, i ^ away) for i in range(shards)])]
    ppermute x10, starting transfers between devices: 11.4 us -> 12.2 us  [swap(): return lax.ppermute(a, 'dp', [(i, i ^ away) for i in range(shards)])]
  transfers between devices with their start and end apart: 10 -> 10, of which waited for: 5 -> 6; matrix products, arithmetic and copies ran while one was open for 0% -> 0% of each run, Pallas kernels for 4% -> 5%
where the time goes in v7:
time: 40.7 us; the launch traced here: 40.4 us
  starting transfers between devices  12.2 us (30%)
  Pallas kernels  11.3 us (28%)
  blocking collectives  10.7 us (26%)
  waiting for transfers between devices  5.34 us (13%)
  between operations  0.84 us (2%)
    ppermute x10, starting transfers between devices, swap(): return lax.ppermute(a, 'dp', [(i, i ^ away) for i in range(shards)])  12.2 us
    all_to_all x1, blocking collectives, paired(): stats = lax.all_to_all(stats, 'dp', 0, 0, tiled=True)  10.7 us
    ppermute x10, waiting for transfers between devices, swap(): return lax.ppermute(a, 'dp', [(i, i ^ away) for i in range(shards)])  5.34 us
    pallas_call x1, Pallas kernels, paired(): pl.pallas_call(functools.partial(logits_kernel, order), out_shape=jax.Sha...  4.67 us
    pallas_call x1, Pallas kernels, paired(): pl.pallas_call(functools.partial(hidden_kernel, order, prefix, cap_len),...  3.16 us
    pallas_call x1, Pallas kernels, paired(): pl.pallas_call(functools.partial(keys_kernel, blocks), out_shape=pltpu.VM...  1.85 us
    pallas_call x1, Pallas kernels, paired(): pl.pallas_call(pack_kernel, out_shape=jax.ShapeDtypeStruct((piece_rows +...  0.88 us
  transfers between devices with their start and end apart: 10, of which 6 were waited for; matrix products, arithmetic and copies ran while one was open for 0% of the time, Pallas kernels for 5%

profile of v7, /device:TPU:0, one launch (start us, length us, event | category | flops | bytes accessed | tf_op | source)
XLA Modules:
  0.0 40.4 jit_solution(2240360473028284638)
XLA Ops:
  0.0 0.9 %pack.1.refs_0_ = bf16[56,768]{1,0:T(8,128)(2,1)S(1)} custom-call(s32[1,2]{1,0:T(1,128)} %cand_hbm.1, s32[1,4]{1,0:T(1,128)} %ids_hbm.1, bf16[1,32,768]{2,1,0:T(8,128)(2,1)} %rows_hbm.1, bf16[1,4,4096]{2,1,0:T(4,128)(2,1)} %states_hbm.1), custom_call_target="tpu_custom_call" | custom-call | tf_op jit(solution)/shard_map/pack/pallas_call | solution.py:270
  0.9 5.1 %collective-permute-start.2 = (bf16[56,768]{1,0:T(8,128)(2,1)S(1)}, bf16[56,768]{1,0:T(8,128)(2,1)S(1)}, u32[]{:S(2)}, u32[]{:S(2)}) collective-permute-start(bf16[56,768]{1,0:T(8,128)(2,1)S(1)} %pack.1.refs_0_), channel_id=1, source_target_pairs={{0,12},{1,13},{2,14},{3,15},{4,8},{5,9},{6,10},{7,11},{8,4},{9,5},... | collective-permute-start | bytes 258056 | tf_op jit(solution)/shard_map/ppermute | solution.py:268
  6.0 1.5 %collective-permute-start = (bf16[56,768]{1,0:T(8,128)(2,1)S(1)}, bf16[56,768]{1,0:T(8,128)(2,1)S(1)}, u32[]{:S(2)}, u32[]{:S(2)}) collective-permute-start(bf16[56,768]{1,0:T(8,128)(2,1)S(1)} %pack.1.refs_0_), channel_id=1, source_target_pairs={{0,2},{1,3},{2,0},{3,1},{4,6},{5,7},{6,4},{7,5},{8,10},{9,11},{10,... | collective-permute-start | bytes 258056 | tf_op jit(solution)/shard_map/ppermute | solution.py:268
  7.5 0.0 collective-permute-start.1
  7.5 0.6 %collective-permute-start.3 = (bf16[56,768]{1,0:T(8,128)(2,1)S(1)}, bf16[56,768]{1,0:T(8,128)(2,1)S(1)}, u32[]{:S(2)}, u32[]{:S(2)}) collective-permute-start(bf16[56,768]{1,0:T(8,128)(2,1)S(1)} %pack.1.refs_0_), channel_id=1, source_target_pairs={{0,10},{1,11},{2,8},{3,9},{4,14},{5,15},{6,12},{7,13},{8,2},{9,3},... | collective-permute-start | bytes 258056 | tf_op jit(solution)/shard_map/ppermute | solution.py:268
  8.1 1.8 %collective-permute-start.4 = (bf16[56,768]{1,0:T(8,128)(2,1)S(1)}, bf16[56,768]{1,0:T(8,128)(2,1)S(1)}, u32[]{:S(2)}, u32[]{:S(2)}) collective-permute-start(bf16[56,768]{1,0:T(8,128)(2,1)S(1)} %pack.1.refs_0_), channel_id=1, source_target_pairs={{0,6},{1,7},{2,4},{3,5},{4,2},{5,3},{6,0},{7,1},{8,14},{9,15},{10,... | collective-permute-start | bytes 258056 | tf_op jit(solution)/shard_map/ppermute | solution.py:268
  10.5 0.0 copy-start
  10.5 0.0 copy-start.2
  10.6 0.0 slice-start
  10.6 0.0 slice-start.1
  10.6 0.0 slice-start.2
  10.6 0.0 copy-start.1
  10.6 0.0 slice-start.3
  10.6 0.0 collective-permute-done.2.refs_3_
  10.6 1.4 %collective-permute-start.5 = (bf16[56,768]{1,0:T(8,128)(2,1)S(1)}, bf16[56,768]{1,0:T(8,128)(2,1)S(1)}, u32[]{:S(2)}, u32[]{:S(2)}) collective-permute-start(bf16[56,768]{1,0:T(8,128)(2,1)S(1)} %collective-permute-done.2.refs_3_), channel_id=1, source_target_pairs={{0,4},{1,5},{2,6},{3,7},{4,0},{5,1},{6,2},{7,3},{8,12},{9,13},{10,... | collective-permute-start | bytes 258056 | tf_op jit(solution)/shard_map/ppermute | solution.py:268
  12.1 0.0 collective-permute-done.refs_1_
  12.1 1.1 %collective-permute-start.6 = (bf16[56,768]{1,0:T(8,128)(2,1)S(1)}, bf16[56,768]{1,0:T(8,128)(2,1)S(1)}, u32[]{:S(2)}, u32[]{:S(2)}) collective-permute-start(bf16[56,768]{1,0:T(8,128)(2,1)S(1)} %collective-permute-done.2.refs_3_), channel_id=1, source_target_pairs={{0,2},{1,3},{2,0},{3,1},{4,6},{5,7},{6,4},{7,5},{8,10},{9,11},{10,... | collective-permute-start | bytes 258056 | tf_op jit(solution)/shard_map/ppermute | solution.py:268
  13.2 0.8 %collective-permute-done.1.refs_2_ = bf16[56,768]{1,0:T(8,128)(2,1)S(1)} collective-permute-done((bf16[56,768]{1,0:T(8,128)(2,1)S(1)}, bf16[56,768]{1,0:T(8,128)(2,1)S(1)}, u32[]{:S(2)}, u32[]{:S(2)}) %collective-permute-start.1) | collective-permute-done | bytes 86048 | tf_op jit(solution)/shard_map/ppermute | solution.py:268
  14.0 0.1 collective-permute-start.7
  14.1 0.3 collective-permute-done.3.refs_0_.refs_4_
  14.4 2.1 %collective-permute-done.4.refs_1_.refs_5_ = bf16[56,768]{1,0:T(8,128)(2,1)S(1)} collective-permute-done((bf16[56,768]{1,0:T(8,128)(2,1)S(1)}, bf16[56,768]{1,0:T(8,128)(2,1)S(1)}, u32[]{:S(2)}, u32[]{:S(2)}) %collective-permute-start.4) | collective-permute-done | bytes 86048 | tf_op jit(solution)/shard_map/ppermute | solution.py:268
  16.4 0.3 collective-permute-done.5.refs_2_.refs_6_
  16.8 0.3 collective-permute-done.6.refs_3_.refs_7_
  17.1 0.1 collective-permute-start.8
  17.2 1.8 %keys.1.refs_5_ = bf16[256,4096]{1,0:T(8,128)(2,1)S(1)} custom-call(bf16[56,768]{1,0:T(8,128)(2,1)S(1)} %pack.1.refs_0_, bf16[56,768]{1,0:T(8,128)(2,1)S(1)} %collective-permute-done.refs_1_, bf16[56,768]{1,0:T(8,128)(2,1)S(1)} %collective-permute-done.1.refs_2_, bf16[56,768]{1,0:T(8,128)(2,1)S(1)} %collective-permute-done.2.refs_3_, ...), custom_call_target="tpu_custom_call" | custom-call | flops 1610612736 | bytes 12582912 | tf_op jit(solution)/shard_map/keys/pallas_call | solution.py:318
  19.0 0.0 collective-permute-done.8.refs_4_
  19.1 3.2 %hidden.1.mine_ref = bf16[64,4224]{1,0:T(8,128)(2,1)S(1)} custom-call(s32[1]{0:T(128)} %bitcast.pos_ref.refs_0_, bf16[128,768]{1,0:T(8,128)(2,1)S(1)} %collect.2.refs_1_, bf16[128,768]{1,0:T(8,128)(2,1)S(1)} %collect.3.refs_2_, bf16[128,768]{1,0:T(8,128)(2,1)S(1)} %collective-permute-done.7.refs_3_, bf16[128,768]{1,0:T(8,128)(2,1)S(1)} %collective-permute-done.8.refs_4_, ...), custom_call_target="tpu_custom_call" | custom-call | tf_op jit(solution)/shard_map/hidden/pallas_call | solution.py:331
  22.2 0.5 %collective-permute-start.9 = (bf16[64,4224]{1,0:T(8,128)(2,1)S(1)}, bf16[64,4224]{1,0:T(8,128)(2,1)S(1)}, u32[]{:S(2)}, u32[]{:S(2)}) collective-permute-start(bf16[64,4224]{1,0:T(8,128)(2,1)S(1)} %hidden.1.mine_ref), channel_id=1, source_target_pairs={{0,1},{1,0},{2,3},{3,2},{4,5},{5,4},{6,7},{7,6},{8,9},{9,8},{10,11... | collective-permute-start | bytes 1622024 | tf_op jit(solution)/shard_map/ppermute | solution.py:268
  22.8 1.6 %collective-permute-done.9.other_ref = bf16[64,4224]{1,0:T(8,128)(2,1)S(1)} collective-permute-done((bf16[64,4224]{1,0:T(8,128)(2,1)S(1)}, bf16[64,4224]{1,0:T(8,128)(2,1)S(1)}, u32[]{:S(2)}, u32[]{:S(2)}) %collective-permute-start.9) | collective-permute-done | bytes 540704 | tf_op jit(solution)/shard_map/ppermute | solution.py:268
  24.3 4.7 %logits.1 = f32[16,1,128]{2,1,0:T(1,128)S(1)} custom-call(s32[1]{0:T(128)} %bitcast.pos_ref.refs_0_, bf16[64,4224]{1,0:T(8,128)(2,1)S(1)} %hidden.1.mine_ref, bf16[64,4224]{1,0:T(8,128)(2,1)S(1)} %collective-permute-done.9.other_ref, bf16[2008,4096]{1,0:T(8,128)(2,1)S(1)} %bitcast.7, f32[1,128]{1,0:T(1,128)S(1)} %length.1.length_ref), custom_call_target="tpu_custom_call" | custom-call | tf_op jit(solution)/shard_map/logits/pallas_call | solution.py:348
  29.0 10.7 %all_to_all.5.stats_ref = f32[16,1,128]{2,1,0:T(1,128)S(1)} all-to-all(f32[16,1,128]{2,1,0:T(1,128)S(1)} %logits.1), channel_id=1, replica_groups=mesh['groups'=2,'dp'=16] {'dp'}, dimensions={0} | all-to-all | bytes 16384 | tf_op jit(solution)/shard_map/all_to_all | solution.py:358
  39.7 0.7 %finish.1 = f32[1,2,4]{2,1,0:T(2,128)} custom-call(f32[16,1,128]{2,1,0:T(1,128)S(1)} %all_to_all.5.stats_ref, bf16[64,4224]{1,0:T(8,128)(2,1)S(1)} %hidden.1.mine_ref), custom_call_target="tpu_custom_call" | custom-call | tf_op jit(solution)/shard_map/finish/pallas_call | solution.py:359
  (12 shorter events, 0.1 us)
Async XLA Ops:
  0.9 9.8 %collective-permute-start.2 = (bf16[56,768]{1,0:T(8,128)(2,1)S(1)}, bf16[56,768]{1,0:T(8,128)(2,1)S(1)}, u32[]{:S(2)}, u32[]{:S(2)}) collective-permute-start(bf16[56,768]{1,0:T(8,128)(2,1)S(1)} %pack.1.refs_0_), channel_id=1, source_target_pairs={{0,12},{1,13},{2,14},{3,15},{4,8},{5,9},{6,10},{7,11},{8,4},{9,5},... | collective-permute-start | bytes 258056 | tf_op jit(solution)/shard_map/ppermute | solution.py:268
  6.0 6.1 %collective-permute-start = (bf16[56,768]{1,0:T(8,128)(2,1)S(1)}, bf16[56,768]{1,0:T(8,128)(2,1)S(1)}, u32[]{:S(2)}, u32[]{:S(2)}) collective-permute-start(bf16[56,768]{1,0:T(8,128)(2,1)S(1)} %pack.1.refs_0_), channel_id=1, source_target_pairs={{0,2},{1,3},{2,0},{3,1},{4,6},{5,7},{6,4},{7,5},{8,10},{9,11},{10,... | collective-permute-start | bytes 258056 | tf_op jit(solution)/shard_map/ppermute | solution.py:268
  7.5 6.5 %collective-permute-start.1 = (bf16[56,768]{1,0:T(8,128)(2,1)S(1)}, bf16[56,768]{1,0:T(8,128)(2,1)S(1)}, u32[]{:S(2)}, u32[]{:S(2)}) collective-permute-start(bf16[56,768]{1,0:T(8,128)(2,1)S(1)} %pack.1.refs_0_), channel_id=1, source_target_pairs={{0,4},{1,5},{2,6},{3,7},{4,0},{5,1},{6,2},{7,3},{8,12},{9,13},{10,... | collective-permute-start | bytes 258056 | tf_op jit(solution)/shard_map/ppermute | solution.py:268
  7.5 6.8 %collective-permute-start.3 = (bf16[56,768]{1,0:T(8,128)(2,1)S(1)}, bf16[56,768]{1,0:T(8,128)(2,1)S(1)}, u32[]{:S(2)}, u32[]{:S(2)}) collective-permute-start(bf16[56,768]{1,0:T(8,128)(2,1)S(1)} %pack.1.refs_0_), channel_id=1, source_target_pairs={{0,10},{1,11},{2,8},{3,9},{4,14},{5,15},{6,12},{7,13},{8,2},{9,3},... | collective-permute-start | bytes 258056 | tf_op jit(solution)/shard_map/ppermute | solution.py:268
  8.1 8.3 %collective-permute-start.4 = (bf16[56,768]{1,0:T(8,128)(2,1)S(1)}, bf16[56,768]{1,0:T(8,128)(2,1)S(1)}, u32[]{:S(2)}, u32[]{:S(2)}) collective-permute-start(bf16[56,768]{1,0:T(8,128)(2,1)S(1)} %pack.1.refs_0_), channel_id=1, source_target_pairs={{0,6},{1,7},{2,4},{3,5},{4,2},{5,3},{6,0},{7,1},{8,14},{9,15},{10,... | collective-permute-start | bytes 258056 | tf_op jit(solution)/shard_map/ppermute | solution.py:268
  10.5 6.6 %copy-start = (bf16[768,4096]{1,0:T(8,128)(2,1)S(1)}, bf16[768,4096]{1,0:T(8,128)(2,1)}, u32[]{:S(2)}) copy-start(bf16[768,4096]{1,0:T(8,128)(2,1)} %refs_8_.1) | copy-start | bytes 18874372
  10.5 6.6 %copy-start.2 = (bf16[4096]{0:T(1024)(128)(2,1)S(1)}, bf16[4096]{0:T(1024)(128)(2,1)}, u32[]{:S(2)}) copy-start(bf16[4096]{0:T(1024)(128)(2,1)} %refs_9_.1) | copy-start | bytes 24580
  10.6 13.8 %slice-start = ((s8[16449536]{0:T(1024)(128)(4,1)}), s8[4194304]{0:T(1024)(128)(4,1)S(1)}, s32[]{:S(2)}) async-start(s8[16449536]{0:T(1024)(128)(4,1)} %bitcast.5), calls=%async_computation.1 | async-start | bytes 8388608
  10.6 13.7 %slice-start.1 = ((s8[16449536]{0:T(1024)(128)(4,1)}), s8[4194304]{0:T(1024)(128)(4,1)S(1)}, s32[]{:S(2)}) async-start(s8[16449536]{0:T(1024)(128)(4,1)} %bitcast.5), calls=%async_computation.2 | async-start | bytes 8388608
  10.6 13.7 %slice-start.2 = ((s8[16449536]{0:T(1024)(128)(4,1)}), s8[4194304]{0:T(1024)(128)(4,1)S(1)}, s32[]{:S(2)}) async-start(s8[16449536]{0:T(1024)(128)(4,1)} %bitcast.5), calls=%async_computation.3 | async-start | bytes 8388608
  10.6 8.4 %copy-start.1 = (f32[4096]{0:T(1024)S(1)}, f32[4096]{0:T(1024)}, u32[]{:S(2)}) copy-start(f32[4096]{0:T(1024)} %param.16) | copy-start | bytes 49156
  10.6 13.7 %slice-start.3 = ((s8[16449536]{0:T(1024)(128)(4,1)}), s8[3866624]{0:T(1024)(128)(4,1)S(1)}, s32[]{:S(2)}) async-start(s8[16449536]{0:T(1024)(128)(4,1)} %bitcast.5), calls=%async_computation.4 | async-start | bytes 7733248
  10.6 6.1 %collective-permute-start.5 = (bf16[56,768]{1,0:T(8,128)(2,1)S(1)}, bf16[56,768]{1,0:T(8,128)(2,1)S(1)}, u32[]{:S(2)}, u32[]{:S(2)}) collective-permute-start(bf16[56,768]{1,0:T(8,128)(2,1)S(1)} %collective-permute-done.2.refs_3_), channel_id=1, source_target_pairs={{0,4},{1,5},{2,6},{3,7},{4,0},{5,1},{6,2},{7,3},{8,12},{9,13},{10,... | collective-permute-start | bytes 258056 | tf_op jit(solution)/shard_map/ppermute | solution.py:268
  12.1 5.0 %collective-permute-start.6 = (bf16[56,768]{1,0:T(8,128)(2,1)S(1)}, bf16[56,768]{1,0:T(8,128)(2,1)S(1)}, u32[]{:S(2)}, u32[]{:S(2)}) collective-permute-start(bf16[56,768]{1,0:T(8,128)(2,1)S(1)} %collective-permute-done.2.refs_3_), channel_id=1, source_target_pairs={{0,2},{1,3},{2,0},{3,1},{4,6},{5,7},{6,4},{7,5},{8,10},{9,11},{10,... | collective-permute-start | bytes 258056 | tf_op jit(solution)/shard_map/ppermute | solution.py:268
  14.0 5.0 %collective-permute-start.7 = (bf16[128,768]{1,0:T(8,128)(2,1)S(1)}, bf16[128,768]{1,0:T(8,128)(2,1)S(1)}, u32[]{:S(2)}, u32[]{:S(2)}) collective-permute-start(bf16[128,768]{1,0:T(8,128)(2,1)S(1)} %collect.2.refs_1_), channel_id=1, source_target_pairs={{0,1},{1,0},{2,3},{3,2},{4,5},{5,4},{6,7},{7,6},{8,9},{9,8},{10,11... | collective-permute-start | bytes 589832 | tf_op jit(solution)/shard_map/ppermute | solution.py:268
  17.1 2.0 %collective-permute-start.8 = (bf16[128,768]{1,0:T(8,128)(2,1)S(1)}, bf16[128,768]{1,0:T(8,128)(2,1)S(1)}, u32[]{:S(2)}, u32[]{:S(2)}) collective-permute-start(bf16[128,768]{1,0:T(8,128)(2,1)S(1)} %collect.3.refs_2_), channel_id=1, source_target_pairs={{0,1},{1,0},{2,3},{3,2},{4,5},{5,4},{6,7},{7,6},{8,9},{9,8},{10,11... | collective-permute-start | bytes 589832 | tf_op jit(solution)/shard_map/ppermute | solution.py:268
  22.2 2.1 %collective-permute-start.9 = (bf16[64,4224]{1,0:T(8,128)(2,1)S(1)}, bf16[64,4224]{1,0:T(8,128)(2,1)S(1)}, u32[]{:S(2)}, u32[]{:S(2)}) collective-permute-start(bf16[64,4224]{1,0:T(8,128)(2,1)S(1)} %hidden.1.mine_ref), channel_id=1, source_target_pairs={{0,1},{1,0},{2,3},{3,2},{4,5},{5,4},{6,7},{7,6},{8,9},{9,8},{10,11... | collective-permute-start | bytes 1622024 | tf_op jit(solution)/shard_map/ppermute | solution.py:268

commit v8 on v7

--- a/solution.py
+++ b/solution.py
@@ -21,6 +21,7 @@
 VMEM = pl.BlockSpec(memory_space=pltpu.VMEM)
 SMEM = pl.BlockSpec(memory_space=pltpu.SMEM)
 HBM = pl.BlockSpec(memory_space=pltpu.HBM)
+ANY = pl.BlockSpec(memory_space=pl.ANY)
 ROWS_BY_ROWS = (((1,), (1,)), ((), ()))
 
 
@@ -88,9 +89,9 @@
     return [(i, min(total, i + piece)) for i in range(0, total, piece)]
 
 
-def collect_kernel(*refs):
-    *msgs, out_ref = refs
-    held = out_ref.shape[0] // len(msgs)
+def collect_kernel(count, *refs):
+    msgs, out_ref = refs[:count], refs[-1]
+    held = out_ref.shape[0] // count
     for i, msg in enumerate(msgs):
         out_ref[i * held : (i + 1) * held, :] = msg[0:held, :]
 
@@ -109,7 +110,7 @@
 
 def hidden_kernel(order, prefix, cap_len, *refs):
     pos_ref, *cap_refs = refs[:5]
-    keys, gain_ref, out_ref, caps, query, mixed, bias, scores, weights = refs[5:]
+    near_keys, far_keys, gain_ref, out_ref, caps, query, mixed, bias, scores, weights = refs[5:]
     blocks = len(order)
     width = caps.shape[1]
     model_width = mixed.shape[1]
@@ -164,7 +165,7 @@
 
     def keys_of(g, cols):
         q = query[g * group_rows : (g + 1) * group_rows, cols]
-        return q, jnp.concatenate([keys[g * image_keys : (g + 1) * image_keys, cols], q], 0)
+        return q, jnp.concatenate([(near_keys, far_keys)[g][:, cols], q], 0)
 
     for n, (g, cols) in enumerate(tiles):
         q, key = keys_of(g, cols)
@@ -299,39 +300,43 @@
     got[6] = swap(message, 6)
     got[12], length = lax.optimization_barrier((got[12], length))
     got[8], got[14] = swap(got[12], 4), swap(got[12], 2)
-    order = (0, 2, 4, 12, 10, 6, 8, 14)
+    order = (0, 2, 4, 12, 6, 10, 14, 8)
     mine = [got[away] for away in order]
 
-    def collect(msgs):
+    def collect(msgs, *after):
         return pl.pallas_call(
-            collect_kernel,
+            functools.partial(collect_kernel, len(msgs)),
             out_shape=jax.ShapeDtypeStruct((len(msgs) * held, width), jnp.bfloat16),
-            in_specs=[VMEM] * len(msgs),
+            in_specs=[VMEM] * len(msgs) + [ANY] * len(after),
             out_specs=VMEM,
             compiler_params=pltpu.CompilerParams(vmem_limit_bytes=2 * MIB),
             name="collect",
-        )(*msgs)
-
-    near, far = collect(mine[: blocks // 2]), collect(mine[blocks // 2 :])
+        )(*msgs, *after)
+
+
+    def keys_of(msgs):
+        rows = len(msgs) * prefix
+        return pl.pallas_call(
+            functools.partial(keys_kernel, len(msgs)),
+            out_shape=pltpu.VMEM((rows, model_width), jnp.bfloat16),
+            in_specs=[VMEM] * (len(msgs) + 2),
+            out_specs=VMEM,
+            scratch_shapes=[pltpu.VMEM((rows, width), jnp.bfloat16)],
+            compiler_params=pltpu.CompilerParams(vmem_limit_bytes=8 * MIB),
+            cost_estimate=pl.CostEstimate(
+                flops=2 * rows * width * model_width, bytes_accessed=4 * width * model_width, transcendentals=0
+            ),
+            name="keys",
+        )(*msgs, in_vmem(proj_weight), in_vmem(proj_bias))
+
+    near, near_keys = collect(mine[: blocks // 2]), keys_of(mine[: blocks // 2])
+    far, far_keys = collect(mine[blocks // 2 :], near_keys), keys_of(mine[blocks // 2 :])
     other_near, other_far = swap(near, 1), swap(far, 1)
-
-    keys = pl.pallas_call(
-        functools.partial(keys_kernel, blocks),
-        out_shape=pltpu.VMEM((blocks * prefix, model_width), jnp.bfloat16),
-        in_specs=[VMEM] * (blocks + 2),
-        out_specs=VMEM,
-        scratch_shapes=[pltpu.VMEM((blocks * prefix, width), jnp.bfloat16)],
-        compiler_params=pltpu.CompilerParams(vmem_limit_bytes=8 * MIB),
-        cost_estimate=pl.CostEstimate(
-            flops=2 * blocks * prefix * width * model_width, bytes_accessed=4 * width * model_width, transcendentals=0
-        ),
-        name="keys",
-    )(*mine, in_vmem(proj_weight), in_vmem(proj_bias))
 
     hidden = pl.pallas_call(
         functools.partial(hidden_kernel, order, prefix, cap_len),
         out_shape=jax.ShapeDtypeStruct((row_total, model_width + LANES), jnp.bfloat16),
-        in_specs=[SMEM] + [VMEM] * 6,
+        in_specs=[SMEM] + [VMEM] * 7,
         out_specs=VMEM,
         scratch_shapes=[
             pltpu.VMEM((2 * blocks * held, width), jnp.bfloat16),
@@ -343,7 +348,7 @@
         ],
         compiler_params=pltpu.CompilerParams(vmem_limit_bytes=16 * MIB),
         name="hidden",
-    )(position, near, far, other_near, other_far, keys, in_vmem(norm_gain.reshape(1, -1)))
+    )(position, near, far, other_near, other_far, near_keys, far_keys, in_vmem(norm_gain.reshape(1, -1)))
 
     stats = pl.pallas_call(
         functools.partial(logits_kernel, order),

time: 40.7 us -> 40.2 us (0.988)
  waiting for transfers between devices: 5.34 us -> 4.05 us
  starting transfers between devices: 12.2 us -> 12.7 us
    ppermute x10, waiting for transfers between devices: 5.34 us -> 4.05 us  [swap(): return lax.ppermute(a, 'dp', [(i, i ^ away) for i in range(shards)])]
    ppermute x10, starting transfers between devices: 12.2 us -> 12.7 us  [swap(): return lax.ppermute(a, 'dp', [(i, i ^ away) for i in range(shards)])]
    pallas_call x3 -> x4, Pallas kernels: 1.88 us -> 2.1 us  [the longest x2 2.07 us: keys_of(): pl.pallas_call(functools.partial(keys_kernel, len(msgs)), out_shape=pltpu...]
  transfers between devices with their start and end apart: 10 -> 10, of which waited for: 6 -> 4; matrix products, arithmetic and copies ran while one was open for 0% -> 0% of each run, Pallas kernels for 5% -> 5%
where the time goes in v8:
time: 40.2 us; the launch traced here: 40 us
  starting transfers between devices  12.7 us (32%)
  Pallas kernels  11.7 us (29%)
  blocking collectives  10.7 us (27%)
  waiting for transfers between devices  4.05 us (10%)
  between operations  0.84 us (2%)
    ppermute x10, starting transfers between devices, swap(): return lax.ppermute(a, 'dp', [(i, i ^ away) for i in range(shards)])  12.7 us
    all_to_all x1, blocking collectives, paired(): stats = lax.all_to_all(stats, 'dp', 0, 0, tiled=True)  10.7 us
    pallas_call x1, Pallas kernels, paired(): pl.pallas_call(functools.partial(logits_kernel, order), out_shape=jax.Sha...  4.67 us
    ppermute x10, waiting for transfers between devices, swap(): return lax.ppermute(a, 'dp', [(i, i ^ away) for i in range(shards)])  4.05 us
    pallas_call x1, Pallas kernels, paired(): pl.pallas_call(functools.partial(hidden_kernel, order, prefix, cap_len),...  3.3 us
    pallas_call x2, Pallas kernels, keys_of(): pl.pallas_call(functools.partial(keys_kernel, len(msgs)), out_shape=pltpu...  2.07 us
    pallas_call x1, Pallas kernels, paired(): pl.pallas_call(pack_kernel, out_shape=jax.ShapeDtypeStruct((piece_rows +...  0.88 us
  transfers between devices with their start and end apart: 10, of which 4 were waited for; matrix products, arithmetic and copies ran while one was open for 0% of the time, Pallas kernels for 5%

profile of v8, /device:TPU:0, one launch (start us, length us, event | category | flops | bytes accessed | tf_op | source)
XLA Modules:
  0.0 40.0 jit_solution(1324886945459878065)
XLA Ops:
  0.0 0.9 %pack.1.refs_0_ = bf16[56,768]{1,0:T(8,128)(2,1)S(1)} custom-call(s32[1,2]{1,0:T(1,128)} %cand_hbm.1, s32[1,4]{1,0:T(1,128)} %ids_hbm.1, bf16[1,32,768]{2,1,0:T(8,128)(2,1)} %rows_hbm.1, bf16[1,4,4096]{2,1,0:T(4,128)(2,1)} %states_hbm.1), custom_call_target="tpu_custom_call" | custom-call | tf_op jit(solution)/shard_map/pack/pallas_call | solution.py:271
  0.9 5.1 %collective-permute-start.2 = (bf16[56,768]{1,0:T(8,128)(2,1)S(1)}, bf16[56,768]{1,0:T(8,128)(2,1)S(1)}, u32[]{:S(2)}, u32[]{:S(2)}) collective-permute-start(bf16[56,768]{1,0:T(8,128)(2,1)S(1)} %pack.1.refs_0_), channel_id=1, source_target_pairs={{0,12},{1,13},{2,14},{3,15},{4,8},{5,9},{6,10},{7,11},{8,4},{9,5},... | collective-permute-start | bytes 258056 | tf_op jit(solution)/shard_map/ppermute | solution.py:269
  6.0 1.5 %collective-permute-start = (bf16[56,768]{1,0:T(8,128)(2,1)S(1)}, bf16[56,768]{1,0:T(8,128)(2,1)S(1)}, u32[]{:S(2)}, u32[]{:S(2)}) collective-permute-start(bf16[56,768]{1,0:T(8,128)(2,1)S(1)} %pack.1.refs_0_), channel_id=1, source_target_pairs={{0,2},{1,3},{2,0},{3,1},{4,6},{5,7},{6,4},{7,5},{8,10},{9,11},{10,... | collective-permute-start | bytes 258056 | tf_op jit(solution)/shard_map/ppermute | solution.py:269
  7.5 0.6 %collective-permute-start.4 = (bf16[56,768]{1,0:T(8,128)(2,1)S(1)}, bf16[56,768]{1,0:T(8,128)(2,1)S(1)}, u32[]{:S(2)}, u32[]{:S(2)}) collective-permute-start(bf16[56,768]{1,0:T(8,128)(2,1)S(1)} %pack.1.refs_0_), channel_id=1, source_target_pairs={{0,10},{1,11},{2,8},{3,9},{4,14},{5,15},{6,12},{7,13},{8,2},{9,3},... | collective-permute-start | bytes 258056 | tf_op jit(solution)/shard_map/ppermute | solution.py:269
  8.1 1.8 %collective-permute-start.3 = (bf16[56,768]{1,0:T(8,128)(2,1)S(1)}, bf16[56,768]{1,0:T(8,128)(2,1)S(1)}, u32[]{:S(2)}, u32[]{:S(2)}) collective-permute-start(bf16[56,768]{1,0:T(8,128)(2,1)S(1)} %pack.1.refs_0_), channel_id=1, source_target_pairs={{0,6},{1,7},{2,4},{3,5},{4,2},{5,3},{6,0},{7,1},{8,14},{9,15},{10,... | collective-permute-start | bytes 258056 | tf_op jit(solution)/shard_map/ppermute | solution.py:269
  10.5 0.0 copy-start
  10.5 0.0 copy-start.1
  10.6 0.0 slice-start
  10.6 0.0 slice-start.2
  10.6 0.0 copy-start.2
  10.6 0.0 collective-permute-done.2.refs_3_
  10.6 1.4 %collective-permute-start.6 = (bf16[56,768]{1,0:T(8,128)(2,1)S(1)}, bf16[56,768]{1,0:T(8,128)(2,1)S(1)}, u32[]{:S(2)}, u32[]{:S(2)}) collective-permute-start(bf16[56,768]{1,0:T(8,128)(2,1)S(1)} %collective-permute-done.2.refs_3_), channel_id=1, source_target_pairs={{0,4},{1,5},{2,6},{3,7},{4,0},{5,1},{6,2},{7,3},{8,12},{9,13},{10,... | collective-permute-start | bytes 258056 | tf_op jit(solution)/shard_map/ppermute | solution.py:269
  12.0 0.0 collective-permute-done.1.refs_2_
  12.0 1.9 %collective-permute-start.5 = (bf16[56,768]{1,0:T(8,128)(2,1)S(1)}, bf16[56,768]{1,0:T(8,128)(2,1)S(1)}, u32[]{:S(2)}, u32[]{:S(2)}) collective-permute-start(bf16[56,768]{1,0:T(8,128)(2,1)S(1)} %collective-permute-done.2.refs_3_), channel_id=1, source_target_pairs={{0,2},{1,3},{2,0},{3,1},{4,6},{5,7},{6,4},{7,5},{8,10},{9,11},{10,... | collective-permute-start | bytes 258056 | tf_op jit(solution)/shard_map/ppermute | solution.py:269
  13.9 0.0 collective-permute-done.refs_1_
  14.0 0.0 slice-start.3
  14.0 0.1 collective-permute-start.7
  14.1 1.1 %keys.2.refs_4_.refs_5_ = bf16[128,4096]{1,0:T(8,128)(2,1)S(1)} custom-call(bf16[56,768]{1,0:T(8,128)(2,1)S(1)} %pack.1.refs_0_, bf16[56,768]{1,0:T(8,128)(2,1)S(1)} %collective-permute-done.refs_1_, bf16[56,768]{1,0:T(8,128)(2,1)S(1)} %collective-permute-done.1.refs_2_, bf16[56,768]{1,0:T(8,128)(2,1)S(1)} %collective-permute-done.2.refs_3_, ...), custom_call_target="tpu_custom_call" | custom-call | flops 805306368 | bytes 12582912 | tf_op jit(solution)/shard_map/keys/pallas_call | solution.py:319
  15.2 0.0 collective-permute-done.4.refs_1_
  15.2 0.9 %collective-permute-done.3.refs_0_ = bf16[56,768]{1,0:T(8,128)(2,1)S(1)} collective-permute-done((bf16[56,768]{1,0:T(8,128)(2,1)S(1)}, bf16[56,768]{1,0:T(8,128)(2,1)S(1)}, u32[]{:S(2)}, u32[]{:S(2)}) %collective-permute-start.3) | collective-permute-done | bytes 86048 | tf_op jit(solution)/shard_map/ppermute | solution.py:269
  16.1 0.0 collective-permute-done.6.refs_3_
  16.1 0.9 %collective-permute-done.5.refs_2_ = bf16[56,768]{1,0:T(8,128)(2,1)S(1)} collective-permute-done((bf16[56,768]{1,0:T(8,128)(2,1)S(1)}, bf16[56,768]{1,0:T(8,128)(2,1)S(1)}, u32[]{:S(2)}, u32[]{:S(2)}) %collective-permute-start.5) | collective-permute-done | bytes 86048 | tf_op jit(solution)/shard_map/ppermute | solution.py:269
  17.0 0.1 collective-permute-start.8
  17.1 1.0 %keys.3.refs_6_ = bf16[128,4096]{1,0:T(8,128)(2,1)S(1)} custom-call(bf16[56,768]{1,0:T(8,128)(2,1)S(1)} %collective-permute-done.3.refs_0_, bf16[56,768]{1,0:T(8,128)(2,1)S(1)} %collective-permute-done.4.refs_1_, bf16[56,768]{1,0:T(8,128)(2,1)S(1)} %collective-permute-done.5.refs_2_, bf16[56,768]{1,0:T(8,128)(2,1)S(1)} %collective-permute-done.6.refs_3_, ...), custom_call_target="tpu_custom_call" | custom-call | flops 805306368 | bytes 12582912 | tf_op jit(solution)/shard_map/keys/pallas_call | solution.py:319
  18.1 0.0 collective-permute-done.7.refs_3_
  18.1 0.4 %collective-permute-done.8.refs_4_ = bf16[128,768]{1,0:T(8,128)(2,1)S(1)} collective-permute-done((bf16[128,768]{1,0:T(8,128)(2,1)S(1)}, bf16[128,768]{1,0:T(8,128)(2,1)S(1)}, u32[]{:S(2)}, u32[]{:S(2)}) %collective-permute-start.8) | collective-permute-done | bytes 196640 | tf_op jit(solution)/shard_map/ppermute | solution.py:269
  18.5 3.3 %hidden.1.mine_ref = bf16[64,4224]{1,0:T(8,128)(2,1)S(1)} custom-call(s32[1]{0:T(128)} %bitcast.pos_ref.refs_0_, bf16[128,768]{1,0:T(8,128)(2,1)S(1)} %collect.2.refs_1_, bf16[128,768]{1,0:T(8,128)(2,1)S(1)} %collect.3.refs_2_, bf16[128,768]{1,0:T(8,128)(2,1)S(1)} %collective-permute-done.7.refs_3_, bf16[128,768]{1,0:T(8,128)(2,1)S(1)} %collective-permute-done.8.refs_4_, ...), custom_call_target="tpu_custom_call" | custom-call | tf_op jit(solution)/shard_map/hidden/pallas_call | solution.py:336
  21.8 0.2 collective-permute-start.9
  22.1 1.8 %collective-permute-done.9.other_ref = bf16[64,4224]{1,0:T(8,128)(2,1)S(1)} collective-permute-done((bf16[64,4224]{1,0:T(8,128)(2,1)S(1)}, bf16[64,4224]{1,0:T(8,128)(2,1)S(1)}, u32[]{:S(2)}, u32[]{:S(2)}) %collective-permute-start.9) | collective-permute-done | bytes 540704 | tf_op jit(solution)/shard_map/ppermute | solution.py:269
  23.9 4.7 %logits.1 = f32[16,1,128]{2,1,0:T(1,128)S(1)} custom-call(s32[1]{0:T(128)} %bitcast.pos_ref.refs_0_, bf16[64,4224]{1,0:T(8,128)(2,1)S(1)} %hidden.1.mine_ref, bf16[64,4224]{1,0:T(8,128)(2,1)S(1)} %collective-permute-done.9.other_ref, bf16[2008,4096]{1,0:T(8,128)(2,1)S(1)} %bitcast.7, f32[1,128]{1,0:T(1,128)S(1)} %length.1.length_ref), custom_call_target="tpu_custom_call" | custom-call | tf_op jit(solution)/shard_map/logits/pallas_call | solution.py:353
  28.6 10.7 %all_to_all.5.stats_ref = f32[16,1,128]{2,1,0:T(1,128)S(1)} all-to-all(f32[16,1,128]{2,1,0:T(1,128)S(1)} %logits.1), channel_id=1, replica_groups=mesh['groups'=2,'dp'=16] {'dp'}, dimensions={0} | all-to-all | bytes 16384 | tf_op jit(solution)/shard_map/all_to_all | solution.py:363
  39.3 0.7 %finish.1 = f32[1,2,4]{2,1,0:T(2,128)} custom-call(f32[16,1,128]{2,1,0:T(1,128)S(1)} %all_to_all.5.stats_ref, bf16[64,4224]{1,0:T(8,128)(2,1)S(1)} %hidden.1.mine_ref), custom_call_target="tpu_custom_call" | custom-call | tf_op jit(solution)/shard_map/finish/pallas_call | solution.py:364
  (13 shorter events, 0.1 us)
Async XLA Ops:
  0.9 9.7 %collective-permute-start.2 = (bf16[56,768]{1,0:T(8,128)(2,1)S(1)}, bf16[56,768]{1,0:T(8,128)(2,1)S(1)}, u32[]{:S(2)}, u32[]{:S(2)}) collective-permute-start(bf16[56,768]{1,0:T(8,128)(2,1)S(1)} %pack.1.refs_0_), channel_id=1, source_target_pairs={{0,12},{1,13},{2,14},{3,15},{4,8},{5,9},{6,10},{7,11},{8,4},{9,5},... | collective-permute-start | bytes 258056 | tf_op jit(solution)/shard_map/ppermute | solution.py:269
  6.0 6.0 %collective-permute-start.1 = (bf16[56,768]{1,0:T(8,128)(2,1)S(1)}, bf16[56,768]{1,0:T(8,128)(2,1)S(1)}, u32[]{:S(2)}, u32[]{:S(2)}) collective-permute-start(bf16[56,768]{1,0:T(8,128)(2,1)S(1)} %pack.1.refs_0_), channel_id=1, source_target_pairs={{0,4},{1,5},{2,6},{3,7},{4,0},{5,1},{6,2},{7,3},{8,12},{9,13},{10,... | collective-permute-start | bytes 258056 | tf_op jit(solution)/shard_map/ppermute | solution.py:269
  6.0 7.9 %collective-permute-start = (bf16[56,768]{1,0:T(8,128)(2,1)S(1)}, bf16[56,768]{1,0:T(8,128)(2,1)S(1)}, u32[]{:S(2)}, u32[]{:S(2)}) collective-permute-start(bf16[56,768]{1,0:T(8,128)(2,1)S(1)} %pack.1.refs_0_), channel_id=1, source_target_pairs={{0,2},{1,3},{2,0},{3,1},{4,6},{5,7},{6,4},{7,5},{8,10},{9,11},{10,... | collective-permute-start | bytes 258056 | tf_op jit(solution)/shard_map/ppermute | solution.py:269
  7.5 7.6 %collective-permute-start.4 = (bf16[56,768]{1,0:T(8,128)(2,1)S(1)}, bf16[56,768]{1,0:T(8,128)(2,1)S(1)}, u32[]{:S(2)}, u32[]{:S(2)}) collective-permute-start(bf16[56,768]{1,0:T(8,128)(2,1)S(1)} %pack.1.refs_0_), channel_id=1, source_target_pairs={{0,10},{1,11},{2,8},{3,9},{4,14},{5,15},{6,12},{7,13},{8,2},{9,3},... | collective-permute-start | bytes 258056 | tf_op jit(solution)/shard_map/ppermute | solution.py:269
  8.1 8.0 %collective-permute-start.3 = (bf16[56,768]{1,0:T(8,128)(2,1)S(1)}, bf16[56,768]{1,0:T(8,128)(2,1)S(1)}, u32[]{:S(2)}, u32[]{:S(2)}) collective-permute-start(bf16[56,768]{1,0:T(8,128)(2,1)S(1)} %pack.1.refs_0_), channel_id=1, source_target_pairs={{0,6},{1,7},{2,4},{3,5},{4,2},{5,3},{6,0},{7,1},{8,14},{9,15},{10,... | collective-permute-start | bytes 258056 | tf_op jit(solution)/shard_map/ppermute | solution.py:269
  10.5 3.5 %copy-start = (bf16[768,4096]{1,0:T(8,128)(2,1)S(1)}, bf16[768,4096]{1,0:T(8,128)(2,1)}, u32[]{:S(2)}) copy-start(bf16[768,4096]{1,0:T(8,128)(2,1)} %refs_4_.3) | copy-start | bytes 18874372
  10.5 3.5 %copy-start.1 = (bf16[4096]{0:T(1024)(128)(2,1)S(1)}, bf16[4096]{0:T(1024)(128)(2,1)}, u32[]{:S(2)}) copy-start(bf16[4096]{0:T(1024)(128)(2,1)} %refs_5_.3) | copy-start | bytes 24580
  10.6 13.3 %slice-start = ((s8[16449536]{0:T(1024)(128)(4,1)}), s8[4194304]{0:T(1024)(128)(4,1)S(1)}, s32[]{:S(2)}) async-start(s8[16449536]{0:T(1024)(128)(4,1)} %bitcast.5), calls=%async_computation.1 | async-start | bytes 8388608
  10.6 13.3 %slice-start.1 = ((s8[16449536]{0:T(1024)(128)(4,1)}), s8[4194304]{0:T(1024)(128)(4,1)S(1)}, s32[]{:S(2)}) async-start(s8[16449536]{0:T(1024)(128)(4,1)} %bitcast.5), calls=%async_computation.2 | async-start | bytes 8388608
  10.6 13.3 %slice-start.2 = ((s8[16449536]{0:T(1024)(128)(4,1)}), s8[4194304]{0:T(1024)(128)(4,1)S(1)}, s32[]{:S(2)}) async-start(s8[16449536]{0:T(1024)(128)(4,1)} %bitcast.5), calls=%async_computation.3 | async-start | bytes 8388608
  10.6 7.9 %copy-start.2 = (f32[4096]{0:T(1024)S(1)}, f32[4096]{0:T(1024)}, u32[]{:S(2)}) copy-start(f32[4096]{0:T(1024)} %param.16) | copy-start | bytes 49156
  10.6 5.5 %collective-permute-start.6 = (bf16[56,768]{1,0:T(8,128)(2,1)S(1)}, bf16[56,768]{1,0:T(8,128)(2,1)S(1)}, u32[]{:S(2)}, u32[]{:S(2)}) collective-permute-start(bf16[56,768]{1,0:T(8,128)(2,1)S(1)} %collective-permute-done.2.refs_3_), channel_id=1, source_target_pairs={{0,4},{1,5},{2,6},{3,7},{4,0},{5,1},{6,2},{7,3},{8,12},{9,13},{10,... | collective-permute-start | bytes 258056 | tf_op jit(solution)/shard_map/ppermute | solution.py:269
  12.0 5.0 %collective-permute-start.5 = (bf16[56,768]{1,0:T(8,128)(2,1)S(1)}, bf16[56,768]{1,0:T(8,128)(2,1)S(1)}, u32[]{:S(2)}, u32[]{:S(2)}) collective-permute-start(bf16[56,768]{1,0:T(8,128)(2,1)S(1)} %collective-permute-done.2.refs_3_), channel_id=1, source_target_pairs={{0,2},{1,3},{2,0},{3,1},{4,6},{5,7},{6,4},{7,5},{8,10},{9,11},{10,... | collective-permute-start | bytes 258056 | tf_op jit(solution)/shard_map/ppermute | solution.py:269
  14.0 9.9 %slice-start.3 = ((s8[16449536]{0:T(1024)(128)(4,1)}), s8[3866624]{0:T(1024)(128)(4,1)S(1)}, s32[]{:S(2)}) async-start(s8[16449536]{0:T(1024)(128)(4,1)} %bitcast.5), calls=%async_computation.4 | async-start | bytes 7733248
  14.0 4.1 %collective-permute-start.7 = (bf16[128,768]{1,0:T(8,128)(2,1)S(1)}, bf16[128,768]{1,0:T(8,128)(2,1)S(1)}, u32[]{:S(2)}, u32[]{:S(2)}) collective-permute-start(bf16[128,768]{1,0:T(8,128)(2,1)S(1)} %collect.2.refs_1_), channel_id=1, source_target_pairs={{0,1},{1,0},{2,3},{3,2},{4,5},{5,4},{6,7},{7,6},{8,9},{9,8},{10,11... | collective-permute-start | bytes 589832 | tf_op jit(solution)/shard_map/ppermute | solution.py:269
  17.0 1.5 %collective-permute-start.8 = (bf16[128,768]{1,0:T(8,128)(2,1)S(1)}, bf16[128,768]{1,0:T(8,128)(2,1)S(1)}, u32[]{:S(2)}, u32[]{:S(2)}) collective-permute-start(bf16[128,768]{1,0:T(8,128)(2,1)S(1)} %collect.3.refs_2_), channel_id=1, source_target_pairs={{0,1},{1,0},{2,3},{3,2},{4,5},{5,4},{6,7},{7,6},{8,9},{9,8},{10,11... | collective-permute-start | bytes 589832 | tf_op jit(solution)/shard_map/ppermute | solution.py:269
  21.8 2.0 %collective-permute-start.9 = (bf16[64,4224]{1,0:T(8,128)(2,1)S(1)}, bf16[64,4224]{1,0:T(8,128)(2,1)S(1)}, u32[]{:S(2)}, u32[]{:S(2)}) collective-permute-start(bf16[64,4224]{1,0:T(8,128)(2,1)S(1)} %hidden.1.mine_ref), channel_id=1, source_target_pairs={{0,1},{1,0},{2,3},{3,2},{4,5},{5,4},{6,7},{7,6},{8,9},{9,8},{10,11... | collective-permute-start | bytes 1622024 | tf_op jit(solution)/shard_map/ppermute | solution.py:269

commit v9 on v8

--- a/solution.py
+++ b/solution.py
@@ -297,7 +297,7 @@
         name="length",
     )(position, caption_lengths, in_hbm(head_weight.T), in_hbm(head_weight.T), in_hbm(proj_weight))
     got[10] = swap(message, 10)
-    got[6] = swap(message, 6)
+    got[6] = swap(got[4], 2)
     got[12], length = lax.optimization_barrier((got[12], length))
     got[8], got[14] = swap(got[12], 4), swap(got[12], 2)
     order = (0, 2, 4, 12, 6, 10, 14, 8)

time: 40.2 us -> 40.2 us (level)
  starting transfers between devices: 12.7 us -> 11.6 us
  waiting for transfers between devices: 4.05 us -> 4.92 us
    ppermute x10, starting transfers between devices: 12.7 us -> 11.6 us  [swap(): return lax.ppermute(a, 'dp', [(i, i ^ away) for i in range(shards)])]
    ppermute x10, waiting for transfers between devices: 4.05 us -> 4.92 us  [swap(): return lax.ppermute(a, 'dp', [(i, i ^ away) for i in range(shards)])]
  transfers between devices with their start and end apart: 10 -> 10, of which waited for: 4 -> 6; matrix products, arithmetic and copies ran while one was open for 0% -> 0% of each run, Pallas kernels for 5% -> 5%
where the time goes in v9:
time: 40.2 us; the launch traced here: 40 us
  Pallas kernels  11.7 us (29%)
  starting transfers between devices  11.6 us (29%)
  blocking collectives  10.9 us (27%)
  waiting for transfers between devices  4.92 us (12%)
  between operations  0.84 us (2%)
    ppermute x10, starting transfers between devices, swap(): return lax.ppermute(a, 'dp', [(i, i ^ away) for i in range(shards)])  11.6 us
    all_to_all x1, blocking collectives, paired(): stats = lax.all_to_all(stats, 'dp', 0, 0, tiled=True)  10.9 us
    ppermute x10, waiting for transfers between devices, swap(): return lax.ppermute(a, 'dp', [(i, i ^ away) for i in range(shards)])  4.92 us
    pallas_call x1, Pallas kernels, paired(): pl.pallas_call(functools.partial(logits_kernel, order), out_shape=jax.Sha...  4.67 us
    pallas_call x1, Pallas kernels, paired(): pl.pallas_call(functools.partial(hidden_kernel, order, prefix, cap_len),...  3.31 us
    pallas_call x2, Pallas kernels, keys_of(): pl.pallas_call(functools.partial(keys_kernel, len(msgs)), out_shape=pltpu...  2.11 us
    pallas_call x1, Pallas kernels, paired(): pl.pallas_call(pack_kernel, out_shape=jax.ShapeDtypeStruct((piece_rows +...  0.88 us
  transfers between devices with their start and end apart: 10, of which 6 were waited for; matrix products, arithmetic and copies ran while one was open for 0% of the time, Pallas kernels for 5%

profile of v9, /device:TPU:0, one launch (start us, length us, event | category | flops | bytes accessed | tf_op | source)
XLA Modules:
  0.0 40.0 jit_solution(2427471122750408881)
XLA Ops:
  0.0 0.9 %pack.1.refs_0_ = bf16[56,768]{1,0:T(8,128)(2,1)S(1)} custom-call(s32[1,2]{1,0:T(1,128)} %cand_hbm.1, s32[1,4]{1,0:T(1,128)} %ids_hbm.1, bf16[1,32,768]{2,1,0:T(8,128)(2,1)} %rows_hbm.1, bf16[1,4,4096]{2,1,0:T(4,128)(2,1)} %states_hbm.1), custom_call_target="tpu_custom_call" | custom-call | tf_op jit(solution)/shard_map/pack/pallas_call | solution.py:271
  0.9 5.1 %collective-permute-start.2 = (bf16[56,768]{1,0:T(8,128)(2,1)S(1)}, bf16[56,768]{1,0:T(8,128)(2,1)S(1)}, u32[]{:S(2)}, u32[]{:S(2)}) collective-permute-start(bf16[56,768]{1,0:T(8,128)(2,1)S(1)} %pack.1.refs_0_), channel_id=1, source_target_pairs={{0,12},{1,13},{2,14},{3,15},{4,8},{5,9},{6,10},{7,11},{8,4},{9,5},... | collective-permute-start | bytes 258056 | tf_op jit(solution)/shard_map/ppermute | solution.py:269
  6.0 0.0 collective-permute-start.1
  6.0 1.5 %collective-permute-start = (bf16[56,768]{1,0:T(8,128)(2,1)S(1)}, bf16[56,768]{1,0:T(8,128)(2,1)S(1)}, u32[]{:S(2)}, u32[]{:S(2)}) collective-permute-start(bf16[56,768]{1,0:T(8,128)(2,1)S(1)} %pack.1.refs_0_), channel_id=1, source_target_pairs={{0,2},{1,3},{2,0},{3,1},{4,6},{5,7},{6,4},{7,5},{8,10},{9,11},{10,... | collective-permute-start | bytes 258056 | tf_op jit(solution)/shard_map/ppermute | solution.py:269
  7.5 0.6 %collective-permute-start.4 = (bf16[56,768]{1,0:T(8,128)(2,1)S(1)}, bf16[56,768]{1,0:T(8,128)(2,1)S(1)}, u32[]{:S(2)}, u32[]{:S(2)}) collective-permute-start(bf16[56,768]{1,0:T(8,128)(2,1)S(1)} %pack.1.refs_0_), channel_id=1, source_target_pairs={{0,10},{1,11},{2,8},{3,9},{4,14},{5,15},{6,12},{7,13},{8,2},{9,3},... | collective-permute-start | bytes 258056 | tf_op jit(solution)/shard_map/ppermute | solution.py:269
  8.8 0.0 copy-start
  8.8 0.0 copy-start.1
  8.8 0.0 slice-start
  8.8 0.0 slice-start.1
  8.8 0.0 slice-start.2
  8.8 0.0 copy-start.2
  8.8 0.5 %collective-permute-done.2.refs_3_ = bf16[56,768]{1,0:T(8,128)(2,1)S(1)} collective-permute-done((bf16[56,768]{1,0:T(8,128)(2,1)S(1)}, bf16[56,768]{1,0:T(8,128)(2,1)S(1)}, u32[]{:S(2)}, u32[]{:S(2)}) %collective-permute-start.2) | collective-permute-done | bytes 86048 | tf_op jit(solution)/shard_map/ppermute | solution.py:269
  9.4 1.0 %collective-permute-start.6 = (bf16[56,768]{1,0:T(8,128)(2,1)S(1)}, bf16[56,768]{1,0:T(8,128)(2,1)S(1)}, u32[]{:S(2)}, u32[]{:S(2)}) collective-permute-start(bf16[56,768]{1,0:T(8,128)(2,1)S(1)} %collective-permute-done.2.refs_3_), channel_id=1, source_target_pairs={{0,4},{1,5},{2,6},{3,7},{4,0},{5,1},{6,2},{7,3},{8,12},{9,13},{10,... | collective-permute-start | bytes 258056 | tf_op jit(solution)/shard_map/ppermute | solution.py:269
  10.4 1.2 %collective-permute-start.5 = (bf16[56,768]{1,0:T(8,128)(2,1)S(1)}, bf16[56,768]{1,0:T(8,128)(2,1)S(1)}, u32[]{:S(2)}, u32[]{:S(2)}) collective-permute-start(bf16[56,768]{1,0:T(8,128)(2,1)S(1)} %collective-permute-done.2.refs_3_), channel_id=1, source_target_pairs={{0,2},{1,3},{2,0},{3,1},{4,6},{5,7},{6,4},{7,5},{8,10},{9,11},{10,... | collective-permute-start | bytes 258056 | tf_op jit(solution)/shard_map/ppermute | solution.py:269
  11.6 0.2 collective-permute-done.1.refs_2_
  11.8 1.7 %collective-permute-start.3 = (bf16[56,768]{1,0:T(8,128)(2,1)S(1)}, bf16[56,768]{1,0:T(8,128)(2,1)S(1)}, u32[]{:S(2)}, u32[]{:S(2)}) collective-permute-start(bf16[56,768]{1,0:T(8,128)(2,1)S(1)} %collective-permute-done.1.refs_2_), channel_id=1, source_target_pairs={{0,2},{1,3},{2,0},{3,1},{4,6},{5,7},{6,4},{7,5},{8,10},{9,11},{10,... | collective-permute-start | bytes 258056 | tf_op jit(solution)/shard_map/ppermute | solution.py:269
  13.6 0.0 collective-permute-done.refs_1_
  13.6 0.0 slice-start.3
  13.6 0.1 collective-permute-start.7
  13.7 1.1 %keys.2.refs_4_.refs_5_ = bf16[128,4096]{1,0:T(8,128)(2,1)S(1)} custom-call(bf16[56,768]{1,0:T(8,128)(2,1)S(1)} %pack.1.refs_0_, bf16[56,768]{1,0:T(8,128)(2,1)S(1)} %collective-permute-done.refs_1_, bf16[56,768]{1,0:T(8,128)(2,1)S(1)} %collective-permute-done.1.refs_2_, bf16[56,768]{1,0:T(8,128)(2,1)S(1)} %collective-permute-done.2.refs_3_, ...), custom_call_target="tpu_custom_call" | custom-call | flops 805306368 | bytes 12582912 | tf_op jit(solution)/shard_map/keys/pallas_call | solution.py:319
  14.8 0.0 collective-permute-done.4.refs_1_
  14.8 1.1 %collective-permute-done.5.refs_2_ = bf16[56,768]{1,0:T(8,128)(2,1)S(1)} collective-permute-done((bf16[56,768]{1,0:T(8,128)(2,1)S(1)}, bf16[56,768]{1,0:T(8,128)(2,1)S(1)}, u32[]{:S(2)}, u32[]{:S(2)}) %collective-permute-start.5) | collective-permute-done | bytes 86048 | tf_op jit(solution)/shard_map/ppermute | solution.py:269
  15.9 0.9 %collective-permute-done.3.refs_0_ = bf16[56,768]{1,0:T(8,128)(2,1)S(1)} collective-permute-done((bf16[56,768]{1,0:T(8,128)(2,1)S(1)}, bf16[56,768]{1,0:T(8,128)(2,1)S(1)}, u32[]{:S(2)}, u32[]{:S(2)}) %collective-permute-start.3) | collective-permute-done | bytes 86048 | tf_op jit(solution)/shard_map/ppermute | solution.py:269
  16.8 0.1 collective-permute-start.8
  16.9 1.1 %keys.3.refs_6_ = bf16[128,4096]{1,0:T(8,128)(2,1)S(1)} custom-call(bf16[56,768]{1,0:T(8,128)(2,1)S(1)} %collective-permute-done.3.refs_0_, bf16[56,768]{1,0:T(8,128)(2,1)S(1)} %collective-permute-done.4.refs_1_, bf16[56,768]{1,0:T(8,128)(2,1)S(1)} %collective-permute-done.5.refs_2_, bf16[56,768]{1,0:T(8,128)(2,1)S(1)} %collective-permute-done.6.refs_3_, ...), custom_call_target="tpu_custom_call" | custom-call | flops 805306368 | bytes 12582912 | tf_op jit(solution)/shard_map/keys/pallas_call | solution.py:319
  18.0 0.4 collective-permute-done.8.refs_4_
  18.4 3.3 %hidden.1.mine_ref = bf16[64,4224]{1,0:T(8,128)(2,1)S(1)} custom-call(s32[1]{0:T(128)} %bitcast.pos_ref.refs_0_, bf16[128,768]{1,0:T(8,128)(2,1)S(1)} %collect.2.refs_1_, bf16[128,768]{1,0:T(8,128)(2,1)S(1)} %collect.3.refs_2_, bf16[128,768]{1,0:T(8,128)(2,1)S(1)} %collective-permute-done.7.refs_3_, bf16[128,768]{1,0:T(8,128)(2,1)S(1)} %collective-permute-done.8.refs_4_, ...), custom_call_target="tpu_custom_call" | custom-call | tf_op jit(solution)/shard_map/hidden/pallas_call | solution.py:336
  21.7 0.2 collective-permute-start.9
  21.9 1.8 %collective-permute-done.9.other_ref = bf16[64,4224]{1,0:T(8,128)(2,1)S(1)} collective-permute-done((bf16[64,4224]{1,0:T(8,128)(2,1)S(1)}, bf16[64,4224]{1,0:T(8,128)(2,1)S(1)}, u32[]{:S(2)}, u32[]{:S(2)}) %collective-permute-start.9) | collective-permute-done | bytes 540704 | tf_op jit(solution)/shard_map/ppermute | solution.py:269
  23.7 4.7 %logits.1 = f32[16,1,128]{2,1,0:T(1,128)S(1)} custom-call(s32[1]{0:T(128)} %bitcast.pos_ref.refs_0_, bf16[64,4224]{1,0:T(8,128)(2,1)S(1)} %hidden.1.mine_ref, bf16[64,4224]{1,0:T(8,128)(2,1)S(1)} %collective-permute-done.9.other_ref, bf16[2008,4096]{1,0:T(8,128)(2,1)S(1)} %bitcast.7, f32[1,128]{1,0:T(1,128)S(1)} %length.1.length_ref), custom_call_target="tpu_custom_call" | custom-call | tf_op jit(solution)/shard_map/logits/pallas_call | solution.py:353
  28.4 10.9 %all_to_all.5.stats_ref = f32[16,1,128]{2,1,0:T(1,128)S(1)} all-to-all(f32[16,1,128]{2,1,0:T(1,128)S(1)} %logits.1), channel_id=1, replica_groups=mesh['groups'=2,'dp'=16] {'dp'}, dimensions={0} | all-to-all | bytes 16384 | tf_op jit(solution)/shard_map/all_to_all | solution.py:363
  39.3 0.7 %finish.1 = f32[1,2,4]{2,1,0:T(2,128)} custom-call(f32[16,1,128]{2,1,0:T(1,128)S(1)} %all_to_all.5.stats_ref, bf16[64,4224]{1,0:T(8,128)(2,1)S(1)} %hidden.1.mine_ref), custom_call_target="tpu_custom_call" | custom-call | tf_op jit(solution)/shard_map/finish/pallas_call | solution.py:364
  (13 shorter events, 0.1 us)
Async XLA Ops:
  0.9 8.5 %collective-permute-start.2 = (bf16[56,768]{1,0:T(8,128)(2,1)S(1)}, bf16[56,768]{1,0:T(8,128)(2,1)S(1)}, u32[]{:S(2)}, u32[]{:S(2)}) collective-permute-start(bf16[56,768]{1,0:T(8,128)(2,1)S(1)} %pack.1.refs_0_), channel_id=1, source_target_pairs={{0,12},{1,13},{2,14},{3,15},{4,8},{5,9},{6,10},{7,11},{8,4},{9,5},... | collective-permute-start | bytes 258056 | tf_op jit(solution)/shard_map/ppermute | solution.py:269
  6.0 5.8 %collective-permute-start.1 = (bf16[56,768]{1,0:T(8,128)(2,1)S(1)}, bf16[56,768]{1,0:T(8,128)(2,1)S(1)}, u32[]{:S(2)}, u32[]{:S(2)}) collective-permute-start(bf16[56,768]{1,0:T(8,128)(2,1)S(1)} %pack.1.refs_0_), channel_id=1, source_target_pairs={{0,4},{1,5},{2,6},{3,7},{4,0},{5,1},{6,2},{7,3},{8,12},{9,13},{10,... | collective-permute-start | bytes 258056 | tf_op jit(solution)/shard_map/ppermute | solution.py:269
  6.0 7.6 %collective-permute-start = (bf16[56,768]{1,0:T(8,128)(2,1)S(1)}, bf16[56,768]{1,0:T(8,128)(2,1)S(1)}, u32[]{:S(2)}, u32[]{:S(2)}) collective-permute-start(bf16[56,768]{1,0:T(8,128)(2,1)S(1)} %pack.1.refs_0_), channel_id=1, source_target_pairs={{0,2},{1,3},{2,0},{3,1},{4,6},{5,7},{6,4},{7,5},{8,10},{9,11},{10,... | collective-permute-start | bytes 258056 | tf_op jit(solution)/shard_map/ppermute | solution.py:269
  7.5 7.2 %collective-permute-start.4 = (bf16[56,768]{1,0:T(8,128)(2,1)S(1)}, bf16[56,768]{1,0:T(8,128)(2,1)S(1)}, u32[]{:S(2)}, u32[]{:S(2)}) collective-permute-start(bf16[56,768]{1,0:T(8,128)(2,1)S(1)} %pack.1.refs_0_), channel_id=1, source_target_pairs={{0,10},{1,11},{2,8},{3,9},{4,14},{5,15},{6,12},{7,13},{8,2},{9,3},... | collective-permute-start | bytes 258056 | tf_op jit(solution)/shard_map/ppermute | solution.py:269
  8.8 4.9 %copy-start = (bf16[768,4096]{1,0:T(8,128)(2,1)S(1)}, bf16[768,4096]{1,0:T(8,128)(2,1)}, u32[]{:S(2)}) copy-start(bf16[768,4096]{1,0:T(8,128)(2,1)} %refs_4_.3) | copy-start | bytes 18874372
  8.8 4.9 %copy-start.1 = (bf16[4096]{0:T(1024)(128)(2,1)S(1)}, bf16[4096]{0:T(1024)(128)(2,1)}, u32[]{:S(2)}) copy-start(bf16[4096]{0:T(1024)(128)(2,1)} %refs_5_.3) | copy-start | bytes 24580
  8.8 14.9 %slice-start = ((s8[16449536]{0:T(1024)(128)(4,1)}), s8[4194304]{0:T(1024)(128)(4,1)S(1)}, s32[]{:S(2)}) async-start(s8[16449536]{0:T(1024)(128)(4,1)} %bitcast.5), calls=%async_computation.1 | async-start | bytes 8388608
  8.8 14.9 %slice-start.1 = ((s8[16449536]{0:T(1024)(128)(4,1)}), s8[4194304]{0:T(1024)(128)(4,1)S(1)}, s32[]{:S(2)}) async-start(s8[16449536]{0:T(1024)(128)(4,1)} %bitcast.5), calls=%async_computation.2 | async-start | bytes 8388608
  8.8 14.9 %slice-start.2 = ((s8[16449536]{0:T(1024)(128)(4,1)}), s8[4194304]{0:T(1024)(128)(4,1)S(1)}, s32[]{:S(2)}) async-start(s8[16449536]{0:T(1024)(128)(4,1)} %bitcast.5), calls=%async_computation.3 | async-start | bytes 8388608
  8.8 9.5 %copy-start.2 = (f32[4096]{0:T(1024)S(1)}, f32[4096]{0:T(1024)}, u32[]{:S(2)}) copy-start(f32[4096]{0:T(1024)} %param.16) | copy-start | bytes 49156
  9.4 5.4 %collective-permute-start.6 = (bf16[56,768]{1,0:T(8,128)(2,1)S(1)}, bf16[56,768]{1,0:T(8,128)(2,1)S(1)}, u32[]{:S(2)}, u32[]{:S(2)}) collective-permute-start(bf16[56,768]{1,0:T(8,128)(2,1)S(1)} %collective-permute-done.2.refs_3_), channel_id=1, source_target_pairs={{0,4},{1,5},{2,6},{3,7},{4,0},{5,1},{6,2},{7,3},{8,12},{9,13},{10,... | collective-permute-start | bytes 258056 | tf_op jit(solution)/shard_map/ppermute | solution.py:269
  10.4 5.5 %collective-permute-start.5 = (bf16[56,768]{1,0:T(8,128)(2,1)S(1)}, bf16[56,768]{1,0:T(8,128)(2,1)S(1)}, u32[]{:S(2)}, u32[]{:S(2)}) collective-permute-start(bf16[56,768]{1,0:T(8,128)(2,1)S(1)} %collective-permute-done.2.refs_3_), channel_id=1, source_target_pairs={{0,2},{1,3},{2,0},{3,1},{4,6},{5,7},{6,4},{7,5},{8,10},{9,11},{10,... | collective-permute-start | bytes 258056 | tf_op jit(solution)/shard_map/ppermute | solution.py:269
  11.8 5.0 %collective-permute-start.3 = (bf16[56,768]{1,0:T(8,128)(2,1)S(1)}, bf16[56,768]{1,0:T(8,128)(2,1)S(1)}, u32[]{:S(2)}, u32[]{:S(2)}) collective-permute-start(bf16[56,768]{1,0:T(8,128)(2,1)S(1)} %collective-permute-done.1.refs_2_), channel_id=1, source_target_pairs={{0,2},{1,3},{2,0},{3,1},{4,6},{5,7},{6,4},{7,5},{8,10},{9,11},{10,... | collective-permute-start | bytes 258056 | tf_op jit(solution)/shard_map/ppermute | solution.py:269
  13.6 10.1 %slice-start.3 = ((s8[16449536]{0:T(1024)(128)(4,1)}), s8[3866624]{0:T(1024)(128)(4,1)S(1)}, s32[]{:S(2)}) async-start(s8[16449536]{0:T(1024)(128)(4,1)} %bitcast.5), calls=%async_computation.4 | async-start | bytes 7733248
  13.6 4.4 %collective-permute-start.7 = (bf16[128,768]{1,0:T(8,128)(2,1)S(1)}, bf16[128,768]{1,0:T(8,128)(2,1)S(1)}, u32[]{:S(2)}, u32[]{:S(2)}) collective-permute-start(bf16[128,768]{1,0:T(8,128)(2,1)S(1)} %collect.2.refs_1_), channel_id=1, source_target_pairs={{0,1},{1,0},{2,3},{3,2},{4,5},{5,4},{6,7},{7,6},{8,9},{9,8},{10,11... | collective-permute-start | bytes 589832 | tf_op jit(solution)/shard_map/ppermute | solution.py:269
  16.8 1.5 %collective-permute-start.8 = (bf16[128,768]{1,0:T(8,128)(2,1)S(1)}, bf16[128,768]{1,0:T(8,128)(2,1)S(1)}, u32[]{:S(2)}, u32[]{:S(2)}) collective-permute-start(bf16[128,768]{1,0:T(8,128)(2,1)S(1)} %collect.3.refs_2_), channel_id=1, source_target_pairs={{0,1},{1,0},{2,3},{3,2},{4,5},{5,4},{6,7},{7,6},{8,9},{9,8},{10,11... | collective-permute-start | bytes 589832 | tf_op jit(solution)/shard_map/ppermute | solution.py:269
  21.7 2.0 %collective-permute-start.9 = (bf16[64,4224]{1,0:T(8,128)(2,1)S(1)}, bf16[64,4224]{1,0:T(8,128)(2,1)S(1)}, u32[]{:S(2)}, u32[]{:S(2)}) collective-permute-start(bf16[64,4224]{1,0:T(8,128)(2,1)S(1)} %hidden.1.mine_ref), channel_id=1, source_target_pairs={{0,1},{1,0},{2,3},{3,2},{4,5},{5,4},{6,7},{7,6},{8,9},{9,8},{10,11... | collective-permute-start | bytes 1622024 | tf_op jit(solution)/shard_map/ppermute | solution.py:269

commit v10 on v9

--- a/solution.py
+++ b/solution.py
@@ -180,9 +180,10 @@
     for n, (g, cols) in enumerate(tiles):
         q, key = keys_of(g, cols)
         out = dot(weights[n], key)
-        value = q.astype(jnp.float32)
-        for h in range(heads):
-            value += jnp.where(lane == h, out[h * group_rows : (h + 1) * group_rows], 0.0)
+        mine = out[0:group_rows]
+        for h in range(1, heads):
+            mine = jnp.where(lane == h, out[h * group_rows : (h + 1) * group_rows], mine)
+        value = q.astype(jnp.float32) + mine
         mixed[g * group_rows : (g + 1) * group_rows, cols] = value
         squares[g] += value * value
     square = jnp.concatenate(squares, 0)

time: 40.2 us -> 40.2 us (level)
  no operation moved by 1% of the time
where the time goes in v10:
time: 40.2 us; the launch traced here: 40 us
  Pallas kernels  11.7 us (29%)
  starting transfers between devices  11.6 us (29%)
  blocking collectives  10.9 us (27%)
  waiting for transfers between devices  4.92 us (12%)
  between operations  0.84 us (2%)
    ppermute x10, starting transfers between devices, swap(): return lax.ppermute(a, 'dp', [(i, i ^ away) for i in range(shards)])  11.6 us
    all_to_all x1, blocking collectives, paired(): stats = lax.all_to_all(stats, 'dp', 0, 0, tiled=True)  10.9 us
    ppermute x10, waiting for transfers between devices, swap(): return lax.ppermute(a, 'dp', [(i, i ^ away) for i in range(shards)])  4.92 us
    pallas_call x1, Pallas kernels, paired(): pl.pallas_call(functools.partial(logits_kernel, order), out_shape=jax.Sha...  4.67 us
    pallas_call x1, Pallas kernels, paired(): pl.pallas_call(functools.partial(hidden_kernel, order, prefix, cap_len),...  3.27 us
    pallas_call x2, Pallas kernels, keys_of(): pl.pallas_call(functools.partial(keys_kernel, len(msgs)), out_shape=pltpu...  2.11 us
    pallas_call x1, Pallas kernels, paired(): pl.pallas_call(pack_kernel, out_shape=jax.ShapeDtypeStruct((piece_rows +...  0.88 us
  transfers between devices with their start and end apart: 10, of which 6 were waited for; matrix products, arithmetic and copies ran while one was open for 0% of the time, Pallas kernels for 5%

profile of v10, /device:TPU:0, one launch (start us, length us, event | category | flops | bytes accessed | tf_op | source)
XLA Modules:
  0.0 40.0 jit_solution(1938037506275333641)
XLA Ops:
  0.0 0.9 %pack.1.refs_0_ = bf16[56,768]{1,0:T(8,128)(2,1)S(1)} custom-call(s32[1,2]{1,0:T(1,128)} %cand_hbm.1, s32[1,4]{1,0:T(1,128)} %ids_hbm.1, bf16[1,32,768]{2,1,0:T(8,128)(2,1)} %rows_hbm.1, bf16[1,4,4096]{2,1,0:T(4,128)(2,1)} %states_hbm.1), custom_call_target="tpu_custom_call" | custom-call | tf_op jit(solution)/shard_map/pack/pallas_call | solution.py:272
  0.9 5.1 %collective-permute-start.2 = (bf16[56,768]{1,0:T(8,128)(2,1)S(1)}, bf16[56,768]{1,0:T(8,128)(2,1)S(1)}, u32[]{:S(2)}, u32[]{:S(2)}) collective-permute-start(bf16[56,768]{1,0:T(8,128)(2,1)S(1)} %pack.1.refs_0_), channel_id=1, source_target_pairs={{0,12},{1,13},{2,14},{3,15},{4,8},{5,9},{6,10},{7,11},{8,4},{9,5},... | collective-permute-start | bytes 258056 | tf_op jit(solution)/shard_map/ppermute | solution.py:270
  6.0 0.0 collective-permute-start.1
  6.0 1.5 %collective-permute-start = (bf16[56,768]{1,0:T(8,128)(2,1)S(1)}, bf16[56,768]{1,0:T(8,128)(2,1)S(1)}, u32[]{:S(2)}, u32[]{:S(2)}) collective-permute-start(bf16[56,768]{1,0:T(8,128)(2,1)S(1)} %pack.1.refs_0_), channel_id=1, source_target_pairs={{0,2},{1,3},{2,0},{3,1},{4,6},{5,7},{6,4},{7,5},{8,10},{9,11},{10,... | collective-permute-start | bytes 258056 | tf_op jit(solution)/shard_map/ppermute | solution.py:270
  7.5 0.6 %collective-permute-start.4 = (bf16[56,768]{1,0:T(8,128)(2,1)S(1)}, bf16[56,768]{1,0:T(8,128)(2,1)S(1)}, u32[]{:S(2)}, u32[]{:S(2)}) collective-permute-start(bf16[56,768]{1,0:T(8,128)(2,1)S(1)} %pack.1.refs_0_), channel_id=1, source_target_pairs={{0,10},{1,11},{2,8},{3,9},{4,14},{5,15},{6,12},{7,13},{8,2},{9,3},... | collective-permute-start | bytes 258056 | tf_op jit(solution)/shard_map/ppermute | solution.py:270
  8.8 0.0 copy-start
  8.8 0.0 copy-start.1
  8.8 0.0 slice-start
  8.8 0.0 slice-start.1
  8.8 0.0 slice-start.2
  8.8 0.0 copy-start.2
  8.8 0.5 %collective-permute-done.2.refs_3_ = bf16[56,768]{1,0:T(8,128)(2,1)S(1)} collective-permute-done((bf16[56,768]{1,0:T(8,128)(2,1)S(1)}, bf16[56,768]{1,0:T(8,128)(2,1)S(1)}, u32[]{:S(2)}, u32[]{:S(2)}) %collective-permute-start.2) | collective-permute-done | bytes 86048 | tf_op jit(solution)/shard_map/ppermute | solution.py:270
  9.4 1.0 %collective-permute-start.6 = (bf16[56,768]{1,0:T(8,128)(2,1)S(1)}, bf16[56,768]{1,0:T(8,128)(2,1)S(1)}, u32[]{:S(2)}, u32[]{:S(2)}) collective-permute-start(bf16[56,768]{1,0:T(8,128)(2,1)S(1)} %collective-permute-done.2.refs_3_), channel_id=1, source_target_pairs={{0,4},{1,5},{2,6},{3,7},{4,0},{5,1},{6,2},{7,3},{8,12},{9,13},{10,... | collective-permute-start | bytes 258056 | tf_op jit(solution)/shard_map/ppermute | solution.py:270
  10.4 1.2 %collective-permute-start.5 = (bf16[56,768]{1,0:T(8,128)(2,1)S(1)}, bf16[56,768]{1,0:T(8,128)(2,1)S(1)}, u32[]{:S(2)}, u32[]{:S(2)}) collective-permute-start(bf16[56,768]{1,0:T(8,128)(2,1)S(1)} %collective-permute-done.2.refs_3_), channel_id=1, source_target_pairs={{0,2},{1,3},{2,0},{3,1},{4,6},{5,7},{6,4},{7,5},{8,10},{9,11},{10,... | collective-permute-start | bytes 258056 | tf_op jit(solution)/shard_map/ppermute | solution.py:270
  11.6 0.2 collective-permute-done.1.refs_2_
  11.8 1.7 %collective-permute-start.3 = (bf16[56,768]{1,0:T(8,128)(2,1)S(1)}, bf16[56,768]{1,0:T(8,128)(2,1)S(1)}, u32[]{:S(2)}, u32[]{:S(2)}) collective-permute-start(bf16[56,768]{1,0:T(8,128)(2,1)S(1)} %collective-permute-done.1.refs_2_), channel_id=1, source_target_pairs={{0,2},{1,3},{2,0},{3,1},{4,6},{5,7},{6,4},{7,5},{8,10},{9,11},{10,... | collective-permute-start | bytes 258056 | tf_op jit(solution)/shard_map/ppermute | solution.py:270
  13.6 0.0 collective-permute-done.refs_1_
  13.6 0.0 slice-start.3
  13.6 0.1 collective-permute-start.7
  13.7 1.1 %keys.2.refs_4_.refs_5_ = bf16[128,4096]{1,0:T(8,128)(2,1)S(1)} custom-call(bf16[56,768]{1,0:T(8,128)(2,1)S(1)} %pack.1.refs_0_, bf16[56,768]{1,0:T(8,128)(2,1)S(1)} %collective-permute-done.refs_1_, bf16[56,768]{1,0:T(8,128)(2,1)S(1)} %collective-permute-done.1.refs_2_, bf16[56,768]{1,0:T(8,128)(2,1)S(1)} %collective-permute-done.2.refs_3_, ...), custom_call_target="tpu_custom_call" | custom-call | flops 805306368 | bytes 12582912 | tf_op jit(solution)/shard_map/keys/pallas_call | solution.py:320
  14.8 0.0 collective-permute-done.4.refs_1_
  14.8 1.1 %collective-permute-done.5.refs_2_ = bf16[56,768]{1,0:T(8,128)(2,1)S(1)} collective-permute-done((bf16[56,768]{1,0:T(8,128)(2,1)S(1)}, bf16[56,768]{1,0:T(8,128)(2,1)S(1)}, u32[]{:S(2)}, u32[]{:S(2)}) %collective-permute-start.5) | collective-permute-done | bytes 86048 | tf_op jit(solution)/shard_map/ppermute | solution.py:270
  15.9 0.9 %collective-permute-done.3.refs_0_ = bf16[56,768]{1,0:T(8,128)(2,1)S(1)} collective-permute-done((bf16[56,768]{1,0:T(8,128)(2,1)S(1)}, bf16[56,768]{1,0:T(8,128)(2,1)S(1)}, u32[]{:S(2)}, u32[]{:S(2)}) %collective-permute-start.3) | collective-permute-done | bytes 86048 | tf_op jit(solution)/shard_map/ppermute | solution.py:270
  16.8 0.1 collective-permute-start.8
  16.9 1.1 %keys.3.refs_6_ = bf16[128,4096]{1,0:T(8,128)(2,1)S(1)} custom-call(bf16[56,768]{1,0:T(8,128)(2,1)S(1)} %collective-permute-done.3.refs_0_, bf16[56,768]{1,0:T(8,128)(2,1)S(1)} %collective-permute-done.4.refs_1_, bf16[56,768]{1,0:T(8,128)(2,1)S(1)} %collective-permute-done.5.refs_2_, bf16[56,768]{1,0:T(8,128)(2,1)S(1)} %collective-permute-done.6.refs_3_, ...), custom_call_target="tpu_custom_call" | custom-call | flops 805306368 | bytes 12582912 | tf_op jit(solution)/shard_map/keys/pallas_call | solution.py:320
  18.0 0.4 collective-permute-done.8.refs_4_
  18.4 3.3 %hidden.1.mine_ref = bf16[64,4224]{1,0:T(8,128)(2,1)S(1)} custom-call(s32[1]{0:T(128)} %bitcast.pos_ref.refs_0_, bf16[128,768]{1,0:T(8,128)(2,1)S(1)} %collect.2.refs_1_, bf16[128,768]{1,0:T(8,128)(2,1)S(1)} %collect.3.refs_2_, bf16[128,768]{1,0:T(8,128)(2,1)S(1)} %collective-permute-done.7.refs_3_, bf16[128,768]{1,0:T(8,128)(2,1)S(1)} %collective-permute-done.8.refs_4_, ...), custom_call_target="tpu_custom_call" | custom-call | tf_op jit(solution)/shard_map/hidden/pallas_call | solution.py:337
  21.6 0.2 collective-permute-start.9
  21.9 1.8 %collective-permute-done.9.other_ref = bf16[64,4224]{1,0:T(8,128)(2,1)S(1)} collective-permute-done((bf16[64,4224]{1,0:T(8,128)(2,1)S(1)}, bf16[64,4224]{1,0:T(8,128)(2,1)S(1)}, u32[]{:S(2)}, u32[]{:S(2)}) %collective-permute-start.9) | collective-permute-done | bytes 540704 | tf_op jit(solution)/shard_map/ppermute | solution.py:270
  23.7 4.7 %logits.1 = f32[16,1,128]{2,1,0:T(1,128)S(1)} custom-call(s32[1]{0:T(128)} %bitcast.pos_ref.refs_0_, bf16[64,4224]{1,0:T(8,128)(2,1)S(1)} %hidden.1.mine_ref, bf16[64,4224]{1,0:T(8,128)(2,1)S(1)} %collective-permute-done.9.other_ref, bf16[2008,4096]{1,0:T(8,128)(2,1)S(1)} %bitcast.7, f32[1,128]{1,0:T(1,128)S(1)} %length.1.length_ref), custom_call_target="tpu_custom_call" | custom-call | tf_op jit(solution)/shard_map/logits/pallas_call | solution.py:354
  28.3 10.9 %all_to_all.5.stats_ref = f32[16,1,128]{2,1,0:T(1,128)S(1)} all-to-all(f32[16,1,128]{2,1,0:T(1,128)S(1)} %logits.1), channel_id=1, replica_groups=mesh['groups'=2,'dp'=16] {'dp'}, dimensions={0} | all-to-all | bytes 16384 | tf_op jit(solution)/shard_map/all_to_all | solution.py:364
  39.2 0.7 %finish.1 = f32[1,2,4]{2,1,0:T(2,128)} custom-call(f32[16,1,128]{2,1,0:T(1,128)S(1)} %all_to_all.5.stats_ref, bf16[64,4224]{1,0:T(8,128)(2,1)S(1)} %hidden.1.mine_ref), custom_call_target="tpu_custom_call" | custom-call | tf_op jit(solution)/shard_map/finish/pallas_call | solution.py:365
  (13 shorter events, 0.1 us)
Async XLA Ops:
  0.9 8.5 %collective-permute-start.2 = (bf16[56,768]{1,0:T(8,128)(2,1)S(1)}, bf16[56,768]{1,0:T(8,128)(2,1)S(1)}, u32[]{:S(2)}, u32[]{:S(2)}) collective-permute-start(bf16[56,768]{1,0:T(8,128)(2,1)S(1)} %pack.1.refs_0_), channel_id=1, source_target_pairs={{0,12},{1,13},{2,14},{3,15},{4,8},{5,9},{6,10},{7,11},{8,4},{9,5},... | collective-permute-start | bytes 258056 | tf_op jit(solution)/shard_map/ppermute | solution.py:270
  6.0 5.8 %collective-permute-start.1 = (bf16[56,768]{1,0:T(8,128)(2,1)S(1)}, bf16[56,768]{1,0:T(8,128)(2,1)S(1)}, u32[]{:S(2)}, u32[]{:S(2)}) collective-permute-start(bf16[56,768]{1,0:T(8,128)(2,1)S(1)} %pack.1.refs_0_), channel_id=1, source_target_pairs={{0,4},{1,5},{2,6},{3,7},{4,0},{5,1},{6,2},{7,3},{8,12},{9,13},{10,... | collective-permute-start | bytes 258056 | tf_op jit(solution)/shard_map/ppermute | solution.py:270
  6.0 7.6 %collective-permute-start = (bf16[56,768]{1,0:T(8,128)(2,1)S(1)}, bf16[56,768]{1,0:T(8,128)(2,1)S(1)}, u32[]{:S(2)}, u32[]{:S(2)}) collective-permute-start(bf16[56,768]{1,0:T(8,128)(2,1)S(1)} %pack.1.refs_0_), channel_id=1, source_target_pairs={{0,2},{1,3},{2,0},{3,1},{4,6},{5,7},{6,4},{7,5},{8,10},{9,11},{10,... | collective-permute-start | bytes 258056 | tf_op jit(solution)/shard_map/ppermute | solution.py:270
  7.5 7.2 %collective-permute-start.4 = (bf16[56,768]{1,0:T(8,128)(2,1)S(1)}, bf16[56,768]{1,0:T(8,128)(2,1)S(1)}, u32[]{:S(2)}, u32[]{:S(2)}) collective-permute-start(bf16[56,768]{1,0:T(8,128)(2,1)S(1)} %pack.1.refs_0_), channel_id=1, source_target_pairs={{0,10},{1,11},{2,8},{3,9},{4,14},{5,15},{6,12},{7,13},{8,2},{9,3},... | collective-permute-start | bytes 258056 | tf_op jit(solution)/shard_map/ppermute | solution.py:270
  8.8 4.9 %copy-start = (bf16[768,4096]{1,0:T(8,128)(2,1)S(1)}, bf16[768,4096]{1,0:T(8,128)(2,1)}, u32[]{:S(2)}) copy-start(bf16[768,4096]{1,0:T(8,128)(2,1)} %refs_4_.3) | copy-start | bytes 18874372
  8.8 4.9 %copy-start.1 = (bf16[4096]{0:T(1024)(128)(2,1)S(1)}, bf16[4096]{0:T(1024)(128)(2,1)}, u32[]{:S(2)}) copy-start(bf16[4096]{0:T(1024)(128)(2,1)} %refs_5_.3) | copy-start | bytes 24580
  8.8 14.8 %slice-start = ((s8[16449536]{0:T(1024)(128)(4,1)}), s8[4194304]{0:T(1024)(128)(4,1)S(1)}, s32[]{:S(2)}) async-start(s8[16449536]{0:T(1024)(128)(4,1)} %bitcast.5), calls=%async_computation.1 | async-start | bytes 8388608
  8.8 14.8 %slice-start.1 = ((s8[16449536]{0:T(1024)(128)(4,1)}), s8[4194304]{0:T(1024)(128)(4,1)S(1)}, s32[]{:S(2)}) async-start(s8[16449536]{0:T(1024)(128)(4,1)} %bitcast.5), calls=%async_computation.2 | async-start | bytes 8388608
  8.8 14.8 %slice-start.2 = ((s8[16449536]{0:T(1024)(128)(4,1)}), s8[4194304]{0:T(1024)(128)(4,1)S(1)}, s32[]{:S(2)}) async-start(s8[16449536]{0:T(1024)(128)(4,1)} %bitcast.5), calls=%async_computation.3 | async-start | bytes 8388608
  8.8 9.5 %copy-start.2 = (f32[4096]{0:T(1024)S(1)}, f32[4096]{0:T(1024)}, u32[]{:S(2)}) copy-start(f32[4096]{0:T(1024)} %param.16) | copy-start | bytes 49156
  9.4 5.4 %collective-permute-start.6 = (bf16[56,768]{1,0:T(8,128)(2,1)S(1)}, bf16[56,768]{1,0:T(8,128)(2,1)S(1)}, u32[]{:S(2)}, u32[]{:S(2)}) collective-permute-start(bf16[56,768]{1,0:T(8,128)(2,1)S(1)} %collective-permute-done.2.refs_3_), channel_id=1, source_target_pairs={{0,4},{1,5},{2,6},{3,7},{4,0},{5,1},{6,2},{7,3},{8,12},{9,13},{10,... | collective-permute-start | bytes 258056 | tf_op jit(solution)/shard_map/ppermute | solution.py:270
  10.4 5.5 %collective-permute-start.5 = (bf16[56,768]{1,0:T(8,128)(2,1)S(1)}, bf16[56,768]{1,0:T(8,128)(2,1)S(1)}, u32[]{:S(2)}, u32[]{:S(2)}) collective-permute-start(bf16[56,768]{1,0:T(8,128)(2,1)S(1)} %collective-permute-done.2.refs_3_), channel_id=1, source_target_pairs={{0,2},{1,3},{2,0},{3,1},{4,6},{5,7},{6,4},{7,5},{8,10},{9,11},{10,... | collective-permute-start | bytes 258056 | tf_op jit(solution)/shard_map/ppermute | solution.py:270
  11.8 5.0 %collective-permute-start.3 = (bf16[56,768]{1,0:T(8,128)(2,1)S(1)}, bf16[56,768]{1,0:T(8,128)(2,1)S(1)}, u32[]{:S(2)}, u32[]{:S(2)}) collective-permute-start(bf16[56,768]{1,0:T(8,128)(2,1)S(1)} %collective-permute-done.1.refs_2_), channel_id=1, source_target_pairs={{0,2},{1,3},{2,0},{3,1},{4,6},{5,7},{6,4},{7,5},{8,10},{9,11},{10,... | collective-permute-start | bytes 258056 | tf_op jit(solution)/shard_map/ppermute | solution.py:270
  13.6 10.1 %slice-start.3 = ((s8[16449536]{0:T(1024)(128)(4,1)}), s8[3866624]{0:T(1024)(128)(4,1)S(1)}, s32[]{:S(2)}) async-start(s8[16449536]{0:T(1024)(128)(4,1)} %bitcast.5), calls=%async_computation.4 | async-start | bytes 7733248
  13.6 4.4 %collective-permute-start.7 = (bf16[128,768]{1,0:T(8,128)(2,1)S(1)}, bf16[128,768]{1,0:T(8,128)(2,1)S(1)}, u32[]{:S(2)}, u32[]{:S(2)}) collective-permute-start(bf16[128,768]{1,0:T(8,128)(2,1)S(1)} %collect.2.refs_1_), channel_id=1, source_target_pairs={{0,1},{1,0},{2,3},{3,2},{4,5},{5,4},{6,7},{7,6},{8,9},{9,8},{10,11... | collective-permute-start | bytes 589832 | tf_op jit(solution)/shard_map/ppermute | solution.py:270
  16.8 1.5 %collective-permute-start.8 = (bf16[128,768]{1,0:T(8,128)(2,1)S(1)}, bf16[128,768]{1,0:T(8,128)(2,1)S(1)}, u32[]{:S(2)}, u32[]{:S(2)}) collective-permute-start(bf16[128,768]{1,0:T(8,128)(2,1)S(1)} %collect.3.refs_2_), channel_id=1, source_target_pairs={{0,1},{1,0},{2,3},{3,2},{4,5},{5,4},{6,7},{7,6},{8,9},{9,8},{10,11... | collective-permute-start | bytes 589832 | tf_op jit(solution)/shard_map/ppermute | solution.py:270
  21.6 2.0 %collective-permute-start.9 = (bf16[64,4224]{1,0:T(8,128)(2,1)S(1)}, bf16[64,4224]{1,0:T(8,128)(2,1)S(1)}, u32[]{:S(2)}, u32[]{:S(2)}) collective-permute-start(bf16[64,4224]{1,0:T(8,128)(2,1)S(1)} %hidden.1.mine_ref), channel_id=1, source_target_pairs={{0,1},{1,0},{2,3},{3,2},{4,5},{5,4},{6,7},{7,6},{8,9},{9,8},{10,11... | collective-permute-start | bytes 1622024 | tf_op jit(solution)/shard_map/ppermute | solution.py:270
